TPU v7x, 32 devices: a whole 2x2x4 slice. The times are simulated.
32 devices in a mesh: gx: 4 (over x, core), gy: 8 (over z, y).
Axes of the slice: x: 2, y: 2, z: 4, core: 2. Of those that a mesh axis runs over, the one named last changes fastest.
Arguments:
- multipoles: bfloat16 [165, 8192], P(None, ('gx', 'gy')), may hold values from -6 to 6
- operators: bfloat16 [64, 165, 165], replicated, may hold values from -0.125 to 0.125
- boundary: int32 [5, 4096], P(None, ('gx', 'gy')), may hold values from 0 to 767, as said below
- pair_target: int32 [64, 4096], P(None, ('gx', 'gy')), may hold values from 0 to 255
- pair_source: int32 [64, 4096], P(None, ('gx', 'gy')), may hold values from 0 to 895
- pair_count: int32 [64, 32], P(None, ('gx', 'gy')), may hold values from 1 to 128, as said below
Outputs:
- local_expansions: float32 [165, 8192], P(None, ('gx', 'gy'))
Inputs may be any that keep to these rules, and one draw needn't show every extreme that they name: `boundary`: on every device and cut l, the list holds 128 distinct columns in increasing order, all below 256 + l * 128, and always includes column 256 + l * 128 - 1. `pair_count`: on every device, some class uses all 128 slots.
All inputs are finite; a program needn't handle non-finite values.
Results may differ from a plain program's by a relative error of at most 0.0003.
Values may be sent and summed in bfloat16 or wider, within the bound.
No kernel may reach another device: no remote copies, remote signals or barrier semaphores. Data moves between devices by JAX's collectives and lax.ppermute only.
A program may use at most 64 MiB of HBM per device.

v0:
```python
import math

import jax
import jax.numpy as jnp
from jax import lax
from jax.sharding import PartitionSpec as P


def from_partner(block, axis, distance):
    count = lax.axis_size(axis)
    route = []
    for low in range(count):
        high = low | 1 << distance
        if high != low and high < count:
            route += [(low, high), (high, low)]
    return lax.ppermute(block, axis, route)


def translate(expansion, operators, sources, source_index, target_index, active):
    class_count = operators.shape[0]
    coefficients = operators.shape[1]
    block_size = math.gcd(class_count, 8)
    block_count = class_count // block_size

    def translate_block(partial_value, pieces):
        operator_block, source_rows, target_rows, active_rows = pieces
        gathered = jnp.take(sources, source_rows, axis=1)
        translated = jnp.einsum(
            "cij,jcs->ics", operator_block, gathered, preferred_element_type=jnp.float32
        )
        translated = jnp.where(active_rows[None], translated, 0.0)
        partial_value = partial_value.at[:, target_rows.reshape(-1)].add(
            translated.reshape(coefficients, -1)
        )
        return (partial_value, None)

    pieces = (
        operators.reshape(block_count, block_size, coefficients, coefficients),
        source_index.reshape(block_count, block_size, -1),
        target_index.reshape(block_count, block_size, -1),
        active.reshape(block_count, block_size, -1),
    )
    expansion, _ = lax.scan(translate_block, expansion, pieces)
    return expansion


def per_device(multipoles, operators, boundary, pair_target, pair_source, pair_count):
    coefficients, own_cells = multipoles.shape
    cut_count, sent_count = boundary.shape
    pool_width = own_cells + cut_count * sent_count
    active = lax.broadcasted_iota(jnp.int32, pair_target.shape, 1) < pair_count
    expansion = jnp.zeros((coefficients, pool_width), jnp.float32)
    cell_pool = multipoles
    for cut_level in range(cut_count):
        cut_bit = cut_count - 1 - cut_level
        exported = jnp.take(cell_pool, boundary[cut_level], axis=1)
        received = from_partner(exported, ("gx", "gy"), cut_bit)
        cell_pool = jnp.concatenate([cell_pool, received], axis=1)
    source_all = jnp.concatenate([pair_source, pair_target[::-1]], axis=1)
    target_all = jnp.concatenate([pair_target, pair_source[::-1]], axis=1)
    active_all = jnp.concatenate([active, active[::-1]], axis=1)
    expansion = translate(expansion, operators, cell_pool, source_all, target_all, active_all)
    for cut_level in reversed(range(cut_count)):
        first_column = own_cells + cut_level * sent_count
        outgoing = expansion[:, first_column : first_column + sent_count]
        returned = from_partner(outgoing, ("gx", "gy"), cut_count - 1 - cut_level)
        expansion = expansion[:, :first_column].at[:, boundary[cut_level]].add(returned)
    return expansion


def solution(mesh):
    in_specs = (
        P(None, ("gx", "gy")),
        P(),
        P(None, ("gx", "gy")),
        P(None, ("gx", "gy")),
        P(None, ("gx", "gy")),
        P(None, ("gx", "gy")),
    )
    out_specs = P(None, ("gx", "gy"))
    return jax.shard_map(
        per_device, mesh=mesh, in_specs=in_specs, out_specs=out_specs, check_vma=False
    )
```

profile of v0, /device:TPU:0, one launch (start us, length us, event | category | flops | bytes accessed | tf_op | source)
XLA Modules:
  0.0 285.4 jit_solution(10128371529358574701)
XLA Ops:
  3.7 3.0 %collective-permute-start = (bf16[165,128]{0,1:T(8,128)(2,1)S(1)}, bf16[165,128]{0,1:T(8,128)(2,1)S(1)}, u32[]{:S(2)}, u32[]{:S(2)}) collective-permute-start(bf16[165,128]{0,1:T(8,128)(2,1)S(1)} %select_bitcast_fusion.4), channel_id=1, source_target_pairs={{0,16},{16,0},{1,17},{17,1},{2,18},{18,2},{3,19},{19,3},{4,20},{20... | collective-permute-start | bytes 126728 | tf_op jit(solution)/shard_map/ppermute | solution.py:16
  13.8 2.7 collective-permute-start.2
  16.5 4.0 %collective-permute-done.2 = bf16[165,128]{0,1:T(8,128)(2,1)S(1)} collective-permute-done((bf16[165,128]{0,1:T(8,128)(2,1)S(1)}, bf16[165,128]{0,1:T(8,128)(2,1)S(1)}, u32[]{:S(2)}, u32[]{:S(2)}) %collective-permute-start.2) | collective-permute-done | bytes 42272 | tf_op jit(solution)/shard_map/ppermute | solution.py:16
  22.1 3.7 %collective-permute-done.3 = bf16[165,128]{0,1:T(8,128)(2,1)S(1)} collective-permute-done((bf16[165,128]{0,1:T(8,128)(2,1)S(1)}, bf16[165,128]{0,1:T(8,128)(2,1)S(1)}, u32[]{:S(2)}, u32[]{:S(2)}) %collective-permute-start.3) | collective-permute-done | bytes 42272 | tf_op jit(solution)/shard_map/ppermute | solution.py:16
  28.9 8.0 %copy.25 = bf16[64,165,165]{2,1,0:T(8,128)(2,1)} copy(bf16[64,165,165]{2,0,1:T(8,128)(2,1)} %param.9) | data formatting | bytes 6969600 | tf_op args[1]
  37.0 215.1 %while.10 = (s32[]{:T(128)}, f32[165,896]{0,1:T(8,128)S(1)}, s32[8,8,256]{2,1,0:T(8,128)}, pred[8,8,256]{2,1,0:T(8,128)(4,1)}, s32[8,8,256]{2,1,0:T(8,128)S(1)},...) while((s32[]{:T(128)}, f32[165,896]{0,1:T(8,128)S(1)}, ...), condition=%wide.region_2.3_spmd, body=%wide.region_0.0_spmd.sunk | while | flops 112553984 | bytes 20494960 | solution.py:43
  37.1 7.5 %gather_fusion = bf16[2048,165]{1,0:T(8,128)(2,1)S(1)} fusion(bf16[165,896]{0,1:T(8,128)(2,1)S(1)} %get-tuple-element.145, s32[2048]{0:T(1024)S(1)} %broadcast_clamp_fusion.2), kind=kCustom, calls=%fused_computation.clone.1 | custom fusion | bytes 1359872 | tf_op jit(solution)/shard_map/while/body/eval_jaxpr/jit(_take)/gather | solution.py:27
  49.4 1.8 copy.41
  52.0 11.9 %scatter_fusion = f32[165,896]{0,1:T(8,128)S(1)} fusion(f32[165,896]{0,1:T(8,128)S(1)} %get-tuple-element.132, s32[2048]{0:T(1024)S(1)} %bitcast.126, f32[2048,165]{1,0:T(8,128)S(1)} %copy.41), kind=kCustom, calls=%fused_computation.6.clone.1 | custom fusion | flops 337920 | bytes 4063232 | tf_op jit(solution)/shard_map/while/body/eval_jaxpr/scatter-add | solution.py:32
  63.9 7.5 %gather_fusion = bf16[2048,165]{1,0:T(8,128)(2,1)S(1)} fusion(bf16[165,896]{0,1:T(8,128)(2,1)S(1)} %get-tuple-element.145, s32[2048]{0:T(1024)S(1)} %broadcast_clamp_fusion.2), kind=kCustom, calls=%fused_computation.clone.1 | custom fusion | bytes 1359872 | tf_op jit(solution)/shard_map/while/body/eval_jaxpr/jit(_take)/gather | solution.py:27
  76.3 1.8 copy.41
  78.8 11.9 %scatter_fusion = f32[165,896]{0,1:T(8,128)S(1)} fusion(f32[165,896]{0,1:T(8,128)S(1)} %get-tuple-element.132, s32[2048]{0:T(1024)S(1)} %bitcast.126, f32[2048,165]{1,0:T(8,128)S(1)} %copy.41), kind=kCustom, calls=%fused_computation.6.clone.1 | custom fusion | flops 337920 | bytes 4063232 | tf_op jit(solution)/shard_map/while/body/eval_jaxpr/scatter-add | solution.py:32
  90.8 7.5 %gather_fusion = bf16[2048,165]{1,0:T(8,128)(2,1)S(1)} fusion(bf16[165,896]{0,1:T(8,128)(2,1)S(1)} %get-tuple-element.145, s32[2048]{0:T(1024)S(1)} %broadcast_clamp_fusion.2), kind=kCustom, calls=%fused_computation.clone.1 | custom fusion | bytes 1359872 | tf_op jit(solution)/shard_map/while/body/eval_jaxpr/jit(_take)/gather | solution.py:27
  103.2 1.8 copy.41
  105.7 11.9 %scatter_fusion = f32[165,896]{0,1:T(8,128)S(1)} fusion(f32[165,896]{0,1:T(8,128)S(1)} %get-tuple-element.132, s32[2048]{0:T(1024)S(1)} %bitcast.126, f32[2048,165]{1,0:T(8,128)S(1)} %copy.41), kind=kCustom, calls=%fused_computation.6.clone.1 | custom fusion | flops 337920 | bytes 4063232 | tf_op jit(solution)/shard_map/while/body/eval_jaxpr/scatter-add | solution.py:32
  117.7 7.5 %gather_fusion = bf16[2048,165]{1,0:T(8,128)(2,1)S(1)} fusion(bf16[165,896]{0,1:T(8,128)(2,1)S(1)} %get-tuple-element.145, s32[2048]{0:T(1024)S(1)} %broadcast_clamp_fusion.2), kind=kCustom, calls=%fused_computation.clone.1 | custom fusion | bytes 1359872 | tf_op jit(solution)/shard_map/while/body/eval_jaxpr/jit(_take)/gather | solution.py:27
  130.1 1.8 copy.41
  132.6 11.9 %scatter_fusion = f32[165,896]{0,1:T(8,128)S(1)} fusion(f32[165,896]{0,1:T(8,128)S(1)} %get-tuple-element.132, s32[2048]{0:T(1024)S(1)} %bitcast.126, f32[2048,165]{1,0:T(8,128)S(1)} %copy.41), kind=kCustom, calls=%fused_computation.6.clone.1 | custom fusion | flops 337920 | bytes 4063232 | tf_op jit(solution)/shard_map/while/body/eval_jaxpr/scatter-add | solution.py:32
  144.6 7.5 %gather_fusion = bf16[2048,165]{1,0:T(8,128)(2,1)S(1)} fusion(bf16[165,896]{0,1:T(8,128)(2,1)S(1)} %get-tuple-element.145, s32[2048]{0:T(1024)S(1)} %broadcast_clamp_fusion.2), kind=kCustom, calls=%fused_computation.clone.1 | custom fusion | bytes 1359872 | tf_op jit(solution)/shard_map/while/body/eval_jaxpr/jit(_take)/gather | solution.py:27
  159.5 11.9 %scatter_fusion = f32[165,896]{0,1:T(8,128)S(1)} fusion(f32[165,896]{0,1:T(8,128)S(1)} %get-tuple-element.132, s32[2048]{0:T(1024)S(1)} %bitcast.126, f32[2048,165]{1,0:T(8,128)S(1)} %copy.41), kind=kCustom, calls=%fused_computation.6.clone.1 | custom fusion | flops 337920 | bytes 4063232 | tf_op jit(solution)/shard_map/while/body/eval_jaxpr/scatter-add | solution.py:32
  171.5 7.5 %gather_fusion = bf16[2048,165]{1,0:T(8,128)(2,1)S(1)} fusion(bf16[165,896]{0,1:T(8,128)(2,1)S(1)} %get-tuple-element.145, s32[2048]{0:T(1024)S(1)} %broadcast_clamp_fusion.2), kind=kCustom, calls=%fused_computation.clone.1 | custom fusion | bytes 1359872 | tf_op jit(solution)/shard_map/while/body/eval_jaxpr/jit(_take)/gather | solution.py:27
  186.4 11.9 %scatter_fusion = f32[165,896]{0,1:T(8,128)S(1)} fusion(f32[165,896]{0,1:T(8,128)S(1)} %get-tuple-element.132, s32[2048]{0:T(1024)S(1)} %bitcast.126, f32[2048,165]{1,0:T(8,128)S(1)} %copy.41), kind=kCustom, calls=%fused_computation.6.clone.1 | custom fusion | flops 337920 | bytes 4063232 | tf_op jit(solution)/shard_map/while/body/eval_jaxpr/scatter-add | solution.py:32
  198.4 7.5 %gather_fusion = bf16[2048,165]{1,0:T(8,128)(2,1)S(1)} fusion(bf16[165,896]{0,1:T(8,128)(2,1)S(1)} %get-tuple-element.145, s32[2048]{0:T(1024)S(1)} %broadcast_clamp_fusion.2), kind=kCustom, calls=%fused_computation.clone.1 | custom fusion | bytes 1359872 | tf_op jit(solution)/shard_map/while/body/eval_jaxpr/jit(_take)/gather | solution.py:27
  213.3 11.9 %scatter_fusion = f32[165,896]{0,1:T(8,128)S(1)} fusion(f32[165,896]{0,1:T(8,128)S(1)} %get-tuple-element.132, s32[2048]{0:T(1024)S(1)} %bitcast.126, f32[2048,165]{1,0:T(8,128)S(1)} %copy.41), kind=kCustom, calls=%fused_computation.6.clone.1 | custom fusion | flops 337920 | bytes 4063232 | tf_op jit(solution)/shard_map/while/body/eval_jaxpr/scatter-add | solution.py:32
  225.3 7.5 %gather_fusion = bf16[2048,165]{1,0:T(8,128)(2,1)S(1)} fusion(bf16[165,896]{0,1:T(8,128)(2,1)S(1)} %get-tuple-element.145, s32[2048]{0:T(1024)S(1)} %broadcast_clamp_fusion.2), kind=kCustom, calls=%fused_computation.clone.1 | custom fusion | bytes 1359872 | tf_op jit(solution)/shard_map/while/body/eval_jaxpr/jit(_take)/gather | solution.py:27
  240.2 11.9 %scatter_fusion = f32[165,896]{0,1:T(8,128)S(1)} fusion(f32[165,896]{0,1:T(8,128)S(1)} %get-tuple-element.132, s32[2048]{0:T(1024)S(1)} %bitcast.126, f32[2048,165]{1,0:T(8,128)S(1)} %copy.41), kind=kCustom, calls=%fused_computation.6.clone.1 | custom fusion | flops 337920 | bytes 4063232 | tf_op jit(solution)/shard_map/while/body/eval_jaxpr/scatter-add | solution.py:32
  252.7 4.4 %collective-permute-done.5 = f32[165,128]{0,1:T(8,128)S(1)} collective-permute-done((f32[165,128]{0,1:T(8,128)S(1)}, f32[165,128]{0,1:T(8,128)S(1)}, u32[]{:S(2)}, u32[]{:S(2)}) %collective-permute-start.5) | collective-permute-done | bytes 84512 | tf_op jit(solution)/shard_map/ppermute | solution.py:16
  259.6 4.4 %collective-permute-done.6 = f32[165,128]{0,1:T(8,128)S(1)} collective-permute-done((f32[165,128]{0,1:T(8,128)S(1)}, f32[165,128]{0,1:T(8,128)S(1)}, u32[]{:S(2)}, u32[]{:S(2)}) %collective-permute-start.6) | collective-permute-done | bytes 84512 | tf_op jit(solution)/shard_map/ppermute | solution.py:16
  263.9 1.8 scatter_custom_fusion.2
  265.8 2.0 collective-permute-start.7
  267.8 5.3 %collective-permute-done.7 = f32[165,128]{0,1:T(8,128)S(1)} collective-permute-done((f32[165,128]{0,1:T(8,128)S(1)}, f32[165,128]{0,1:T(8,128)S(1)}, u32[]{:S(2)}, u32[]{:S(2)}) %collective-permute-start.7) | collective-permute-done | bytes 84512 | tf_op jit(solution)/shard_map/ppermute | solution.py:16
  278.2 5.0 %collective-permute-done.9 = f32[165,128]{0,1:T(8,128)S(1)} collective-permute-done((f32[165,128]{0,1:T(8,128)S(1)}, f32[165,128]{0,1:T(8,128)S(1)}, u32[]{:S(2)}, u32[]{:S(2)}) %collective-permute-start.9) | collective-permute-done | bytes 84512 | tf_op jit(solution)/shard_map/ppermute | solution.py:16
  (174 shorter events, 77.6 us)
Async XLA Ops:
  0.9 7.4 %copy-start = (s32[128]{0:T(128)}, s32[128]{0:T(128)S(1)}, u32[]{:S(2)}) copy-start(s32[128]{0:T(128)S(1)} %get-tuple-element.75) | copy-start | bytes 1540
  0.9 7.4 %copy-start.1 = (s32[128]{0:T(128)}, s32[128]{0:T(128)S(1)}, u32[]{:S(2)}) copy-start(s32[128]{0:T(128)S(1)} %get-tuple-element.76) | copy-start | bytes 1540
  0.9 9.6 %copy-start.2 = (s32[128]{0:T(128)}, s32[128]{0:T(128)S(1)}, u32[]{:S(2)}) copy-start(s32[128]{0:T(128)S(1)} %get-tuple-element.72) | copy-start | bytes 1540
  3.7 6.8 %collective-permute-start = (bf16[165,128]{0,1:T(8,128)(2,1)S(1)}, bf16[165,128]{0,1:T(8,128)(2,1)S(1)}, u32[]{:S(2)}, u32[]{:S(2)}) collective-permute-start(bf16[165,128]{0,1:T(8,128)(2,1)S(1)} %select_bitcast_fusion.4), channel_id=1, source_target_pairs={{0,16},{16,0},{1,17},{17,1},{2,18},{18,2},{3,19},{19,3},{4,20},{20... | collective-permute-start | bytes 126728 | tf_op jit(solution)/shard_map/ppermute | solution.py:16
  11.5 1.3 collective-permute-start.1
  13.8 6.6 %collective-permute-start.2 = (bf16[165,128]{0,1:T(8,128)(2,1)S(1)}, bf16[165,128]{0,1:T(8,128)(2,1)S(1)}, u32[]{:S(2)}, u32[]{:S(2)}) collective-permute-start(bf16[165,128]{0,1:T(8,128)(2,1)S(1)} %select_bitcast_fusion.2), channel_id=1, source_target_pairs={{0,4},{4,0},{1,5},{5,1},{2,6},{6,2},{3,7},{7,3},{8,12},{12,8},{9,1... | collective-permute-start | bytes 126728 | tf_op jit(solution)/shard_map/ppermute | solution.py:16
  21.4 4.3 %collective-permute-start.3 = (bf16[165,128]{0,1:T(8,128)(2,1)S(1)}, bf16[165,128]{0,1:T(8,128)(2,1)S(1)}, u32[]{:S(2)}, u32[]{:S(2)}) collective-permute-start(bf16[165,128]{0,1:T(8,128)(2,1)S(1)} %select_bitcast_fusion.1), channel_id=1, source_target_pairs={{0,2},{2,0},{1,3},{3,1},{4,6},{6,4},{5,7},{7,5},{8,10},{10,8},{9,1... | collective-permute-start | bytes 126728 | tf_op jit(solution)/shard_map/ppermute | solution.py:16
  26.7 10.2 %collective-permute-start.4 = (bf16[165,128]{0,1:T(8,128)(2,1)S(1)}, bf16[165,128]{0,1:T(8,128)(2,1)S(1)}, u32[]{:S(2)}, u32[]{:S(2)}) collective-permute-start(bf16[165,128]{0,1:T(8,128)(2,1)S(1)} %select_bitcast_fusion), channel_id=1, source_target_pairs={{0,1},{1,0},{2,3},{3,2},{4,5},{5,4},{6,7},{7,6},{8,9},{9,8},{10,11... | collective-permute-start | bytes 126728 | tf_op jit(solution)/shard_map/ppermute | solution.py:16
  252.1 5.0 %collective-permute-start.5 = (f32[165,128]{0,1:T(8,128)S(1)}, f32[165,128]{0,1:T(8,128)S(1)}, u32[]{:S(2)}, u32[]{:S(2)}) collective-permute-start(f32[165,128]{0,1:T(8,128)S(1)} %slice.56), channel_id=1, source_target_pairs={{0,1},{1,0},{2,3},{3,2},{4,5},{5,4},{6,7},{7,6},{8,9},{9,8},{10,11... | collective-permute-start | bytes 253448 | tf_op jit(solution)/shard_map/ppermute | solution.py:16
  258.9 5.0 %collective-permute-start.6 = (f32[165,128]{0,1:T(8,128)S(1)}, f32[165,128]{0,1:T(8,128)S(1)}, u32[]{:S(2)}, u32[]{:S(2)}) collective-permute-start(f32[165,128]{0,1:T(8,128)S(1)} %slice.78), channel_id=1, source_target_pairs={{0,2},{2,0},{1,3},{3,1},{4,6},{6,4},{5,7},{7,5},{8,10},{10,8},{9,1... | collective-permute-start | bytes 253448 | tf_op jit(solution)/shard_map/ppermute | solution.py:16
  265.8 7.3 %collective-permute-start.7 = (f32[165,128]{0,1:T(8,128)S(1)}, f32[165,128]{0,1:T(8,128)S(1)}, u32[]{:S(2)}, u32[]{:S(2)}) collective-permute-start(f32[165,128]{0,1:T(8,128)S(1)} %slice.80), channel_id=1, source_target_pairs={{0,4},{4,0},{1,5},{5,1},{2,6},{6,2},{3,7},{7,3},{8,12},{12,8},{9,1... | collective-permute-start | bytes 253448 | tf_op jit(solution)/shard_map/ppermute | solution.py:16
  274.7 1.4 collective-permute-start.8
  277.6 5.6 %collective-permute-start.9 = (f32[165,128]{0,1:T(8,128)S(1)}, f32[165,128]{0,1:T(8,128)S(1)}, u32[]{:S(2)}, u32[]{:S(2)}) collective-permute-start(f32[165,128]{0,1:T(8,128)S(1)} %slice.84), channel_id=1, source_target_pairs={{0,16},{16,0},{1,17},{17,1},{2,18},{18,2},{3,19},{19,3},{4,20},{20... | collective-permute-start | bytes 253448 | tf_op jit(solution)/shard_map/ppermute | solution.py:16
where the time goes:
time: 287 us; the launch traced here: 285 us
  local copies, waits for them, and re-layouts  123 us (43%)
  other arithmetic  109 us (38%)
  waiting for transfers between devices  29.3 us (10%)
  starting transfers between devices  11.8 us (4%)
  matrix products  11.5 us (4%)
    scatter-add x8, other arithmetic, translate_block(): partial_value.at[:, target_rows.reshape(-1)]  95.3 us
    gather x16, local copies, waits for them, and re-layouts, translate_block(): gathered = jnp.take(sources, source_rows, axis=1)  64.2 us
    ppermute x10, waiting for transfers between devices, from_partner(): return lax.ppermute(block, axis, route)  29.3 us
    while x40, local copies, waits for them, and re-layouts  19.6 us
    reshape x8, local copies, waits for them, and re-layouts, translate_block(): translated.reshape(coefficients, -1)  14.4 us
    ppermute x10, starting transfers between devices, from_partner(): return lax.ppermute(block, axis, route)  11.8 us
    dot_general x8, matrix products, translate_block(): jnp.einsum('cij,jcs->ics', operator_block, gathered, preferred_element_ty...  11.5 us
    unnamed x12, local copies, waits for them, and re-layouts  9.04 us
  transfers between devices with their start and end apart: 10, of which 8 were waited for; matrix products, arithmetic and copies ran while one was open for 4% of the time, Pallas kernels for 0%

commit v1 on v0

v1 whole, which is shorter than its diff:
```python
import jax
import jax.numpy as jnp
from jax import lax
from jax.experimental import pallas as pl
from jax.experimental.pallas import tpu as pltpu
from jax.sharding import PartitionSpec as P

LANES = 128
GROUP = 4
VMEM = pl.BlockSpec(memory_space=pltpu.VMEM)


def from_partner(block, axes, distance):
    count = lax.axis_size(axes)
    route = []
    for low in range(count):
        high = low | 1 << distance
        if high != low and high < count:
            route += [(low, high), (high, low)]
    return lax.ppermute(block, axes, route)


def one_hot(row, first, height):
    blocks = []
    for low in range(0, height, LANES):
        near = (row - (first + low)).astype(jnp.float32).astype(jnp.bfloat16)
        place = lax.broadcasted_iota(jnp.int32, (LANES, row.shape[1]), 0)
        place = place.astype(jnp.float32).astype(jnp.bfloat16)
        blocks.append(jnp.where(place == near, 1.0, 0.0).astype(jnp.bfloat16))
    return jnp.concatenate(blocks, axis=0) if len(blocks) > 1 else blocks[0]


def halves(wide):
    high = wide.astype(jnp.bfloat16)
    low = (wide - high.astype(jnp.float32)).astype(jnp.bfloat16)
    return high, low


def dot(a, b):
    return jnp.dot(a, b, preferred_element_type=jnp.float32)


def dot_nt(a, b):
    return lax.dot_general(a, b, (((1,), (1,)), ((), ())), preferred_element_type=jnp.float32)


def move(values, hot, how):
    high, low = halves(values)
    return how(high, hot) + how(low, hot)


def rows_of(ref, classes):
    return jnp.concatenate([ref[i] for i in range(classes)], axis=1)


def reverse_kernel(starts, mult_ref, op_ref, target_ref, source_ref, *refs):
    outs, total = refs[:-1], refs[-1]
    step = pl.program_id(0)
    group = op_ref.shape[0]
    cells = mult_ref.shape[1]

    @pl.when(step == 0)
    def _():
        total[...] = jnp.zeros_like(total)

    targets = rows_of(target_ref, group)
    sources = rows_of(source_ref, group)
    own = dot(mult_ref[...], one_hot(targets, 0, cells)).astype(jnp.bfloat16)
    width = targets.shape[1] // group
    terms = [
        dot(op_ref[group - 1 - i], own[:, i * width : (i + 1) * width]) for i in range(group)
    ]
    high, low = halves(jnp.concatenate(terms, axis=1))
    hot = one_hot(sources, 0, total.shape[1])
    total[...] += dot_nt(high, hot) + dot_nt(low, hot)

    @pl.when(step == pl.num_programs(0) - 1)
    def _():
        for out, first in zip(outs, starts):
            out[...] = total[:, first : first + out.shape[1]]


def forward_kernel(starts, *refs):
    segs = refs[: len(starts)]
    op_ref, target_ref, source_ref, out_ref, pool = refs[len(starts) :]
    step = pl.program_id(0)
    group = op_ref.shape[0]

    @pl.when(step == 0)
    def _():
        out_ref[...] = jnp.zeros_like(out_ref)
        for seg, first in zip(segs, starts):
            pool[:, first : first + seg.shape[1]] = seg[...]

    targets = rows_of(target_ref, group)
    sources = rows_of(source_ref, group)
    taken = dot(pool[...], one_hot(sources, 0, pool.shape[1])).astype(jnp.bfloat16)
    width = targets.shape[1] // group
    terms = [dot(op_ref[i], taken[:, i * width : (i + 1) * width]) for i in range(group)]
    high, low = halves(jnp.concatenate(terms, axis=1))
    hot = one_hot(targets, 0, out_ref.shape[1])
    out_ref[...] += dot_nt(high, hot) + dot_nt(low, hot)


def export_kernel(starts, list_ref, *refs):
    segs, out_ref = refs[:-1], refs[-1]
    row = list_ref[...]
    out = 0.0
    for seg, first in zip(segs, starts):
        out = out + dot(seg[...], one_hot(row, first, seg.shape[1]))
    out_ref[...] = out.astype(jnp.bfloat16)


def return_kernel(first, bases, lists_ref, *refs):
    out_ref = refs[-1]
    returned = refs[bases:-1]
    width = out_ref.shape[1]
    out = refs[0][...]
    for ref in refs[1:bases]:
        out = out + ref[...]
    cut = lists_ref.shape[0] - len(returned)
    for i, ref in enumerate(returned):
        hot = one_hot(lists_ref[cut + i : cut + i + 1, :], first, width)
        out = out + move(ref[...], hot, dot_nt)
    out_ref[...] = out


def call(kernel, out_shape, args, **more):
    return pl.pallas_call(
        kernel,
        out_shape=out_shape,
        in_specs=[VMEM] * len(args),
        out_specs=VMEM,
        **more,
    )(*args)


def per_device(multipoles, operators, boundary, pair_target, pair_source, pair_count):
    coefficients, cells = multipoles.shape
    cuts, sent = boundary.shape
    classes, width = pair_target.shape
    starts = [0] + [cells + cut * sent for cut in range(cuts)]
    sizes = [cells] + [sent] * cuts
    pool_width = cells + cuts * sent
    axes = ("gx", "gy")
    group = GROUP if classes % GROUP == 0 else 1
    steps = classes // group

    active = lax.broadcasted_iota(jnp.int32, pair_target.shape, 1) < pair_count
    source = jnp.where(active, pair_source, -1).reshape(classes, 1, width)
    target = pair_target.reshape(classes, 1, width)

    def whole(rows, columns):
        return pl.BlockSpec((rows, columns), lambda i: (0, 0))

    row_spec = pl.BlockSpec((group, 1, width), lambda i: (i, 0, 0))
    params = pltpu.CompilerParams(vmem_limit_bytes=48 * 1024 * 1024)
    flops = 2 * classes * width * coefficients * (pool_width * 2 + cells + coefficients)
    cost = pl.CostEstimate(flops=flops, bytes_accessed=operators.size * 2, transcendentals=0)

    def f_shape(columns):
        return jax.ShapeDtypeStruct((coefficients, columns), jnp.float32)

    def reverse_body(*refs):
        reverse_kernel(starts, *refs)

    with jax.named_scope("reverse_terms"):
        expansions = pl.pallas_call(
            reverse_body,
            grid=(steps,),
            in_specs=[
                whole(coefficients, cells),
                pl.BlockSpec((group, coefficients, coefficients), lambda i: (steps - 1 - i, 0, 0)),
                row_spec,
                row_spec,
            ],
            out_specs=[whole(coefficients, size) for size in sizes],
            out_shape=[f_shape(size) for size in sizes],
            scratch_shapes=[pltpu.VMEM((coefficients, pool_width), jnp.float32)],
            compiler_params=params,
            cost_estimate=cost,
        )(multipoles, operators, target, source)

    segments = [multipoles]
    for cut in range(cuts):
        def export_body(*refs, cut=cut):
            export_kernel(starts[: cut + 1], *refs)

        exported = call(
            export_body,
            jax.ShapeDtypeStruct((coefficients, sent), jnp.bfloat16),
            [boundary[cut : cut + 1]] + segments,
        )
        segments.append(from_partner(exported, axes, cuts - 1 - cut))

    def forward_body(*refs):
        forward_kernel(starts, *refs)

    with jax.named_scope("forward_terms"):
        local = pl.pallas_call(
            forward_body,
            grid=(steps,),
            in_specs=[whole(coefficients, size) for size in sizes]
            + [
                pl.BlockSpec((group, coefficients, coefficients), lambda i: (i, 0, 0)),
                row_spec,
                row_spec,
            ],
            out_specs=whole(coefficients, cells),
            out_shape=f_shape(cells),
            scratch_shapes=[pltpu.VMEM((coefficients, pool_width), jnp.bfloat16)],
            compiler_params=params,
            cost_estimate=cost,
        )(*segments, operators, target, source)

    returned = []
    for cut in reversed(range(cuts)):
        outgoing = expansions[cut + 1]
        if returned:
            def return_body(*refs, cut=cut):
                return_kernel(starts[cut + 1], 1, *refs)

            outgoing = call(return_body, f_shape(sent), [boundary, outgoing] + returned)
        returned.insert(0, from_partner(outgoing, axes, cuts - 1 - cut))

    def final_body(*refs):
        return_kernel(0, 2, *refs)

    return call(final_body, f_shape(cells), [boundary, expansions[0], local] + returned)


def solution(mesh):
    split = P(None, ("gx", "gy"))
    return jax.shard_map(
        per_device,
        mesh=mesh,
        in_specs=(split, P(), split, split, split, split),
        out_specs=split,
        check_vma=False,
    )
```

time: 287 us -> 107 us (0.37)
  other arithmetic: 109 us -> 0.07 us
  local copies, waits for them, and re-layouts: 123 us -> 23.8 us
  Pallas kernels: 0 us -> 54.5 us
  waiting for transfers between devices: 29.3 us -> 14.9 us
  matrix products: 11.5 us -> 0 us
    scatter-add x13 -> x0, other arithmetic: 103 us -> none  [the longest x8 95.3 us: translate_block(): partial_value.at[:, target_rows.reshape(-1)]]
    gather x21 -> x0, local copies, waits for them, and re-layouts: 68.4 us -> none  [the longest x16 64.2 us: translate_block(): gathered = jnp.take(sources, source_rows, axis=1)]
    pallas_call x0 -> x12, Pallas kernels: none -> 54.5 us  [the longest x1 20.8 us: per_device(): pl.pallas_call(reverse_body, grid=(steps,), in_specs=[whole(coefficients,...]
    while x40 -> x0, local copies, waits for them, and re-layouts: 19.6 us -> none
    ppermute x10, waiting for transfers between devices: 29.3 us -> 14.9 us  [from_partner(): return lax.ppermute(block, axes, route)]
    reshape x8 -> x0, local copies, waits for them, and re-layouts: 14.4 us -> none  [translate_block(): translated.reshape(coefficients, -1)]
    unnamed x12 -> x53, local copies, waits for them, and re-layouts: 9.04 us -> 23.3 us
    dot_general x8 -> x0, matrix products: 11.5 us -> none  [translate_block(): jnp.einsum('cij,jcs->ics', operator_block, gathered, preferred_element_ty...]
  transfers between devices with their start and end apart: 10 -> 10, of which waited for: 8 -> 4; matrix products, arithmetic and copies ran while one was open for 4% -> 1% of each run, Pallas kernels for 0% -> 26%
where the time goes in v1:
time: 107 us; the launch traced here: 106 us
  Pallas kernels  54.5 us (51%)
  local copies, waits for them, and re-layouts  23.8 us (22%)
  waiting for transfers between devices  14.9 us (14%)
  starting transfers between devices  12.4 us (12%)
    unnamed x53, local copies, waits for them, and re-layouts  23.3 us
    pallas_call x1, Pallas kernels, per_device(): pl.pallas_call(reverse_body, grid=(steps,), in_specs=[whole(coefficients,...  20.8 us
    pallas_call x10, Pallas kernels, call(): pl.pallas_call(kernel, out_shape=out_shape, in_specs=[VMEM] * len(args),...  18.9 us
    ppermute x10, waiting for transfers between devices, from_partner(): return lax.ppermute(block, axes, route)  14.9 us
    pallas_call x1, Pallas kernels, per_device(): pl.pallas_call(forward_body, grid=(steps,), in_specs=[whole(coefficients,...  14.8 us
    ppermute x10, starting transfers between devices, from_partner(): return lax.ppermute(block, axes, route)  12.4 us
  transfers between devices with their start and end apart: 10, of which 4 were waited for; matrix products, arithmetic and copies ran while one was open for 1% of the time, Pallas kernels for 26%

profile of v1, /device:TPU:0, one launch (start us, length us, event | category | flops | bytes accessed | tf_op | source)
XLA Modules:
  0.0 105.8 jit_solution(2360378991802981386)
XLA Ops:
  0.0 8.0 %copy.7.refs_1_.refs_6_ = bf16[64,165,165]{2,1,0:T(8,128)(2,1)} copy(bf16[64,165,165]{2,0,1:T(8,128)(2,1)} %param.7) | data formatting | bytes 6969600 | tf_op args[1]
  8.2 20.8 %reverse_terms.1 = (f32[165,256]{1,0:T(8,128)S(1)}, f32[165,128]{1,0:T(8,128)S(1)}, f32[165,128]{1,0:T(8,128)S(1)}, f32[165,128]{1,0:T(8,128)S(1)}, f32[165,128]{1,0:T(8,128)S(1)}, /*index=5*/f32[165,128]{1,0:T(8,128)S(1)}) custom-call(bf16[165,256]{1,0:T(8,128)(2,1)S(1)} %copy-done.1, bf16[64,165,165]{2,1,0:T(8,128)(2,1)} %copy.7.refs_1_.refs_6_, ...), custom_call_target="tpu_custom_call" | custom-call | flops 5982535680 | bytes 3484800 | tf_op jit(solution)/shard_map/reverse_terms/pallas_call | solution.py:168
  29.0 0.7 copy-done.9
  32.2 3.0 %collective-permute-start.5 = (f32[165,128]{1,0:T(8,128)S(1)}, f32[165,128]{1,0:T(8,128)S(1)}, u32[]{:S(2)}, u32[]{:S(2)}) collective-permute-start(f32[165,128]{1,0:T(8,128)S(1)} %get-tuple-element.16), channel_id=1, source_target_pairs={{0,1},{1,0},{2,3},{3,2},{4,5},{5,4},{6,7},{7,6},{8,9},{9,8},{10,11... | collective-permute-start | bytes 253448 | tf_op jit(solution)/shard_map/ppermute | solution.py:20
  35.2 2.5 %collective-permute-done.5.refs_2_.refs_3_.refs_4_.refs_5_.refs_7_ = f32[165,128]{1,0:T(8,128)S(1)} collective-permute-done((f32[165,128]{1,0:T(8,128)S(1)}, f32[165,128]{1,0:T(8,128)S(1)}, u32[]{:S(2)}, u32[]{:S(2)}) %collective-permute-start.5) | collective-permute-done | bytes 84512 | tf_op jit(solution)/shard_map/ppermute | solution.py:20
  38.4 1.8 %shard_map.69 = f32[165,128]{1,0:T(8,128)} custom-call(s32[5,128]{1,0:T(8,128)} %refs_0_.13, f32[165,128]{1,0:T(8,128)} %copy-done.13, f32[165,128]{1,0:T(8,128)} %copy-done.18), custom_call_target="tpu_custom_call" | custom-call | tf_op jit(solution)/shard_map/pallas_call | solution.py:129
  40.2 2.0 %collective-permute-start.6 = (f32[165,128]{1,0:T(8,128)}, f32[165,128]{1,0:T(8,128)S(1)}, u32[]{:S(2)}, u32[]{:S(2)}) collective-permute-start(f32[165,128]{1,0:T(8,128)} %shard_map.69), channel_id=1, source_target_pairs={{0,2},{2,0},{1,3},{3,1},{4,6},{6,4},{5,7},{7,5},{8,10},{10,8},{9,1... | collective-permute-start | bytes 253448 | tf_op jit(solution)/shard_map/ppermute | solution.py:20
  42.8 1.7 %shard_map.64 = bf16[165,128]{1,0:T(8,128)(2,1)} custom-call(s32[1,128]{1,0:T(1,128)} %get-tuple-element.21.refs_0_, bf16[165,256]{1,0:T(8,128)(2,1)} %refs_0_.8), custom_call_target="tpu_custom_call" | custom-call | tf_op jit(solution)/shard_map/pallas_call | solution.py:129
  44.5 1.5 %collective-permute-start = (bf16[165,128]{1,0:T(8,128)(2,1)}, bf16[165,128]{1,0:T(8,128)(2,1)S(1)}, u32[]{:S(2)}, u32[]{:S(2)}) collective-permute-start(bf16[165,128]{1,0:T(8,128)(2,1)} %shard_map.64), channel_id=1, source_target_pairs={{0,16},{16,0},{1,17},{17,1},{2,18},{18,2},{3,19},{19,3},{4,20},{20... | collective-permute-start | bytes 126728 | tf_op jit(solution)/shard_map/ppermute | solution.py:20
  46.0 2.7 %collective-permute-done.refs_2_.refs_1_ = bf16[165,128]{1,0:T(8,128)(2,1)S(1)} collective-permute-done((bf16[165,128]{1,0:T(8,128)(2,1)}, bf16[165,128]{1,0:T(8,128)(2,1)S(1)}, u32[]{:S(2)}, u32[]{:S(2)}) %collective-permute-start) | collective-permute-done | bytes 42272 | tf_op jit(solution)/shard_map/ppermute | solution.py:20
  49.3 1.7 %shard_map.65 = bf16[165,128]{1,0:T(8,128)(2,1)} custom-call(s32[1,128]{1,0:T(1,128)} %get-tuple-element.20.refs_0_, bf16[165,256]{1,0:T(8,128)(2,1)} %refs_0_.8, bf16[165,128]{1,0:T(8,128)(2,1)} %copy-done.3), custom_call_target="tpu_custom_call" | custom-call | tf_op jit(solution)/shard_map/pallas_call | solution.py:129
  51.1 0.6 copy-done.19
  51.7 1.9 %shard_map.70 = f32[165,128]{1,0:T(8,128)} custom-call(s32[5,128]{1,0:T(8,128)} %refs_0_.13, f32[165,128]{1,0:T(8,128)} %copy-done.12, f32[165,128]{1,0:T(8,128)} %copy-done.19, f32[165,128]{1,0:T(8,128)} %copy-done.18), custom_call_target="tpu_custom_call" | custom-call | tf_op jit(solution)/shard_map/pallas_call | solution.py:129
  53.6 2.6 %collective-permute-start.7 = (f32[165,128]{1,0:T(8,128)}, f32[165,128]{1,0:T(8,128)S(1)}, u32[]{:S(2)}, u32[]{:S(2)}) collective-permute-start(f32[165,128]{1,0:T(8,128)} %shard_map.70), channel_id=1, source_target_pairs={{0,4},{4,0},{1,5},{5,1},{2,6},{6,2},{3,7},{7,3},{8,12},{12,8},{9,1... | collective-permute-start | bytes 253448 | tf_op jit(solution)/shard_map/ppermute | solution.py:20
  56.8 1.7 %shard_map.66 = bf16[165,128]{1,0:T(8,128)(2,1)} custom-call(s32[1,128]{1,0:T(1,128)} %get-tuple-element.19.refs_0_, bf16[165,256]{1,0:T(8,128)(2,1)} %refs_0_.8, bf16[165,128]{1,0:T(8,128)(2,1)} %copy-done.3, bf16[165,128]{1,0:T(8,128)(2,1)} %copy-done.5), custom_call_target="tpu_custom_call" | custom-call | tf_op jit(solution)/shard_map/pallas_call | solution.py:129
  58.9 5.3 %collective-permute-done.2.refs_4_.refs_3_ = bf16[165,128]{1,0:T(8,128)(2,1)S(1)} collective-permute-done((bf16[165,128]{1,0:T(8,128)(2,1)}, bf16[165,128]{1,0:T(8,128)(2,1)S(1)}, u32[]{:S(2)}, u32[]{:S(2)}) %collective-permute-start.2) | collective-permute-done | bytes 42272 | tf_op jit(solution)/shard_map/ppermute | solution.py:20
  64.8 1.8 %shard_map.67 = bf16[165,128]{1,0:T(8,128)(2,1)} custom-call(s32[1,128]{1,0:T(1,128)} %get-tuple-element.18.refs_0_, bf16[165,256]{1,0:T(8,128)(2,1)} %refs_0_.8, bf16[165,128]{1,0:T(8,128)(2,1)} %copy-done.3, bf16[165,128]{1,0:T(8,128)(2,1)} %copy-done.5, bf16[165,128]{1,0:T(8,128)(2,1)} %copy-done.7), custom_call_target="tpu_custom_call" | custom-call | tf_op jit(solution)/shard_map/pallas_call | solution.py:129
  67.2 2.0 %shard_map.71 = f32[165,128]{1,0:T(8,128)} custom-call(s32[5,128]{1,0:T(8,128)} %refs_0_.13, f32[165,128]{1,0:T(8,128)} %copy-done.11, f32[165,128]{1,0:T(8,128)} %copy-done.20, f32[165,128]{1,0:T(8,128)} %copy-done.19, f32[165,128]{1,0:T(8,128)} %copy-done.18), custom_call_target="tpu_custom_call" | custom-call | tf_op jit(solution)/shard_map/pallas_call | solution.py:129
  69.2 4.2 %collective-permute-done.3.refs_5_.refs_4_ = bf16[165,128]{1,0:T(8,128)(2,1)S(1)} collective-permute-done((bf16[165,128]{1,0:T(8,128)(2,1)}, bf16[165,128]{1,0:T(8,128)(2,1)S(1)}, u32[]{:S(2)}, u32[]{:S(2)}) %collective-permute-start.3) | collective-permute-done | bytes 42272 | tf_op jit(solution)/shard_map/ppermute | solution.py:20
  74.1 1.8 %shard_map.68 = bf16[165,128]{1,0:T(8,128)(2,1)} custom-call(s32[1,128]{1,0:T(1,128)} %get-tuple-element.17.refs_0_, bf16[165,256]{1,0:T(8,128)(2,1)} %refs_0_.8, bf16[165,128]{1,0:T(8,128)(2,1)} %copy-done.3, bf16[165,128]{1,0:T(8,128)(2,1)} %copy-done.5, bf16[165,128]{1,0:T(8,128)(2,1)} %copy-done.7, bf16[165,128]{1,0:T(8,128)(2,1)} %copy-done.15), custom_call_target="tpu_custom_call" | custom-call | tf_op jit(solution)/shard_map/pallas_call | solution.py:129
  75.9 1.5 %collective-permute-start.4 = (bf16[165,128]{1,0:T(8,128)(2,1)}, bf16[165,128]{1,0:T(8,128)(2,1)S(1)}, u32[]{:S(2)}, u32[]{:S(2)}) collective-permute-start(bf16[165,128]{1,0:T(8,128)(2,1)} %shard_map.68), channel_id=1, source_target_pairs={{0,1},{1,0},{2,3},{3,2},{4,5},{5,4},{6,7},{7,6},{8,9},{9,8},{10,11... | collective-permute-start | bytes 126728 | tf_op jit(solution)/shard_map/ppermute | solution.py:20
  78.0 2.1 %shard_map.72 = f32[165,128]{1,0:T(8,128)} custom-call(s32[5,128]{1,0:T(8,128)} %refs_0_.13, f32[165,128]{1,0:T(8,128)} %copy-done.14, f32[165,128]{1,0:T(8,128)} %copy-done.21, f32[165,128]{1,0:T(8,128)} %copy-done.20, f32[165,128]{1,0:T(8,128)} %copy-done.19, f32[165,128]{1,0:T(8,128)} %copy-done.18), custom_call_target="tpu_custom_call" | custom-call | tf_op jit(solution)/shard_map/pallas_call | solution.py:129
  80.1 1.5 %collective-permute-start.9 = (f32[165,128]{1,0:T(8,128)}, f32[165,128]{1,0:T(8,128)S(1)}, u32[]{:S(2)}, u32[]{:S(2)}) collective-permute-start(f32[165,128]{1,0:T(8,128)} %shard_map.72), channel_id=1, source_target_pairs={{0,16},{16,0},{1,17},{17,1},{2,18},{18,2},{3,19},{19,3},{4,20},{20... | collective-permute-start | bytes 253448 | tf_op jit(solution)/shard_map/ppermute | solution.py:20
  81.6 2.6 %copy-done = bf16[64,165,165]{2,1,0:T(8,128)(2,1)S(1)} copy-done((bf16[64,165,165]{2,1,0:T(8,128)(2,1)S(1)}, bf16[64,165,165]{2,1,0:T(8,128)(2,1)}, u32[]{:S(2)}) %copy-start) | copy-done | bytes 3484824
  84.2 0.8 copy-done.4
  85.0 0.8 copy-done.6
  85.7 0.8 copy-done.8
  86.5 0.8 copy-done.16
  87.3 14.8 %forward_terms.1.refs_2_ = f32[165,256]{1,0:T(8,128)S(1)} custom-call(bf16[165,256]{1,0:T(8,128)(2,1)S(1)} %copy-done.2, bf16[165,128]{1,0:T(8,128)(2,1)S(1)} %copy-done.4, bf16[165,128]{1,0:T(8,128)(2,1)S(1)} %copy-done.6, bf16[165,128]{1,0:T(8,128)(2,1)S(1)} %copy-done.8, bf16[165,128]{1,0:T(8,128)(2,1)S(1)} %copy-done.16, ...), custom_call_target="tpu_custom_call" | custom-call | flops 5982535680 | bytes 3484800 | tf_op jit(solution)/shard_map/forward_terms/pallas_call | solution.py:200
  102.2 0.7 copy-done.10
  102.8 0.6 copy-done.23
  103.5 2.4 %shard_map.73 = f32[165,256]{1,0:T(8,128)} custom-call(s32[5,128]{1,0:T(8,128)} %refs_0_.13, f32[165,256]{1,0:T(8,128)} %copy-done.9, f32[165,256]{1,0:T(8,128)} %copy-done.10, f32[165,128]{1,0:T(8,128)} %copy-done.23, f32[165,128]{1,0:T(8,128)} %copy-done.21, f32[165,128]{1,0:T(8,128)} %copy-done.20, f32[165,128]{1,0:T(8,128)} %copy-done.19, ...), custom_call_target="tpu_custom_call" | custom-call | tf_op jit(solution)/shard_map/pallas_call | solution.py:129
  (55 shorter events, 7.9 us)
Async XLA Ops:
  0.0 8.1 %copy-start.25 = (s32[64,1]{0,1:T(1,128)S(1)}, s32[64,1]{0,1:T(1,128)}, u32[]{:S(2)}) copy-start(s32[64,1]{0,1:T(1,128)} %param.11) | copy-start | bytes 772
  0.0 8.1 %copy-start.24 = (s32[64,128]{1,0:T(8,128)S(1)}, s32[64,128]{1,0:T(8,128)}, u32[]{:S(2)}) copy-start(s32[64,128]{1,0:T(8,128)} %param.10) | copy-start | bytes 98308
  0.0 8.1 %copy-start.1 = (bf16[165,256]{1,0:T(8,128)(2,1)S(1)}, bf16[165,256]{1,0:T(8,128)(2,1)}, u32[]{:S(2)}) copy-start(bf16[165,256]{1,0:T(8,128)(2,1)} %refs_0_.8) | copy-start | bytes 253444
  0.0 8.1 %copy-start.17 = (s32[64,128]{1,0:T(8,128)S(1)}, s32[64,128]{1,0:T(8,128)}, u32[]{:S(2)}) copy-start(s32[64,128]{1,0:T(8,128)} %param.9) | copy-start | bytes 98308
  8.2 34.0 %copy-start.22 = (s32[5,128]{1,0:T(8,128)S(1)}, s32[5,128]{1,0:T(8,128)}, u32[]{:S(2)}) copy-start(s32[5,128]{1,0:T(8,128)} %refs_0_.13) | copy-start | bytes 7684
  8.2 73.4 %copy-start.2 = (bf16[165,256]{1,0:T(8,128)(2,1)S(1)}, bf16[165,256]{1,0:T(8,128)(2,1)}, u32[]{:S(2)}) copy-start(bf16[165,256]{1,0:T(8,128)(2,1)} %refs_0_.8) | copy-start | bytes 253444
  29.0 0.7 copy-start.9
  29.7 0.6 copy-start.11
  30.3 0.6 copy-start.12
  31.0 0.6 copy-start.13
  31.6 0.6 copy-start.14
  32.2 5.5 %collective-permute-start.5 = (f32[165,128]{1,0:T(8,128)S(1)}, f32[165,128]{1,0:T(8,128)S(1)}, u32[]{:S(2)}, u32[]{:S(2)}) collective-permute-start(f32[165,128]{1,0:T(8,128)S(1)} %get-tuple-element.16), channel_id=1, source_target_pairs={{0,1},{1,0},{2,3},{3,2},{4,5},{5,4},{6,7},{7,6},{8,9},{9,8},{10,11... | collective-permute-start | bytes 253448 | tf_op jit(solution)/shard_map/ppermute | solution.py:20
  37.7 0.6 copy-start.18
  40.2 10.9 %collective-permute-start.6 = (f32[165,128]{1,0:T(8,128)}, f32[165,128]{1,0:T(8,128)S(1)}, u32[]{:S(2)}, u32[]{:S(2)}) collective-permute-start(f32[165,128]{1,0:T(8,128)} %shard_map.69), channel_id=1, source_target_pairs={{0,2},{2,0},{1,3},{3,1},{4,6},{6,4},{5,7},{7,5},{8,10},{10,8},{9,1... | collective-permute-start | bytes 253448 | tf_op jit(solution)/shard_map/ppermute | solution.py:20
  44.5 4.2 %collective-permute-start = (bf16[165,128]{1,0:T(8,128)(2,1)}, bf16[165,128]{1,0:T(8,128)(2,1)S(1)}, u32[]{:S(2)}, u32[]{:S(2)}) collective-permute-start(bf16[165,128]{1,0:T(8,128)(2,1)} %shard_map.64), channel_id=1, source_target_pairs={{0,16},{16,0},{1,17},{17,1},{2,18},{18,2},{3,19},{19,3},{4,20},{20... | collective-permute-start | bytes 126728 | tf_op jit(solution)/shard_map/ppermute | solution.py:20
  51.0 5.1 %collective-permute-start.1 = (bf16[165,128]{1,0:T(8,128)(2,1)}, bf16[165,128]{1,0:T(8,128)(2,1)S(1)}, u32[]{:S(2)}, u32[]{:S(2)}) collective-permute-start(bf16[165,128]{1,0:T(8,128)(2,1)} %shard_map.65), channel_id=1, source_target_pairs={{0,8},{8,0},{1,9},{9,1},{2,10},{10,2},{3,11},{11,3},{4,12},{12,4},... | collective-permute-start | bytes 126728 | tf_op jit(solution)/shard_map/ppermute | solution.py:20
  51.1 0.6 copy-start.19
  53.6 13.0 %collective-permute-start.7 = (f32[165,128]{1,0:T(8,128)}, f32[165,128]{1,0:T(8,128)S(1)}, u32[]{:S(2)}, u32[]{:S(2)}) collective-permute-start(f32[165,128]{1,0:T(8,128)} %shard_map.70), channel_id=1, source_target_pairs={{0,4},{4,0},{1,5},{5,1},{2,6},{6,2},{3,7},{7,3},{8,12},{12,8},{9,1... | collective-permute-start | bytes 253448 | tf_op jit(solution)/shard_map/ppermute | solution.py:20
  58.5 5.7 %collective-permute-start.2 = (bf16[165,128]{1,0:T(8,128)(2,1)}, bf16[165,128]{1,0:T(8,128)(2,1)S(1)}, u32[]{:S(2)}, u32[]{:S(2)}) collective-permute-start(bf16[165,128]{1,0:T(8,128)(2,1)} %shard_map.66), channel_id=1, source_target_pairs={{0,4},{4,0},{1,5},{5,1},{2,6},{6,2},{3,7},{7,3},{8,12},{12,8},{9,1... | collective-permute-start | bytes 126728 | tf_op jit(solution)/shard_map/ppermute | solution.py:20
  66.6 0.6 copy-start.20
  69.2 8.2 %collective-permute-start.8 = (f32[165,128]{1,0:T(8,128)}, f32[165,128]{1,0:T(8,128)S(1)}, u32[]{:S(2)}, u32[]{:S(2)}) collective-permute-start(f32[165,128]{1,0:T(8,128)} %shard_map.71), channel_id=1, source_target_pairs={{0,8},{8,0},{1,9},{9,1},{2,10},{10,2},{3,11},{11,3},{4,12},{12,4},... | collective-permute-start | bytes 253448 | tf_op jit(solution)/shard_map/ppermute | solution.py:20
  69.2 4.2 %collective-permute-start.3 = (bf16[165,128]{1,0:T(8,128)(2,1)}, bf16[165,128]{1,0:T(8,128)(2,1)S(1)}, u32[]{:S(2)}, u32[]{:S(2)}) collective-permute-start(bf16[165,128]{1,0:T(8,128)(2,1)} %shard_map.67), channel_id=1, source_target_pairs={{0,2},{2,0},{1,3},{3,1},{4,6},{6,4},{5,7},{7,5},{8,10},{10,8},{9,1... | collective-permute-start | bytes 126728 | tf_op jit(solution)/shard_map/ppermute | solution.py:20
  75.9 5.7 %collective-permute-start.4 = (bf16[165,128]{1,0:T(8,128)(2,1)}, bf16[165,128]{1,0:T(8,128)(2,1)S(1)}, u32[]{:S(2)}, u32[]{:S(2)}) collective-permute-start(bf16[165,128]{1,0:T(8,128)(2,1)} %shard_map.68), channel_id=1, source_target_pairs={{0,1},{1,0},{2,3},{3,2},{4,5},{5,4},{6,7},{7,6},{8,9},{9,8},{10,11... | collective-permute-start | bytes 126728 | tf_op jit(solution)/shard_map/ppermute | solution.py:20
  77.4 0.6 copy-start.21
  80.1 22.7 %collective-permute-start.9 = (f32[165,128]{1,0:T(8,128)}, f32[165,128]{1,0:T(8,128)S(1)}, u32[]{:S(2)}, u32[]{:S(2)}) collective-permute-start(f32[165,128]{1,0:T(8,128)} %shard_map.72), channel_id=1, source_target_pairs={{0,16},{16,0},{1,17},{17,1},{2,18},{18,2},{3,19},{19,3},{4,20},{20... | collective-permute-start | bytes 253448 | tf_op jit(solution)/shard_map/ppermute | solution.py:20
  81.6 2.6 %copy-start = (bf16[64,165,165]{2,1,0:T(8,128)(2,1)S(1)}, bf16[64,165,165]{2,1,0:T(8,128)(2,1)}, u32[]{:S(2)}) copy-start(bf16[64,165,165]{2,1,0:T(8,128)(2,1)} %copy.7.refs_1_.refs_6_) | copy-start | bytes 10454404
  84.2 0.8 copy-start.4
  85.0 0.8 copy-start.6
  85.7 0.8 copy-start.8
  86.5 0.8 copy-start.16
  102.2 0.7 copy-start.10
  102.8 0.6 copy-start.23
  (4 other events, 2.5 us)

commit v2 on v0

v2 whole, which is shorter than its diff:
```python
import math

import jax
import jax.numpy as jnp
from jax import lax
from jax.experimental import pallas as pl
from jax.experimental.pallas import tpu as pltpu
from jax.sharding import PartitionSpec as P

LANES = 128
CHUNK = 512
ROWS = CHUNK // LANES
AXES = ("gx", "gy")
VMEM = pl.BlockSpec(memory_space=pltpu.VMEM)
SMEM = pl.BlockSpec(memory_space=pltpu.SMEM)
BF16 = jnp.bfloat16
F32 = jnp.float32


def up(size, multiple):
    return -(-size // multiple) * multiple


def params(mebibytes):
    return pltpu.CompilerParams(vmem_limit_bytes=mebibytes * 1024 * 1024)


def shape(rows, columns, kind):
    return jax.ShapeDtypeStruct((rows, columns), kind)


def call(kernel, out_shape, args, limit=4, scalars=0, scratch=(), flops=0):
    single = not isinstance(out_shape, (tuple, list))
    return pl.pallas_call(
        kernel,
        out_shape=out_shape,
        in_specs=[SMEM] * scalars + [VMEM] * (len(args) - scalars),
        out_specs=VMEM if single else [VMEM] * len(out_shape),
        scratch_shapes=list(scratch),
        compiler_params=params(limit),
        cost_estimate=pl.CostEstimate(flops=flops, bytes_accessed=1024, transcendentals=0),
    )(*args)


def dot(a, b):
    return jnp.dot(a, b, preferred_element_type=F32)


def dot_nt(a, b):
    return lax.dot_general(a, b, (((1,), (1,)), ((), ())), preferred_element_type=F32)


def halves(wide):
    high = wide.astype(BF16)
    return high, (wide - high.astype(F32)).astype(BF16)


def from_partner(block, distance):
    count = lax.axis_size(AXES)
    route = []
    for low in range(count):
        high = low | 1 << distance
        if high != low and high < count:
            route += [(low, high), (high, low)]
    return lax.ppermute(block, AXES, route)


def one_hot(row, first, height):
    place = lax.broadcasted_iota(jnp.int32, (height, row.shape[1]), 0)
    return jnp.where(place == row - first, 1.0, 0.0).astype(BF16)


def fill_hot(hot, index_ref, row, first, height):
    for n in range(ROWS):
        index = index_ref[pl.ds(row + n, 1), :]
        for low in range(0, height, LANES):
            size = min(LANES, height - low)
            hot[low : low + size, n * LANES : (n + 1) * LANES] = one_hot(index, first + low, size)


def total_of(count_ref):
    return lax.fori_loop(0, count_ref.shape[0], lambda i, t: t + count_ref[i], 0, unroll=8)


def pack_kernel(count_ref, target_ref, source_ref, packed_target, packed_source):
    classes, width = target_ref.shape
    lane = lax.broadcasted_iota(jnp.int32, (1, LANES), 1)

    def place(c, offset):
        shift = lax.rem(offset, LANES)
        row = offset // LANES
        keep = lane >= shift
        for ref, out in ((target_ref, packed_target), (source_ref, packed_source)):
            turned = pltpu.roll(ref[pl.ds(c, 1), :], shift, 1)
            out[pl.ds(row, 1), :] = jnp.where(keep, turned, out[pl.ds(row, 1), :])
            out[pl.ds(row + 1, 1), :] = turned
        return offset + count_ref[c]

    total = lax.fori_loop(0, classes, place, 0, unroll=8)
    position = lax.broadcasted_iota(jnp.int32, packed_target.shape, 0) * LANES
    position = position + lax.broadcasted_iota(jnp.int32, packed_target.shape, 1)
    for out in (packed_target, packed_source):
        out[...] = jnp.where(position < total, out[...], -1)


def order_kernel(coefficients, group, in_ref, out_ref):
    rows, classes, _ = in_ref.shape
    step = pl.program_id(0)
    tile = 16
    size = tile * group
    to = lax.broadcasted_iota(jnp.int32, (size, size), 0)
    of = lax.broadcasted_iota(jnp.int32, (size, size), 1)
    swap = (of == lax.rem(to, tile) * group + to // tile).astype(F32).astype(BF16)
    out_ref[...] = jnp.zeros_like(out_ref)
    row = lax.broadcasted_iota(jnp.int32, (size, coefficients), 0) // group
    for i in range(0, rows, tile):
        left = coefficients - step * rows - i
        for c in range(0, classes, group):
            block = in_ref[i : i + tile, c : c + group, :].reshape(size, coefficients)
            block = jnp.where(row < left, block, jnp.zeros_like(block))
            turned = dot(swap, block).astype(BF16)
            out_ref[c : c + group, i : i + tile, :coefficients] = turned.reshape(
                group, tile, coefficients
            )


def terms_kernel(starts, flip, count_ref, index_ref, op_ref, *refs):
    segs = refs[: len(starts)]
    out_ref, pool, hot, picked = refs[len(starts) :]
    classes, rows, depth = op_ref.shape
    height = pool.shape[1]
    total = total_of(count_ref)

    pool[...] = jnp.zeros_like(pool)
    for seg, first in zip(segs, starts):
        pool[: seg.shape[0], first : first + seg.shape[1]] = seg[...]
    picked[rows:, :] = jnp.zeros((depth - rows, picked.shape[1]), BF16)

    def pick(k, _):
        fill_hot(hot, index_ref, k * ROWS, 0, height)
        at = pl.ds(pl.multiple_of(k * CHUNK, CHUNK), CHUNK)
        picked[:rows, at] = dot(pool[...], hot[...]).astype(BF16)
        return 0

    lax.fori_loop(0, pl.cdiv(total, CHUNK), pick, 0)
    last = pl.multiple_of(total // CHUNK * CHUNK, CHUNK)
    out_ref[:, pl.ds(last, CHUNK)] = jnp.zeros((2 * rows, CHUNK), BF16)
    lane = lax.broadcasted_iota(jnp.int32, (rows, LANES), 1)

    def apply(c, offset):
        start = pl.multiple_of(offset // LANES * LANES, LANES)
        c_op = classes - 1 - c if flip else c
        new = dot(op_ref[c_op], picked[:, pl.ds(start, 2 * LANES)])
        keep = lane >= offset - start
        for first, part in zip((0, rows), halves(new)):
            at = pl.ds(start, LANES)
            old = out_ref[first : first + rows, at]
            out_ref[first : first + rows, at] = jnp.where(keep, part[:, :LANES], old)
            out_ref[first : first + rows, pl.ds(start + LANES, LANES)] = part[:, LANES:]
        return offset + count_ref[c]

    lax.fori_loop(0, classes, apply, 0, unroll=8)


def scatter_kernel(starts, count_ref, index_ref, terms_ref, *refs):
    outs = refs[: len(starts)]
    hot, sums = refs[len(starts) :]
    first, height = starts[0], hot.shape[0]
    total = total_of(count_ref)
    sums[...] = jnp.zeros_like(sums)

    def add(k, _):
        fill_hot(hot, index_ref, k * ROWS, first, height)
        at = pl.ds(pl.multiple_of(k * CHUNK, CHUNK), CHUNK)
        sums[...] += dot_nt(terms_ref[:, at], hot[...])
        return 0

    lax.fori_loop(0, pl.cdiv(total, CHUNK), add, 0)
    rows = sums.shape[0] // 2
    for out, start in zip(outs, starts):
        low = start - first
        at = slice(low, low + out.shape[1])
        out[...] = sums[: out.shape[0], at] + sums[rows : rows + out.shape[0], at]


def export_kernel(starts, cut, lists_ref, *refs):
    segs, out_ref = refs[:-1], refs[-1]
    row = lists_ref[cut : cut + 1, :]
    out = 0.0
    for seg, first in zip(segs, starts):
        out = out + dot(seg[...], one_hot(row, first, seg.shape[1]))
    out_ref[...] = out.astype(BF16)


def return_kernel(first, bases, lists_ref, *refs):
    out_ref = refs[-1]
    returned = refs[bases:-1]
    out = refs[0][...]
    for ref in refs[1:bases]:
        out = out + ref[...]
    cut = lists_ref.shape[0] - len(returned)
    for i, ref in enumerate(returned):
        hot = one_hot(lists_ref[cut + i : cut + i + 1, :], first, out_ref.shape[1])
        high, low = halves(ref[...])
        out = out + dot_nt(high, hot) + dot_nt(low, hot)
    out_ref[...] = out


def per_device(multipoles, operators, boundary, pair_target, pair_source, pair_count):
    coefficients, cells = multipoles.shape
    cuts, sent = boundary.shape
    classes, width = pair_target.shape
    starts = [0] + [cells + cut * sent for cut in range(cuts)]
    sizes = [cells] + [sent] * cuts
    pool_width = cells + cuts * sent
    rows, depth = up(coefficients, 16), up(coefficients, LANES)
    packed = classes * width + CHUNK
    counts = pair_count.reshape(classes)

    with jax.named_scope("pack_slots"):
        index_shape = shape(packed // LANES, LANES, jnp.int32)
        targets, sources = call(
            pack_kernel, [index_shape, index_shape], [counts, pair_target, pair_source], scalars=1
        )

    with jax.named_scope("order_operators"):
        group = math.gcd(classes, 16)
        block = 32
        ordered = pl.pallas_call(
            lambda *refs: order_kernel(coefficients, group, *refs),
            grid=(pl.cdiv(rows, block),),
            in_specs=[pl.BlockSpec((block, classes, coefficients), lambda i: (i, 0, 0))],
            out_specs=pl.BlockSpec((classes, block, depth), lambda i: (0, i, 0)),
            out_shape=jax.ShapeDtypeStruct((classes, rows, depth), BF16),
            compiler_params=params(16),
        )(operators.transpose(1, 0, 2))

    def terms(segments, index, flip):
        height = sum(segment.shape[1] for segment in segments)
        return call(
            lambda *refs: terms_kernel(starts[: len(segments)], flip, *refs),
            shape(2 * rows, packed, BF16),
            [counts, index, ordered] + list(segments),
            limit=16,
            scalars=1,
            scratch=[
                pltpu.VMEM((rows, height), BF16),
                pltpu.VMEM((height, CHUNK), BF16),
                pltpu.VMEM((depth, packed), BF16),
            ],
            flops=classes * width * rows * (height + depth),
        )

    def scatter(values, index, first, last):
        height = sum(sizes[first:last])
        return call(
            lambda *refs: scatter_kernel(starts[first:last], *refs),
            [shape(coefficients, size, F32) for size in sizes[first:last]],
            [counts, index, values],
            limit=8,
            scalars=1,
            scratch=[
                pltpu.VMEM((height, CHUNK), BF16),
                pltpu.VMEM((2 * rows, height), F32),
            ],
            flops=classes * width * rows * height * 2,
        )

    with jax.named_scope("reverse_terms"):
        back = terms([multipoles], targets, True)
        sums = [None] * (cuts + 1)
        last = cuts + 1
        while last > 0:
            first = max(last - 2, 0) if last > 2 else 0
            sums[first:last] = scatter(back, sources, first, last)
            last = first

    segments = [multipoles]
    for cut in range(cuts):
        with jax.named_scope("export"):
            exported = call(
                lambda *refs, cut=cut: export_kernel(starts, cut, *refs),
                shape(coefficients, sent, BF16),
                [boundary] + segments,
            )
        segments.append(from_partner(exported, cuts - 1 - cut))

    with jax.named_scope("forward_terms"):
        ahead = terms(segments, sources, False)
        (local,) = scatter(ahead, targets, 0, 1)

    returned = []
    for cut in reversed(range(cuts)):
        outgoing = sums[cut + 1]
        if returned:
            with jax.named_scope("return"):
                outgoing = call(
                    lambda *refs, cut=cut: return_kernel(starts[cut + 1], 1, *refs),
                    shape(coefficients, sent, F32),
                    [boundary, outgoing] + returned,
                )
        returned.insert(0, from_partner(outgoing, cuts - 1 - cut))

    with jax.named_scope("sum"):
        return call(
            lambda *refs: return_kernel(0, 2, *refs),
            shape(coefficients, cells, F32),
            [boundary, sums[0], local] + returned,
        )


def solution(mesh):
    split = P(None, AXES)
    return jax.shard_map(
        per_device,
        mesh=mesh,
        in_specs=(split, P(), split, split, split, split),
        out_specs=split,
        check_vma=False,
    )
```

time: 287 us -> 64 us (0.22)
  local copies, waits for them, and re-layouts: 123 us -> 2.57 us
  other arithmetic: 109 us -> 0 us
  Pallas kernels: 0 us -> 41.9 us
  waiting for transfers between devices: 29.3 us -> 6.81 us
  matrix products: 11.5 us -> 0 us
    scatter-add x13 -> x0, other arithmetic: 103 us -> none  [the longest x8 95.3 us: translate_block(): partial_value.at[:, target_rows.reshape(-1)]]
    gather x21 -> x0, local copies, waits for them, and re-layouts: 68.4 us -> none  [the longest x16 64.2 us: translate_block(): gathered = jnp.take(sources, source_rows, axis=1)]
    pallas_call x0 -> x18, Pallas kernels: none -> 41.9 us  [the longest x17 38 us: call(): pl.pallas_call(kernel, out_shape=out_shape, in_specs=[SMEM] * scalars + [...]
    ppermute x10, waiting for transfers between devices: 29.3 us -> 6.81 us  [from_partner(): return lax.ppermute(block, AXES, route)]
    while x40 -> x0, local copies, waits for them, and re-layouts: 19.6 us -> none
    reshape x8 -> x0, local copies, waits for them, and re-layouts: 14.4 us -> none  [translate_block(): translated.reshape(coefficients, -1)]
    dot_general x8 -> x0, matrix products: 11.5 us -> none  [translate_block(): jnp.einsum('cij,jcs->ics', operator_block, gathered, preferred_element_ty...]
    unnamed x12, local copies, waits for them, and re-layouts: 9.04 us -> 2.57 us
  transfers between devices with their start and end apart: 10 -> 10, of which waited for: 8 -> 3; matrix products, arithmetic and copies ran while one was open for 4% -> 0% of each run, Pallas kernels for 0% -> 37%
where the time goes in v2:
time: 64 us; the launch traced here: 64.3 us
  Pallas kernels  41.9 us (65%)
  starting transfers between devices  12.8 us (20%)
  waiting for transfers between devices  6.81 us (11%)
  local copies, waits for them, and re-layouts  2.57 us (4%)
    pallas_call x17, Pallas kernels, call(): pl.pallas_call(kernel, out_shape=out_shape, in_specs=[SMEM] * scalars + [...  38 us
    ppermute x10, starting transfers between devices, from_partner(): return lax.ppermute(block, AXES, route)  12.8 us
    ppermute x10, waiting for transfers between devices, from_partner(): return lax.ppermute(block, AXES, route)  6.81 us
    pallas_call x1, Pallas kernels, per_device(): pl.pallas_call(lambda *refs: order_kernel(coefficients, group, *refs), gr...  3.93 us
    unnamed x12, local copies, waits for them, and re-layouts  2.57 us
  transfers between devices with their start and end apart: 10, of which 3 were waited for; matrix products, arithmetic and copies ran while one was open for 0% of the time, Pallas kernels for 37%

profile of v2, /device:TPU:0, one launch (start us, length us, event | category | flops | bytes accessed | tf_op | source)
XLA Modules:
  0.0 64.3 jit_solution(11545266174071613418)
XLA Ops:
  0.0 2.5 %copy-done = bf16[64,165,165]{2,0,1:T(8,128)(2,1)S(1)} copy-done((bf16[64,165,165]{2,0,1:T(8,128)(2,1)S(1)}, bf16[64,165,165]{2,0,1:T(8,128)(2,1)}, u32[]{:S(2)}) %copy-start) | copy-done | bytes 3484824
  2.6 3.9 %order_operators.1.refs_2_ = bf16[64,176,256]{2,1,0:T(8,128)(2,1)S(1)} custom-call(bf16[165,64,165]{2,1,0:T(8,128)(2,1)S(1)} %bitcast.2), custom_call_target="tpu_custom_call" | custom-call | tf_op jit(solution)/shard_map/order_operators/pallas_call | solution.py:229
  6.5 1.5 %pack_slots.1 = (s32[68,128]{1,0:T(8,128)S(1)}, s32[68,128]{1,0:T(8,128)S(1)}) custom-call(s32[64]{0:T(128)S(1)} %bitcast.3, s32[64,128]{1,0:T(8,128)S(1)} %copy-done.3, s32[64,128]{1,0:T(8,128)S(1)} %copy-done.4), custom_call_target="tpu_custom_call" | custom-call | bytes 1024 | tf_op jit(solution)/shard_map/pack_slots/pallas_call | solution.py:34
  8.0 8.2 %reverse_terms.4.refs_2_ = bf16[352,8704]{1,0:T(8,128)(2,1)S(1)} custom-call(s32[64]{0:T(128)S(1)} %bitcast.4, s32[68,128]{1,0:T(8,128)S(1)} %get-tuple-element.14.refs_1_, bf16[64,176,256]{2,1,0:T(8,128)(2,1)S(1)} %order_operators.1.refs_2_, bf16[165,256]{1,0:T(8,128)(2,1)S(1)} %copy-done.1), custom_call_target="tpu_custom_call" | custom-call | flops 738197504 | bytes 1024 | tf_op jit(solution)/shard_map/reverse_terms/pallas_call | solution.py:34
  16.2 3.6 %reverse_terms.7 = (f32[165,128]{1,0:T(8,128)S(1)}, f32[165,128]{1,0:T(8,128)S(1)}) custom-call(s32[64]{0:T(128)S(1)} %bitcast.5, s32[68,128]{1,0:T(8,128)S(1)} %get-tuple-element.13.refs_1_, bf16[352,8704]{1,0:T(8,128)(2,1)S(1)} %reverse_terms.4.refs_2_), custom_call_target="tpu_custom_call" | custom-call | flops 738197504 | bytes 1024 | tf_op jit(solution)/shard_map/reverse_terms/pallas_call | solution.py:34
  19.8 3.0 %collective-permute-start.5 = (f32[165,128]{1,0:T(8,128)S(1)}, f32[165,128]{1,0:T(8,128)S(1)}, u32[]{:S(2)}, u32[]{:S(2)}) collective-permute-start(f32[165,128]{1,0:T(8,128)S(1)} %get-tuple-element.20), channel_id=1, source_target_pairs={{0,1},{1,0},{2,3},{3,2},{4,5},{5,4},{6,7},{7,6},{8,9},{9,8},{10,11... | collective-permute-start | bytes 253448 | tf_op jit(solution)/shard_map/ppermute | solution.py:65
  22.8 0.2 export.5
  23.0 1.6 %collective-permute-start = (bf16[165,128]{1,0:T(8,128)(2,1)S(1)}, bf16[165,128]{1,0:T(8,128)(2,1)S(1)}, u32[]{:S(2)}, u32[]{:S(2)}) collective-permute-start(bf16[165,128]{1,0:T(8,128)(2,1)S(1)} %export.5), channel_id=1, source_target_pairs={{0,16},{16,0},{1,17},{17,1},{2,18},{18,2},{3,19},{19,3},{4,20},{20... | collective-permute-start | bytes 126728 | tf_op jit(solution)/shard_map/ppermute | solution.py:65
  24.5 2.5 %collective-permute-done.refs_2_.refs_4_ = bf16[165,128]{1,0:T(8,128)(2,1)S(1)} collective-permute-done((bf16[165,128]{1,0:T(8,128)(2,1)S(1)}, bf16[165,128]{1,0:T(8,128)(2,1)S(1)}, u32[]{:S(2)}, u32[]{:S(2)}) %collective-permute-start) | collective-permute-done | bytes 42272 | tf_op jit(solution)/shard_map/ppermute | solution.py:65
  27.1 0.2 export.6
  27.3 0.1 collective-permute-start.1
  27.3 0.2 return.4
  27.5 1.7 %collective-permute-start.6 = (f32[165,128]{1,0:T(8,128)S(1)}, f32[165,128]{1,0:T(8,128)S(1)}, u32[]{:S(2)}, u32[]{:S(2)}) collective-permute-start(f32[165,128]{1,0:T(8,128)S(1)} %return.4), channel_id=1, source_target_pairs={{0,2},{2,0},{1,3},{3,1},{4,6},{6,4},{5,7},{7,5},{8,10},{10,8},{9,1... | collective-permute-start | bytes 253448 | tf_op jit(solution)/shard_map/ppermute | solution.py:65
  29.3 0.2 export.7
  29.5 2.2 %collective-permute-start.2 = (bf16[165,128]{1,0:T(8,128)(2,1)S(1)}, bf16[165,128]{1,0:T(8,128)(2,1)S(1)}, u32[]{:S(2)}, u32[]{:S(2)}) collective-permute-start(bf16[165,128]{1,0:T(8,128)(2,1)S(1)} %export.7), channel_id=1, source_target_pairs={{0,4},{4,0},{1,5},{5,1},{2,6},{6,2},{3,7},{7,3},{8,12},{12,8},{9,1... | collective-permute-start | bytes 126728 | tf_op jit(solution)/shard_map/ppermute | solution.py:65
  31.7 3.6 %reverse_terms.6 = (f32[165,128]{1,0:T(8,128)S(1)}, f32[165,128]{1,0:T(8,128)S(1)}) custom-call(s32[64]{0:T(128)S(1)} %bitcast.6, s32[68,128]{1,0:T(8,128)S(1)} %get-tuple-element.13.refs_1_, bf16[352,8704]{1,0:T(8,128)(2,1)S(1)} %reverse_terms.4.refs_2_), custom_call_target="tpu_custom_call" | custom-call | flops 738197504 | bytes 1024 | tf_op jit(solution)/shard_map/reverse_terms/pallas_call | solution.py:34
  35.3 0.3 return.5
  35.6 0.5 collective-permute-start.7
  36.1 0.2 export.8
  36.3 1.3 %collective-permute-start.3 = (bf16[165,128]{1,0:T(8,128)(2,1)S(1)}, bf16[165,128]{1,0:T(8,128)(2,1)S(1)}, u32[]{:S(2)}, u32[]{:S(2)}) collective-permute-start(bf16[165,128]{1,0:T(8,128)(2,1)S(1)} %export.8), channel_id=1, source_target_pairs={{0,2},{2,0},{1,3},{3,1},{4,6},{6,4},{5,7},{7,5},{8,10},{10,8},{9,1... | collective-permute-start | bytes 126728 | tf_op jit(solution)/shard_map/ppermute | solution.py:65
  37.6 2.8 %collective-permute-done.3.refs_5_.refs_7_ = bf16[165,128]{1,0:T(8,128)(2,1)S(1)} collective-permute-done((bf16[165,128]{1,0:T(8,128)(2,1)S(1)}, bf16[165,128]{1,0:T(8,128)(2,1)S(1)}, u32[]{:S(2)}, u32[]{:S(2)}) %collective-permute-start.3) | collective-permute-done | bytes 42272 | tf_op jit(solution)/shard_map/ppermute | solution.py:65
  40.4 0.3 export.9
  40.7 0.6 collective-permute-start.4
  41.2 1.5 %collective-permute-done.7.refs_2_.refs_3_.refs_5_ = f32[165,128]{1,0:T(8,128)S(1)} collective-permute-done((f32[165,128]{1,0:T(8,128)S(1)}, f32[165,128]{1,0:T(8,128)S(1)}, u32[]{:S(2)}, u32[]{:S(2)}) %collective-permute-start.7) | collective-permute-done | bytes 84512 | tf_op jit(solution)/shard_map/ppermute | solution.py:65
  42.7 0.3 return.6
  43.0 0.1 collective-permute-start.8
  43.1 4.4 %reverse_terms.5 = (f32[165,256]{1,0:T(8,128)S(1)}, f32[165,128]{1,0:T(8,128)S(1)}) custom-call(s32[64]{0:T(128)S(1)} %bitcast.7, s32[68,128]{1,0:T(8,128)S(1)} %get-tuple-element.13.refs_1_, bf16[352,8704]{1,0:T(8,128)(2,1)S(1)} %reverse_terms.4.refs_2_), custom_call_target="tpu_custom_call" | custom-call | flops 1107296256 | bytes 1024 | tf_op jit(solution)/shard_map/reverse_terms/pallas_call | solution.py:34
  47.5 0.3 return.7
  47.9 1.8 %collective-permute-start.9 = (f32[165,128]{1,0:T(8,128)S(1)}, f32[165,128]{1,0:T(8,128)S(1)}, u32[]{:S(2)}, u32[]{:S(2)}) collective-permute-start(f32[165,128]{1,0:T(8,128)S(1)} %return.7), channel_id=1, source_target_pairs={{0,16},{16,0},{1,17},{17,1},{2,18},{18,2},{3,19},{19,3},{4,20},{20... | collective-permute-start | bytes 253448 | tf_op jit(solution)/shard_map/ppermute | solution.py:65
  49.7 10.0 %forward_terms.2.refs_2_ = bf16[352,8704]{1,0:T(8,128)(2,1)S(1)} custom-call(s32[64]{0:T(128)S(1)} %bitcast.8, s32[68,128]{1,0:T(8,128)S(1)} %get-tuple-element.13.refs_1_, bf16[64,176,256]{2,1,0:T(8,128)(2,1)S(1)} %order_operators.1.refs_2_, bf16[165,256]{1,0:T(8,128)(2,1)S(1)} %copy-done.1, bf16[165,128]{1,0:T(8,128)(2,1)S(1)} %collective-permute-done.refs_2_.refs_4_, ...), custom_call_target="tpu_custom_call" | custom-call | flops 1660944384 | bytes 1024 | tf_op jit(solution)/shard_map/forward_terms/pallas_call | solution.py:34
  59.7 3.5 %forward_terms.3.refs_2_ = f32[165,256]{1,0:T(8,128)S(1)} custom-call(s32[64]{0:T(128)S(1)} %bitcast.9, s32[68,128]{1,0:T(8,128)S(1)} %get-tuple-element.14.refs_1_, bf16[352,8704]{1,0:T(8,128)(2,1)S(1)} %forward_terms.2.refs_2_), custom_call_target="tpu_custom_call" | custom-call | flops 738197504 | bytes 1024 | tf_op jit(solution)/shard_map/forward_terms/pallas_call | solution.py:34
  63.2 1.1 %sum.1 = f32[165,256]{1,0:T(8,128)} custom-call(s32[5,128]{1,0:T(8,128)S(1)} %copy-done.2, f32[165,256]{1,0:T(8,128)S(1)} %get-tuple-element.15.refs_1_, f32[165,256]{1,0:T(8,128)S(1)} %forward_terms.3.refs_2_, f32[165,128]{1,0:T(8,128)S(1)} %collective-permute-done.9.refs_3_, f32[165,128]{1,0:T(8,128)S(1)} %collective-permute-done.8.refs_2_.refs_4_, ...), custom_call_target="tpu_custom_call" | custom-call | bytes 1024 | tf_op jit(solution)/shard_map/sum/pallas_call | solution.py:34
  (18 shorter events, 0.0 us)
Async XLA Ops:
  0.0 6.5 %copy-start.5 = (s32[64,1]{0,1:T(1,128)S(1)}, s32[64,1]{0,1:T(1,128)}, u32[]{:S(2)}) copy-start(s32[64,1]{0,1:T(1,128)} %param.11) | copy-start | bytes 772
  0.0 2.5 %copy-start = (bf16[64,165,165]{2,0,1:T(8,128)(2,1)S(1)}, bf16[64,165,165]{2,0,1:T(8,128)(2,1)}, u32[]{:S(2)}) copy-start(bf16[64,165,165]{2,0,1:T(8,128)(2,1)} %param.7) | copy-start | bytes 10454404
  2.5 4.0 %copy-start.3 = (s32[64,128]{1,0:T(8,128)S(1)}, s32[64,128]{1,0:T(8,128)}, u32[]{:S(2)}) copy-start(s32[64,128]{1,0:T(8,128)} %target_ref.1) | copy-start | bytes 98308
  2.6 4.0 %copy-start.4 = (s32[64,128]{1,0:T(8,128)S(1)}, s32[64,128]{1,0:T(8,128)}, u32[]{:S(2)}) copy-start(s32[64,128]{1,0:T(8,128)} %source_ref.1) | copy-start | bytes 98308
  2.6 5.5 %copy-start.1 = (bf16[165,256]{1,0:T(8,128)(2,1)S(1)}, bf16[165,256]{1,0:T(8,128)(2,1)}, u32[]{:S(2)}) copy-start(bf16[165,256]{1,0:T(8,128)(2,1)} %refs_3_.3) | copy-start | bytes 253444
  8.0 14.8 %copy-start.2 = (s32[5,128]{1,0:T(8,128)S(1)}, s32[5,128]{1,0:T(8,128)}, u32[]{:S(2)}) copy-start(s32[5,128]{1,0:T(8,128)} %refs_0_.19) | copy-start | bytes 7684
  19.8 7.5 %collective-permute-start.5 = (f32[165,128]{1,0:T(8,128)S(1)}, f32[165,128]{1,0:T(8,128)S(1)}, u32[]{:S(2)}, u32[]{:S(2)}) collective-permute-start(f32[165,128]{1,0:T(8,128)S(1)} %get-tuple-element.20), channel_id=1, source_target_pairs={{0,1},{1,0},{2,3},{3,2},{4,5},{5,4},{6,7},{7,6},{8,9},{9,8},{10,11... | collective-permute-start | bytes 253448 | tf_op jit(solution)/shard_map/ppermute | solution.py:65
  23.0 4.1 %collective-permute-start = (bf16[165,128]{1,0:T(8,128)(2,1)S(1)}, bf16[165,128]{1,0:T(8,128)(2,1)S(1)}, u32[]{:S(2)}, u32[]{:S(2)}) collective-permute-start(bf16[165,128]{1,0:T(8,128)(2,1)S(1)} %export.5), channel_id=1, source_target_pairs={{0,16},{16,0},{1,17},{17,1},{2,18},{18,2},{3,19},{19,3},{4,20},{20... | collective-permute-start | bytes 126728 | tf_op jit(solution)/shard_map/ppermute | solution.py:65
  27.3 2.0 %collective-permute-start.1 = (bf16[165,128]{1,0:T(8,128)(2,1)S(1)}, bf16[165,128]{1,0:T(8,128)(2,1)S(1)}, u32[]{:S(2)}, u32[]{:S(2)}) collective-permute-start(bf16[165,128]{1,0:T(8,128)(2,1)S(1)} %export.6), channel_id=1, source_target_pairs={{0,8},{8,0},{1,9},{9,1},{2,10},{10,2},{3,11},{11,3},{4,12},{12,4},... | collective-permute-start | bytes 126728 | tf_op jit(solution)/shard_map/ppermute | solution.py:65
  27.5 7.7 %collective-permute-start.6 = (f32[165,128]{1,0:T(8,128)S(1)}, f32[165,128]{1,0:T(8,128)S(1)}, u32[]{:S(2)}, u32[]{:S(2)}) collective-permute-start(f32[165,128]{1,0:T(8,128)S(1)} %return.4), channel_id=1, source_target_pairs={{0,2},{2,0},{1,3},{3,1},{4,6},{6,4},{5,7},{7,5},{8,10},{10,8},{9,1... | collective-permute-start | bytes 253448 | tf_op jit(solution)/shard_map/ppermute | solution.py:65
  29.5 6.6 %collective-permute-start.2 = (bf16[165,128]{1,0:T(8,128)(2,1)S(1)}, bf16[165,128]{1,0:T(8,128)(2,1)S(1)}, u32[]{:S(2)}, u32[]{:S(2)}) collective-permute-start(bf16[165,128]{1,0:T(8,128)(2,1)S(1)} %export.7), channel_id=1, source_target_pairs={{0,4},{4,0},{1,5},{5,1},{2,6},{6,2},{3,7},{7,3},{8,12},{12,8},{9,1... | collective-permute-start | bytes 126728 | tf_op jit(solution)/shard_map/ppermute | solution.py:65
  35.6 7.2 %collective-permute-start.7 = (f32[165,128]{1,0:T(8,128)S(1)}, f32[165,128]{1,0:T(8,128)S(1)}, u32[]{:S(2)}, u32[]{:S(2)}) collective-permute-start(f32[165,128]{1,0:T(8,128)S(1)} %return.5), channel_id=1, source_target_pairs={{0,4},{4,0},{1,5},{5,1},{2,6},{6,2},{3,7},{7,3},{8,12},{12,8},{9,1... | collective-permute-start | bytes 253448 | tf_op jit(solution)/shard_map/ppermute | solution.py:65
  36.3 4.1 %collective-permute-start.3 = (bf16[165,128]{1,0:T(8,128)(2,1)S(1)}, bf16[165,128]{1,0:T(8,128)(2,1)S(1)}, u32[]{:S(2)}, u32[]{:S(2)}) collective-permute-start(bf16[165,128]{1,0:T(8,128)(2,1)S(1)} %export.8), channel_id=1, source_target_pairs={{0,2},{2,0},{1,3},{3,1},{4,6},{6,4},{5,7},{7,5},{8,10},{10,8},{9,1... | collective-permute-start | bytes 126728 | tf_op jit(solution)/shard_map/ppermute | solution.py:65
  40.7 9.0 %collective-permute-start.4 = (bf16[165,128]{1,0:T(8,128)(2,1)S(1)}, bf16[165,128]{1,0:T(8,128)(2,1)S(1)}, u32[]{:S(2)}, u32[]{:S(2)}) collective-permute-start(bf16[165,128]{1,0:T(8,128)(2,1)S(1)} %export.9), channel_id=1, source_target_pairs={{0,1},{1,0},{2,3},{3,2},{4,5},{5,4},{6,7},{7,6},{8,9},{9,8},{10,11... | collective-permute-start | bytes 126728 | tf_op jit(solution)/shard_map/ppermute | solution.py:65
  43.0 4.5 %collective-permute-start.8 = (f32[165,128]{1,0:T(8,128)S(1)}, f32[165,128]{1,0:T(8,128)S(1)}, u32[]{:S(2)}, u32[]{:S(2)}) collective-permute-start(f32[165,128]{1,0:T(8,128)S(1)} %return.6), channel_id=1, source_target_pairs={{0,8},{8,0},{1,9},{9,1},{2,10},{10,2},{3,11},{11,3},{4,12},{12,4},... | collective-permute-start | bytes 253448 | tf_op jit(solution)/shard_map/ppermute | solution.py:65
  47.9 15.4 %collective-permute-start.9 = (f32[165,128]{1,0:T(8,128)S(1)}, f32[165,128]{1,0:T(8,128)S(1)}, u32[]{:S(2)}, u32[]{:S(2)}) collective-permute-start(f32[165,128]{1,0:T(8,128)S(1)} %return.7), channel_id=1, source_target_pairs={{0,16},{16,0},{1,17},{17,1},{2,18},{18,2},{3,19},{19,3},{4,20},{20... | collective-permute-start | bytes 253448 | tf_op jit(solution)/shard_map/ppermute | solution.py:65

commit v3 on v2

v3 whole, which is shorter than its diff:
```python
import math

import jax
import jax.numpy as jnp
from jax import lax
from jax.experimental import pallas as pl
from jax.experimental.pallas import tpu as pltpu
from jax.sharding import PartitionSpec as P

LANES = 128
CHUNK = 512
PICK_PART = 8
SCATTER_PART = 8
TILE = 16
AXES = ("gx", "gy")
VMEM = pl.BlockSpec(memory_space=pltpu.VMEM)
BF16 = jnp.bfloat16
F32 = jnp.float32


def up(size, multiple):
    return -(-size // multiple) * multiple


def params(mebibytes):
    return pltpu.CompilerParams(vmem_limit_bytes=mebibytes * 1024 * 1024)


def shape(rows, columns, kind):
    return jax.ShapeDtypeStruct((rows, columns), kind)


def call(kernel, out_shape, args, after, limit=4, scratch=(), us=0.3):
    single = not isinstance(out_shape, (tuple, list))
    return pl.pallas_call(
        lambda _, *refs: kernel(*refs),
        out_shape=out_shape,
        in_specs=[pl.BlockSpec(memory_space=pl.ANY)] + [VMEM] * len(args),
        out_specs=VMEM if single else [VMEM] * len(out_shape),
        scratch_shapes=list(scratch),
        compiler_params=params(limit),
        cost_estimate=takes(us),
    )(after, *args)


def takes(us):
    return pl.CostEstimate(flops=int(us * 1e9), bytes_accessed=0, transcendentals=0)


def dot(a, b):
    return jnp.dot(a, b, preferred_element_type=F32)


def dot_nt(a, b):
    return lax.dot_general(a, b, (((1,), (1,)), ((), ())), preferred_element_type=F32)


def halves(wide):
    high = wide.astype(BF16)
    return high, (wide - high.astype(F32)).astype(BF16)


def from_partner(block, distance):
    count = lax.axis_size(AXES)
    route = []
    for low in range(count):
        high = low | 1 << distance
        if high != low and high < count:
            route += [(low, high), (high, low)]
    return lax.ppermute(block, AXES, route)


def one_hot(row, first, height):
    place = lax.broadcasted_iota(jnp.int32, (height, row.shape[1]), 0)
    return jnp.where(place == row - first, 1.0, 0.0).astype(BF16)


def hot_columns(index_ref, row, count, first, height):
    columns = []
    for n in range(count):
        index = index_ref[pl.ds(row + n, 1), :]
        blocks = [
            one_hot(index, first + low, min(LANES, height - low))
            for low in range(0, height, LANES)
        ]
        columns.append(jnp.concatenate(blocks, axis=0))
    return jnp.concatenate(columns, axis=1)


def for_parts(total, largest, body):
    chunks = pl.cdiv(total, CHUNK)
    chunks = jnp.where(lax.rem(chunks, 4) == 3, chunks + 1, chunks)

    def whole(k, _):
        body(k * largest, largest)
        return 0

    lax.fori_loop(0, chunks // largest, whole, 0)
    size = largest // 2
    while size:
        done = chunks // (2 * size) * (2 * size)

        @pl.when(lax.rem(chunks // size, 2) == 1)
        def _(done=done, size=size):
            body(done, size)

        size //= 2


def pick_columns(total, index_ref, pool, picked):
    def pick(first, size):
        lanes = size * CHUNK
        row = first * (CHUNK // LANES)
        hot = hot_columns(index_ref, row, lanes // LANES, 0, pool.shape[1])
        at = pl.ds(pl.multiple_of(first * CHUNK, CHUNK), lanes)
        picked[:, at] = dot(pool[...], hot).astype(BF16)

    for_parts(total, PICK_PART, pick)


def pack_kernel(
    classes, meta_ref, mult_ref, packed_target, packed_source, info_ref, picked, pool
):
    lane = lax.broadcasted_iota(jnp.int32, (1, LANES), 1)

    def place(c, offset):
        info_ref[pl.ds(c, 1), :] = jnp.full((1, LANES), offset, jnp.int32)
        shift = lax.rem(offset, LANES)
        row = offset // LANES
        keep = lane >= shift
        for first, out in ((0, packed_target), (classes, packed_source)):
            turned = pltpu.roll(meta_ref[pl.ds(first + c, 1), :], shift, 1)
            out[pl.ds(row, 1), :] = jnp.where(keep, turned, out[pl.ds(row, 1), :])
            out[pl.ds(row + 1, 1), :] = turned
        return offset + meta_ref[2 * classes + c, 0]

    total = lax.fori_loop(0, classes, place, 0, unroll=8)
    info_ref[classes:, :] = jnp.full((8, LANES), total, jnp.int32)
    position = lax.broadcasted_iota(jnp.int32, packed_target.shape, 0) * LANES
    position = position + lax.broadcasted_iota(jnp.int32, packed_target.shape, 1)
    for out in (packed_target, packed_source):
        out[...] = jnp.where(position < total, out[...], -1)

    pool[...] = jnp.zeros_like(pool)
    pool[: mult_ref.shape[0], :] = mult_ref[...]
    pick_columns(total, packed_target, pool, picked)


def order_kernel(op_ref, ordered):
    for i in range(0, op_ref.shape[0], TILE):
        size = min(TILE, op_ref.shape[0] - i)
        block = jnp.swapaxes(op_ref[i : i + size], 0, 1)
        ordered[:, i : i + size, :] = block


def pick_kernel(starts, info_ref, index_ref, *refs):
    segs = refs[: len(starts)]
    picked, pool = refs[len(starts) :]
    pool[...] = jnp.zeros_like(pool)
    for seg, first in zip(segs, starts):
        pool[: seg.shape[0], first : first + seg.shape[1]] = seg[...]
    pick_columns(info_ref[info_ref.shape[0] - 1, 0], index_ref, pool, picked)


def apply_kernel(flip, info_ref, op_ref, picked, out_ref):
    classes, rows, depth = op_ref.shape
    last = pl.multiple_of(info_ref[classes, 0] // CHUNK * CHUNK, CHUNK)
    out_ref[:, pl.ds(last, 2 * CHUNK)] = jnp.zeros((2 * rows, 2 * CHUNK), BF16)
    lane = lax.broadcasted_iota(jnp.int32, (rows, LANES), 1)

    def apply(c, _):
        offset = info_ref[c, 0]
        start = pl.multiple_of(offset // LANES * LANES, LANES)
        c_op = classes - 1 - c if flip else c
        new = dot(op_ref[c_op], picked[:depth, pl.ds(start, 2 * LANES)])
        keep = lane >= offset - start
        for first, part in zip((0, rows), halves(new)):
            at = pl.ds(start, LANES)
            old = out_ref[first : first + rows, at]
            out_ref[first : first + rows, at] = jnp.where(keep, part[:, :LANES], old)
            out_ref[first : first + rows, pl.ds(start + LANES, LANES)] = part[:, LANES:]
        return 0

    lax.fori_loop(0, classes, apply, 0, unroll=16)


def add_terms(first, info_ref, index_ref, terms_ref, sums):
    def add(part, size):
        lanes = size * CHUNK
        row = part * (CHUNK // LANES)
        hot = hot_columns(index_ref, row, lanes // LANES, first, sums.shape[1])
        at = pl.ds(pl.multiple_of(part * CHUNK, CHUNK), lanes)
        sums[...] += dot_nt(terms_ref[:, at], hot)

    for_parts(info_ref[info_ref.shape[0] - 1, 0], SCATTER_PART, add)


def scatter_kernel(starts, info_ref, index_ref, terms_ref, *refs):
    outs, sums = refs[:-1], refs[-1]
    sums[...] = jnp.zeros_like(sums)
    add_terms(starts[0], info_ref, index_ref, terms_ref, sums)
    rows = sums.shape[0] // 2
    for out, start in zip(outs, starts):
        low = start - starts[0]
        at = slice(low, low + out.shape[1])
        out[...] = sums[: out.shape[0], at] + sums[rows : rows + out.shape[0], at]


def export_kernel(starts, list_row, meta_ref, *refs):
    segs, out_ref = refs[: len(starts)], refs[len(starts)]
    row = meta_ref[list_row : list_row + 1, :]
    out = 0.0
    for seg, first in zip(segs, starts):
        out = out + dot(seg[...], one_hot(row, first, seg.shape[1]))
    out_ref[...] = out.astype(BF16)
    for own in refs[len(starts) + 1 :]:
        own[...] = segs[0][...]


def came_back(first, row, meta_ref, returned, width):
    out = 0.0
    for i, ref in enumerate(returned):
        hot = one_hot(meta_ref[row + i : row + i + 1, :], first, width)
        high, low = halves(ref[...])
        out = out + dot_nt(high, hot) + dot_nt(low, hot)
    return out


def return_kernel(first, row, meta_ref, base_ref, *refs):
    returned, out_ref = refs[:-1], refs[-1]
    out_ref[...] = base_ref[...] + came_back(first, row, meta_ref, returned, out_ref.shape[1])


def local_kernel(
    row, meta_ref, info_ref, target_ref, ahead_ref, source_ref, back_ref, *refs
):
    returned, (out_ref, sums) = refs[:-2], refs[-2:]
    count, rows = out_ref.shape[0], sums.shape[0] // 2
    sums[...] = jnp.zeros_like(sums)
    add_terms(0, info_ref, target_ref, ahead_ref, sums)
    add_terms(0, info_ref, source_ref, back_ref, sums)
    out = came_back(0, row, meta_ref, returned, out_ref.shape[1])
    out_ref[...] = out + (sums[:count, :] + sums[rows : rows + count, :])


def per_device(multipoles, operators, boundary, pair_target, pair_source, pair_count):
    coefficients, cells = multipoles.shape
    cuts, sent = boundary.shape
    classes, width = pair_target.shape
    starts = [0] + [cells + cut * sent for cut in range(cuts)]
    sizes = [cells] + [sent] * cuts
    pool_width = cells + cuts * sent
    rows = up(coefficients, TILE)
    packed = classes * width + 2 * CHUNK + LANES

    index_shape = shape(packed // LANES, LANES, jnp.int32)

    def pick(segments, index, after):
        height = sum(segment.shape[1] for segment in segments)
        return call(
            lambda *refs: pick_kernel(starts, *refs),
            shape(rows, packed, BF16),
            [info, index] + list(segments),
            after,
            limit=16,
            scratch=[pltpu.VMEM((rows, height), BF16)],
            us=2.0,
        )

    def apply(columns, flip, after):
        return call(
            lambda *refs: apply_kernel(flip, *refs),
            shape(2 * rows, packed, BF16),
            [info, ordered, columns],
            after,
            limit=8,
            us=5.0,
        )

    def scatter(values, index, first, last, after):
        height = sum(sizes[first:last])
        return call(
            lambda *refs: scatter_kernel(starts[first:last], *refs),
            [shape(coefficients, size, F32) for size in sizes[first:last]],
            [info, index, values],
            after,
            limit=8,
            scratch=[pltpu.VMEM((2 * rows, height), F32)],
            us=1.0,
        )

    segments, returned, sums = [multipoles], [], [None] * (cuts + 1)
    meta = jnp.concatenate(
        [pair_target, pair_source, jnp.broadcast_to(pair_count, pair_target.shape), boundary], axis=0
    )

    def export(after):
        cut = len(segments) - 1
        with jax.named_scope("export"):
            out = [shape(coefficients, sent, BF16)]
            if cut == 0:
                out.append(shape(coefficients, cells, BF16))
            exported, *own = call(
                lambda *refs: export_kernel(starts[: cut + 1], 3 * classes + cut, *refs),
                out,
                [meta] + segments,
                after,
            )
            segments[:1] = own or segments[:1]
        segments.append(from_partner(exported, cuts - 1 - cut))
        return exported

    def give_back(after):
        cut = cuts - 1 - len(returned)
        outgoing = sums[cut + 1]
        if returned:
            with jax.named_scope("return"):
                outgoing = call(
                    lambda *refs: return_kernel(starts[cut + 1], 3 * classes + cut + 1, *refs),
                    shape(coefficients, sent, F32),
                    [meta, outgoing] + returned,
                    after,
                )
        returned.insert(0, from_partner(outgoing, cuts - 1 - cut))
        return outgoing

    def more_sums(after):
        last = max((cut for cut in range(1, cuts + 1) if sums[cut] is None), default=0)
        if last == 0:
            return after
        first = max(last - 1, 1)
        with jax.named_scope("reverse_sums"):
            sums[first : last + 1] = scatter(back, sources, first, last + 1, after)
        return sums[first]

    step = export(meta)
    with jax.named_scope("pack_slots"):
        targets, sources, info, picked = pl.pallas_call(
            lambda _, *refs: pack_kernel(classes, *refs),
            out_shape=[
                index_shape,
                index_shape,
                shape(classes + 8, LANES, jnp.int32),
                shape(rows, packed, BF16),
            ],
            in_specs=[pl.BlockSpec(memory_space=pl.ANY), VMEM, VMEM],
            out_specs=[VMEM] * 4,
            scratch_shapes=[pltpu.VMEM((rows, cells), BF16)],
            compiler_params=params(8),
            cost_estimate=takes(2.5),
        )(step, meta, segments[0])
    step = export(info)
    with jax.named_scope("order_operators"):
        ordered = call(
            order_kernel,
            jax.ShapeDtypeStruct((classes, rows, coefficients), BF16),
            [operators.transpose(1, 0, 2)],
            step,
            limit=8,
            us=1.3,
        )
    step = export(ordered)
    with jax.named_scope("reverse_terms"):
        back = apply(picked, True, step)
    step = export(back)
    step = more_sums(step)
    step = give_back(step)
    while len(segments) <= cuts:
        step = export(step)
    step = more_sums(step)
    step = give_back(step)
    with jax.named_scope("forward_columns"):
        ahead = pick(segments, sources, step)
    step = give_back(ahead)
    with jax.named_scope("forward_terms"):
        ahead = apply(ahead, False, step)
    step = ahead
    while len(returned) < cuts:
        step = give_back(step)
        step = more_sums(step)
    with jax.named_scope("local_sums"):
        local = call(
            lambda *refs: local_kernel(3 * classes + 1, *refs),
            shape(coefficients, cells, F32),
            [meta, info, targets, ahead, sources, back] + returned[1:],
            step,
            limit=8,
            scratch=[pltpu.VMEM((2 * rows, cells), F32)],
            us=2.0,
        )
    with jax.named_scope("last_sum"):
        return call(
            lambda *refs: return_kernel(0, 3 * classes, *refs),
            shape(coefficients, cells, F32),
            [meta, local, returned[0]],
            local,
        )


def solution(mesh):
    split = P(None, AXES)
    return jax.shard_map(
        per_device,
        mesh=mesh,
        in_specs=(split, P(), split, split, split, split),
        out_specs=split,
        check_vma=False,
    )
```

time: 64 us -> 44.9 us (0.70)
  Pallas kernels: 41.9 us -> 25 us
  waiting for transfers between devices: 6.81 us -> 3.26 us
  starting transfers between devices: 12.8 us -> 13.9 us
  local copies, waits for them, and re-layouts: 2.57 us -> 1.55 us
  other arithmetic: 0 us -> 0.88 us
    pallas_call x18 -> x19, Pallas kernels: 41.9 us -> 25 us  [the longest x18 23 us: call(): pl.pallas_call(lambda _, *refs: kernel(*refs), out_shape=out_shape, in_sp...]
    ppermute x10, waiting for transfers between devices: 6.81 us -> 3.26 us  [from_partner(): return lax.ppermute(block, AXES, route)]
    unnamed x12 -> x6, local copies, waits for them, and re-layouts: 2.57 us -> 0.89 us
    ppermute x10, starting transfers between devices: 12.8 us -> 13.9 us  [from_partner(): return lax.ppermute(block, AXES, route)]
    concatenate x0 -> x1, other arithmetic: none -> 0.88 us  [per_device(): jnp.concatenate([pair_target, pair_source, jnp.broadcast_to(pair_count, p...]
    concatenate x0 -> x1, local copies, waits for them, and re-layouts: none -> 0.66 us  [per_device(): jnp.concatenate([pair_target, pair_source, jnp.broadcast_to(pair_count, p...]
  transfers between devices with their start and end apart: 10 -> 10, of which waited for: 3 -> 4; matrix products, arithmetic and copies ran while one was open for 0% -> 0% of each run, Pallas kernels for 37% -> 50%
where the time goes in v3:
time: 44.9 us; the launch traced here: 44.8 us
  Pallas kernels  25 us (56%)
  starting transfers between devices  13.9 us (31%)
  waiting for transfers between devices  3.26 us (7%)
  local copies, waits for them, and re-layouts  1.55 us (3%)
  other arithmetic  0.88 us (2%)
    pallas_call x18, Pallas kernels, call(): pl.pallas_call(lambda _, *refs: kernel(*refs), out_shape=out_shape, in_sp...  23 us
    ppermute x10, starting transfers between devices, from_partner(): return lax.ppermute(block, AXES, route)  13.9 us
    ppermute x10, waiting for transfers between devices, from_partner(): return lax.ppermute(block, AXES, route)  3.26 us
    pallas_call x1, Pallas kernels, per_device(): pl.pallas_call(lambda _, *refs: pack_kernel(classes, *refs), out_shape=[i...  1.96 us
  transfers between devices with their start and end apart: 10, of which 4 were waited for; matrix products, arithmetic and copies ran while one was open for 0% of the time, Pallas kernels for 50%

profile of v3, /device:TPU:0, one launch (start us, length us, event | category | flops | bytes accessed | tf_op | source)
XLA Modules:
  0.0 44.8 jit_solution(2793412989987258199)
XLA Ops:
  0.0 0.7 %pad.2.clone = s32[197]{0:T(256)S(1)} pad(s32[64]{0:T(128)} %bitcast.5, s32[]{:T(128)} %constant.1), padding=128_5 | pad | bytes 1048 | tf_op jit(solution)/shard_map/concatenate | solution.py:293
  0.7 0.9 %pad_add_fusion._.refs_0_ = s32[197,128]{1,0:T(8,128)S(1)} fusion(s32[5,128]{1,0:T(8,128)} %param.8, s32[64,128]{1,0:T(8,128)} %param.10, s32[64,128]{1,0:T(8,128)} %param.9, s32[197]{0:T(256)S(1)} %pad.2.clone), kind=kLoop, calls=%fused_computation | loop fusion | flops 75648 | bytes 169748 | tf_op jit(solution)/shard_map/concatenate | solution.py:293
  1.6 0.9 %copy-done = bf16[165,256]{1,0:T(8,128)(2,1)S(1)} copy-done((bf16[165,256]{1,0:T(8,128)(2,1)S(1)}, bf16[165,256]{1,0:T(8,128)(2,1)}, u32[]{:S(2)}) %copy-start) | copy-done | bytes 84504
  2.6 3.0 %collective-permute-start = (bf16[165,128]{1,0:T(8,128)(2,1)S(1)}, bf16[165,128]{1,0:T(8,128)(2,1)S(1)}, u32[]{:S(2)}, u32[]{:S(2)}) collective-permute-start(bf16[165,128]{1,0:T(8,128)(2,1)S(1)} %get-tuple-element.15._), channel_id=1, source_target_pairs={{0,16},{16,0},{1,17},{17,1},{2,18},{18,2},{3,19},{19,3},{4,20},{20... | collective-permute-start | bytes 126728 | tf_op jit(solution)/shard_map/ppermute | solution.py:70
  5.6 2.0 %pack_slots.1 = (s32[73,128]{1,0:T(8,128)S(1)}, s32[73,128]{1,0:T(8,128)S(1)}, s32[72,128]{1,0:T(8,128)S(1)}, bf16[176,9344]{1,0:T(8,128)(2,1)S(1)}) custom-call(bf16[165,128]{1,0:T(8,128)(2,1)S(1)} %get-tuple-element.15._, s32[197,128]{1,0:T(8,128)S(1)} %pad_add_fusion._.refs_0_, bf16[165,256]{1,0:T(8,128)(2,1)S(1)} %get-tuple-element.16.refs_1_.refs_2_), custom_call_target="tpu_custom_call" | custom-call | flops 2500000000 | tf_op jit(solution)/shard_map/pack_slots/pallas_call | solution.py:338
  7.9 1.3 %order_operators.1._.refs_1_ = bf16[64,176,165]{2,1,0:T(8,128)(2,1)S(1)} custom-call(bf16[165,128]{1,0:T(8,128)(2,1)S(1)} %export.6._, bf16[165,64,165]{2,1,0:T(8,128)(2,1)S(1)} %bitcast.4), custom_call_target="tpu_custom_call" | custom-call | flops 1300000000 | tf_op jit(solution)/shard_map/order_operators/pallas_call | solution.py:35
  9.2 0.2 export.7._
  9.4 3.2 %collective-permute-start.2 = (bf16[165,128]{1,0:T(8,128)(2,1)S(1)}, bf16[165,128]{1,0:T(8,128)(2,1)S(1)}, u32[]{:S(2)}, u32[]{:S(2)}) collective-permute-start(bf16[165,128]{1,0:T(8,128)(2,1)S(1)} %export.7._), channel_id=1, source_target_pairs={{0,4},{4,0},{1,5},{5,1},{2,6},{6,2},{3,7},{7,3},{8,12},{12,8},{9,1... | collective-permute-start | bytes 126728 | tf_op jit(solution)/shard_map/ppermute | solution.py:70
  12.6 4.6 %reverse_terms.1._.refs_2_.refs_5_ = bf16[352,9344]{1,0:T(8,128)(2,1)S(1)} custom-call(bf16[165,128]{1,0:T(8,128)(2,1)S(1)} %export.7._, s32[72,128]{1,0:T(8,128)S(1)} %get-tuple-element.17._.refs_0_.refs_1_, bf16[64,176,165]{2,1,0:T(8,128)(2,1)S(1)} %order_operators.1._.refs_1_, bf16[176,9344]{1,0:T(8,128)(2,1)S(1)} %get-tuple-element.18.refs_2_), custom_call_target="tpu_custom_call" | custom-call | flops 5000000000 | tf_op jit(solution)/shard_map/reverse_terms/pallas_call | solution.py:35
  17.2 0.2 export.8._
  17.5 1.6 %collective-permute-start.3 = (bf16[165,128]{1,0:T(8,128)(2,1)S(1)}, bf16[165,128]{1,0:T(8,128)(2,1)S(1)}, u32[]{:S(2)}, u32[]{:S(2)}) collective-permute-start(bf16[165,128]{1,0:T(8,128)(2,1)S(1)} %export.8._), channel_id=1, source_target_pairs={{0,2},{2,0},{1,3},{3,1},{4,6},{6,4},{5,7},{7,5},{8,10},{10,8},{9,1... | collective-permute-start | bytes 126728 | tf_op jit(solution)/shard_map/ppermute | solution.py:70
  19.1 1.4 %reverse_sums.3 = (f32[165,128]{1,0:T(8,128)S(1)}, f32[165,128]{1,0:T(8,128)S(1)}) custom-call(bf16[165,128]{1,0:T(8,128)(2,1)S(1)} %export.8._, s32[72,128]{1,0:T(8,128)S(1)} %get-tuple-element.17._.refs_0_.refs_1_, s32[73,128]{1,0:T(8,128)S(1)} %get-tuple-element.19.refs_1_.refs_4_, bf16[352,9344]{1,0:T(8,128)(2,1)S(1)} %reverse_terms.1._.refs_2_.refs_5_), custom_call_target="tpu_custom_call" | custom-call | flops 1000000000 | tf_op jit(solution)/shard_map/reverse_sums/pallas_call | solution.py:35
  20.5 1.3 %collective-permute-start.4 = (f32[165,128]{1,0:T(8,128)S(1)}, f32[165,128]{1,0:T(8,128)S(1)}, u32[]{:S(2)}, u32[]{:S(2)}) collective-permute-start(f32[165,128]{1,0:T(8,128)S(1)} %get-tuple-element.20._), channel_id=1, source_target_pairs={{0,1},{1,0},{2,3},{3,2},{4,5},{5,4},{6,7},{7,6},{8,9},{9,8},{10,11... | collective-permute-start | bytes 253448 | tf_op jit(solution)/shard_map/ppermute | solution.py:70
  21.7 0.3 export.9._
  22.0 1.4 %collective-permute-start.5 = (bf16[165,128]{1,0:T(8,128)(2,1)S(1)}, bf16[165,128]{1,0:T(8,128)(2,1)S(1)}, u32[]{:S(2)}, u32[]{:S(2)}) collective-permute-start(bf16[165,128]{1,0:T(8,128)(2,1)S(1)} %export.9._), channel_id=1, source_target_pairs={{0,1},{1,0},{2,3},{3,2},{4,5},{5,4},{6,7},{7,6},{8,9},{9,8},{10,11... | collective-permute-start | bytes 126728 | tf_op jit(solution)/shard_map/ppermute | solution.py:70
  23.4 1.4 %reverse_sums.4 = (f32[165,128]{1,0:T(8,128)S(1)}, f32[165,128]{1,0:T(8,128)S(1)}) custom-call(bf16[165,128]{1,0:T(8,128)(2,1)S(1)} %export.9._, s32[72,128]{1,0:T(8,128)S(1)} %get-tuple-element.17._.refs_0_.refs_1_, s32[73,128]{1,0:T(8,128)S(1)} %get-tuple-element.19.refs_1_.refs_4_, bf16[352,9344]{1,0:T(8,128)(2,1)S(1)} %reverse_terms.1._.refs_2_.refs_5_), custom_call_target="tpu_custom_call" | custom-call | flops 1000000000 | tf_op jit(solution)/shard_map/reverse_sums/pallas_call | solution.py:35
  24.8 0.7 %collective-permute-done.4.refs_2_.refs_3_.refs_4_.refs_5_.refs_9_ = f32[165,128]{1,0:T(8,128)S(1)} collective-permute-done((f32[165,128]{1,0:T(8,128)S(1)}, f32[165,128]{1,0:T(8,128)S(1)}, u32[]{:S(2)}, u32[]{:S(2)}) %collective-permute-start.4) | collective-permute-done | bytes 84512 | tf_op jit(solution)/shard_map/ppermute | solution.py:70
  25.5 0.2 return.4._
  25.7 0.6 %collective-permute-start.6 = (f32[165,128]{1,0:T(8,128)S(1)}, f32[165,128]{1,0:T(8,128)S(1)}, u32[]{:S(2)}, u32[]{:S(2)}) collective-permute-start(f32[165,128]{1,0:T(8,128)S(1)} %return.4._), channel_id=1, source_target_pairs={{0,2},{2,0},{1,3},{3,1},{4,6},{6,4},{5,7},{7,5},{8,10},{10,8},{9,1... | collective-permute-start | bytes 253448 | tf_op jit(solution)/shard_map/ppermute | solution.py:70
  26.3 2.3 %forward_columns.1._.refs_2_ = bf16[176,9344]{1,0:T(8,128)(2,1)S(1)} custom-call(f32[165,128]{1,0:T(8,128)S(1)} %return.4._, s32[72,128]{1,0:T(8,128)S(1)} %get-tuple-element.17._.refs_0_.refs_1_, s32[73,128]{1,0:T(8,128)S(1)} %get-tuple-element.19.refs_1_.refs_4_, bf16[165,256]{1,0:T(8,128)(2,1)S(1)} %get-tuple-element.16.refs_1_.refs_2_, ...), custom_call_target="tpu_custom_call" | custom-call | flops 2000000000 | tf_op jit(solution)/shard_map/forward_columns/pallas_call | solution.py:35
  28.7 1.6 %collective-permute-done.6.refs_2_.refs_3_.refs_4_.refs_8_ = f32[165,128]{1,0:T(8,128)S(1)} collective-permute-done((f32[165,128]{1,0:T(8,128)S(1)}, f32[165,128]{1,0:T(8,128)S(1)}, u32[]{:S(2)}, u32[]{:S(2)}) %collective-permute-start.6) | collective-permute-done | bytes 84512 | tf_op jit(solution)/shard_map/ppermute | solution.py:70
  30.3 0.3 return.5._
  30.5 1.2 %collective-permute-start.7 = (f32[165,128]{1,0:T(8,128)S(1)}, f32[165,128]{1,0:T(8,128)S(1)}, u32[]{:S(2)}, u32[]{:S(2)}) collective-permute-start(f32[165,128]{1,0:T(8,128)S(1)} %return.5._), channel_id=1, source_target_pairs={{0,4},{4,0},{1,5},{5,1},{2,6},{6,2},{3,7},{7,3},{8,12},{12,8},{9,1... | collective-permute-start | bytes 253448 | tf_op jit(solution)/shard_map/ppermute | solution.py:70
  31.7 4.6 %forward_terms.1._.refs_3_ = bf16[352,9344]{1,0:T(8,128)(2,1)S(1)} custom-call(f32[165,128]{1,0:T(8,128)S(1)} %return.5._, s32[72,128]{1,0:T(8,128)S(1)} %get-tuple-element.17._.refs_0_.refs_1_, bf16[64,176,165]{2,1,0:T(8,128)(2,1)S(1)} %order_operators.1._.refs_1_, bf16[176,9344]{1,0:T(8,128)(2,1)S(1)} %forward_columns.1._.refs_2_), custom_call_target="tpu_custom_call" | custom-call | flops 5000000000 | tf_op jit(solution)/shard_map/forward_terms/pallas_call | solution.py:35
  36.3 0.5 %collective-permute-done.7.refs_2_.refs_3_.refs_7_ = f32[165,128]{1,0:T(8,128)S(1)} collective-permute-done((f32[165,128]{1,0:T(8,128)S(1)}, f32[165,128]{1,0:T(8,128)S(1)}, u32[]{:S(2)}, u32[]{:S(2)}) %collective-permute-start.7) | collective-permute-done | bytes 84512 | tf_op jit(solution)/shard_map/ppermute | solution.py:70
  36.9 0.3 return.6._
  37.3 1.3 %reverse_sums.5._.refs_1_ = f32[165,128]{1,0:T(8,128)S(1)} custom-call(f32[165,128]{1,0:T(8,128)S(1)} %return.6._, s32[72,128]{1,0:T(8,128)S(1)} %get-tuple-element.17._.refs_0_.refs_1_, s32[73,128]{1,0:T(8,128)S(1)} %get-tuple-element.19.refs_1_.refs_4_, bf16[352,9344]{1,0:T(8,128)(2,1)S(1)} %reverse_terms.1._.refs_2_.refs_5_), custom_call_target="tpu_custom_call" | custom-call | flops 1000000000 | tf_op jit(solution)/shard_map/reverse_sums/pallas_call | solution.py:35
  38.6 0.4 return.7._
  38.9 1.5 %collective-permute-start.9 = (f32[165,128]{1,0:T(8,128)S(1)}, f32[165,128]{1,0:T(8,128)S(1)}, u32[]{:S(2)}, u32[]{:S(2)}) collective-permute-start(f32[165,128]{1,0:T(8,128)S(1)} %return.7._), channel_id=1, source_target_pairs={{0,16},{16,0},{1,17},{17,1},{2,18},{18,2},{3,19},{19,3},{4,20},{20... | collective-permute-start | bytes 253448 | tf_op jit(solution)/shard_map/ppermute | solution.py:70
  40.5 3.1 %local_sums.1._.refs_1_ = f32[165,256]{1,0:T(8,128)S(1)} custom-call(f32[165,128]{1,0:T(8,128)S(1)} %return.7._, s32[197,128]{1,0:T(8,128)S(1)} %pad_add_fusion._.refs_0_, s32[72,128]{1,0:T(8,128)S(1)} %get-tuple-element.17._.refs_0_.refs_1_, s32[73,128]{1,0:T(8,128)S(1)} %get-tuple-element.24.refs_2_, bf16[352,9344]{1,0:T(8,128)(2,1)S(1)} %forward_terms.1._.refs_3_, ...), custom_call_target="tpu_custom_call" | custom-call | flops 2000000000 | tf_op jit(solution)/shard_map/local_sums/pallas_call | solution.py:35
  43.5 0.4 collective-permute-done.9.refs_2_
  43.9 0.9 %last_sum.1 = f32[165,256]{1,0:T(8,128)} custom-call(f32[165,256]{1,0:T(8,128)S(1)} %local_sums.1._.refs_1_, s32[197,128]{1,0:T(8,128)S(1)} %pad_add_fusion._.refs_0_, f32[165,256]{1,0:T(8,128)S(1)} %local_sums.1._.refs_1_, f32[165,128]{1,0:T(8,128)S(1)} %collective-permute-done.9.refs_2_), custom_call_target="tpu_custom_call" | custom-call | flops 300000000 | tf_op jit(solution)/shard_map/last_sum/pallas_call | solution.py:35
  (16 shorter events, 0.6 us)
Async XLA Ops:
  1.5 0.9 %copy-start = (bf16[165,256]{1,0:T(8,128)(2,1)S(1)}, bf16[165,256]{1,0:T(8,128)(2,1)}, u32[]{:S(2)}) copy-start(bf16[165,256]{1,0:T(8,128)(2,1)} %refs_1_.1) | copy-start | bytes 253444
  2.4 5.4 %slice-start = ((s8[5406720]{0:T(1024)(128)(4,1)}), s8[4194304]{0:T(1024)(128)(4,1)S(1)}, s32[]{:S(2)}) async-start(s8[5406720]{0:T(1024)(128)(4,1)} %bitcast.2), calls=%async_computation | async-start | bytes 8388608
  2.6 5.0 %collective-permute-start = (bf16[165,128]{1,0:T(8,128)(2,1)S(1)}, bf16[165,128]{1,0:T(8,128)(2,1)S(1)}, u32[]{:S(2)}, u32[]{:S(2)}) collective-permute-start(bf16[165,128]{1,0:T(8,128)(2,1)S(1)} %get-tuple-element.15._), channel_id=1, source_target_pairs={{0,16},{16,0},{1,17},{17,1},{2,18},{18,2},{3,19},{19,3},{4,20},{20... | collective-permute-start | bytes 126728 | tf_op jit(solution)/shard_map/ppermute | solution.py:70
  5.6 2.3 %slice-start.1 = ((s8[5406720]{0:T(1024)(128)(4,1)}), s8[1212416]{0:T(1024)(128)(4,1)S(1)}, s32[]{:S(2)}) async-start(s8[5406720]{0:T(1024)(128)(4,1)} %bitcast.2), calls=%async_computation.1 | async-start | bytes 2424832
  7.8 1.4 %collective-permute-start.1 = (bf16[165,128]{1,0:T(8,128)(2,1)S(1)}, bf16[165,128]{1,0:T(8,128)(2,1)S(1)}, u32[]{:S(2)}, u32[]{:S(2)}) collective-permute-start(bf16[165,128]{1,0:T(8,128)(2,1)S(1)} %export.6._), channel_id=1, source_target_pairs={{0,8},{8,0},{1,9},{9,1},{2,10},{10,2},{3,11},{11,3},{4,12},{12,4},... | collective-permute-start | bytes 126728 | tf_op jit(solution)/shard_map/ppermute | solution.py:70
  9.4 7.8 %collective-permute-start.2 = (bf16[165,128]{1,0:T(8,128)(2,1)S(1)}, bf16[165,128]{1,0:T(8,128)(2,1)S(1)}, u32[]{:S(2)}, u32[]{:S(2)}) collective-permute-start(bf16[165,128]{1,0:T(8,128)(2,1)S(1)} %export.7._), channel_id=1, source_target_pairs={{0,4},{4,0},{1,5},{5,1},{2,6},{6,2},{3,7},{7,3},{8,12},{12,8},{9,1... | collective-permute-start | bytes 126728 | tf_op jit(solution)/shard_map/ppermute | solution.py:70
  17.5 4.3 %collective-permute-start.3 = (bf16[165,128]{1,0:T(8,128)(2,1)S(1)}, bf16[165,128]{1,0:T(8,128)(2,1)S(1)}, u32[]{:S(2)}, u32[]{:S(2)}) collective-permute-start(bf16[165,128]{1,0:T(8,128)(2,1)S(1)} %export.8._), channel_id=1, source_target_pairs={{0,2},{2,0},{1,3},{3,1},{4,6},{6,4},{5,7},{7,5},{8,10},{10,8},{9,1... | collective-permute-start | bytes 126728 | tf_op jit(solution)/shard_map/ppermute | solution.py:70
  20.5 5.0 %collective-permute-start.4 = (f32[165,128]{1,0:T(8,128)S(1)}, f32[165,128]{1,0:T(8,128)S(1)}, u32[]{:S(2)}, u32[]{:S(2)}) collective-permute-start(f32[165,128]{1,0:T(8,128)S(1)} %get-tuple-element.20._), channel_id=1, source_target_pairs={{0,1},{1,0},{2,3},{3,2},{4,5},{5,4},{6,7},{7,6},{8,9},{9,8},{10,11... | collective-permute-start | bytes 253448 | tf_op jit(solution)/shard_map/ppermute | solution.py:70
  22.0 4.3 %collective-permute-start.5 = (bf16[165,128]{1,0:T(8,128)(2,1)S(1)}, bf16[165,128]{1,0:T(8,128)(2,1)S(1)}, u32[]{:S(2)}, u32[]{:S(2)}) collective-permute-start(bf16[165,128]{1,0:T(8,128)(2,1)S(1)} %export.9._), channel_id=1, source_target_pairs={{0,1},{1,0},{2,3},{3,2},{4,5},{5,4},{6,7},{7,6},{8,9},{9,8},{10,11... | collective-permute-start | bytes 126728 | tf_op jit(solution)/shard_map/ppermute | solution.py:70
  25.7 4.6 %collective-permute-start.6 = (f32[165,128]{1,0:T(8,128)S(1)}, f32[165,128]{1,0:T(8,128)S(1)}, u32[]{:S(2)}, u32[]{:S(2)}) collective-permute-start(f32[165,128]{1,0:T(8,128)S(1)} %return.4._), channel_id=1, source_target_pairs={{0,2},{2,0},{1,3},{3,1},{4,6},{6,4},{5,7},{7,5},{8,10},{10,8},{9,1... | collective-permute-start | bytes 253448 | tf_op jit(solution)/shard_map/ppermute | solution.py:70
  30.5 6.4 %collective-permute-start.7 = (f32[165,128]{1,0:T(8,128)S(1)}, f32[165,128]{1,0:T(8,128)S(1)}, u32[]{:S(2)}, u32[]{:S(2)}) collective-permute-start(f32[165,128]{1,0:T(8,128)S(1)} %return.5._), channel_id=1, source_target_pairs={{0,4},{4,0},{1,5},{5,1},{2,6},{6,2},{3,7},{7,3},{8,12},{12,8},{9,1... | collective-permute-start | bytes 253448 | tf_op jit(solution)/shard_map/ppermute | solution.py:70
  37.2 1.4 %collective-permute-start.8 = (f32[165,128]{1,0:T(8,128)S(1)}, f32[165,128]{1,0:T(8,128)S(1)}, u32[]{:S(2)}, u32[]{:S(2)}) collective-permute-start(f32[165,128]{1,0:T(8,128)S(1)} %return.6._), channel_id=1, source_target_pairs={{0,8},{8,0},{1,9},{9,1},{2,10},{10,2},{3,11},{11,3},{4,12},{12,4},... | collective-permute-start | bytes 253448 | tf_op jit(solution)/shard_map/ppermute | solution.py:70
  38.9 5.0 %collective-permute-start.9 = (f32[165,128]{1,0:T(8,128)S(1)}, f32[165,128]{1,0:T(8,128)S(1)}, u32[]{:S(2)}, u32[]{:S(2)}) collective-permute-start(f32[165,128]{1,0:T(8,128)S(1)} %return.7._), channel_id=1, source_target_pairs={{0,16},{16,0},{1,17},{17,1},{2,18},{18,2},{3,19},{19,3},{4,20},{20... | collective-permute-start | bytes 253448 | tf_op jit(solution)/shard_map/ppermute | solution.py:70

commit v4 on v3

--- a/solution.py
+++ b/solution.py
@@ -10,6 +10,7 @@
 LANES = 128
 CHUNK = 512
 PICK_PART = 8
+UNROLL = 16
 SCATTER_PART = 8
 TILE = 16
 AXES = ("gx", "gy")
@@ -30,7 +31,7 @@
     return jax.ShapeDtypeStruct((rows, columns), kind)
 
 
-def call(kernel, out_shape, args, after, limit=4, scratch=(), us=0.3):
+def call(kernel, out_shape, args, after, limit=4, scratch=(), us=0.3, **more):
     single = not isinstance(out_shape, (tuple, list))
     return pl.pallas_call(
         lambda _, *refs: kernel(*refs),
@@ -40,6 +41,7 @@
         scratch_shapes=list(scratch),
         compiler_params=params(limit),
         cost_estimate=takes(us),
+        **more,
     )(after, *args)
 
 
@@ -162,10 +164,12 @@
     pick_columns(info_ref[info_ref.shape[0] - 1, 0], index_ref, pool, picked)
 
 
-def apply_kernel(flip, info_ref, op_ref, picked, out_ref):
+def apply_kernel(flip, first_class, last_class, info_ref, op_ref, picked, *refs):
+    out_ref = refs[-1]
     classes, rows, depth = op_ref.shape
-    last = pl.multiple_of(info_ref[classes, 0] // CHUNK * CHUNK, CHUNK)
-    out_ref[:, pl.ds(last, 2 * CHUNK)] = jnp.zeros((2 * rows, 2 * CHUNK), BF16)
+    if first_class == 0:
+        last = pl.multiple_of(info_ref[classes, 0] // CHUNK * CHUNK, CHUNK)
+        out_ref[:, pl.ds(last, 2 * CHUNK)] = jnp.zeros((2 * rows, 2 * CHUNK), BF16)
     lane = lax.broadcasted_iota(jnp.int32, (rows, LANES), 1)
 
     def apply(c, _):
@@ -181,7 +185,7 @@
             out_ref[first : first + rows, pl.ds(start + LANES, LANES)] = part[:, LANES:]
         return 0
 
-    lax.fori_loop(0, classes, apply, 0, unroll=16)
+    lax.fori_loop(first_class, last_class, apply, 0, unroll=UNROLL)
 
 
 def add_terms(first, info_ref, index_ref, terms_ref, sums):
@@ -264,20 +268,21 @@
             after,
             limit=16,
             scratch=[pltpu.VMEM((rows, height), BF16)],
-            us=2.0,
-        )
-
-    def apply(columns, flip, after):
+            us=4.0,
+        )
+
+    def apply(columns, flip, after, first, last, terms=()):
         return call(
-            lambda *refs: apply_kernel(flip, *refs),
+            lambda *refs: apply_kernel(flip, first, last, *refs),
             shape(2 * rows, packed, BF16),
-            [info, ordered, columns],
+            [info, ordered, columns, *terms],
             after,
             limit=8,
-            us=5.0,
-        )
-
-    def scatter(values, index, first, last, after):
+            us=0.1,
+            input_output_aliases={4: 0} if terms else {},
+        )
+
+    def scatter(values, index, first, last, after, us):
         height = sum(sizes[first:last])
         return call(
             lambda *refs: scatter_kernel(starts[first:last], *refs),
@@ -286,7 +291,7 @@
             after,
             limit=8,
             scratch=[pltpu.VMEM((2 * rows, height), F32)],
-            us=1.0,
+            us=us,
         )
 
     segments, returned, sums = [multipoles], [], [None] * (cuts + 1)
@@ -324,13 +329,13 @@
         returned.insert(0, from_partner(outgoing, cuts - 1 - cut))
         return outgoing
 
-    def more_sums(after):
+    def more_sums(after, us):
         last = max((cut for cut in range(1, cuts + 1) if sums[cut] is None), default=0)
         if last == 0:
             return after
         first = max(last - 1, 1)
         with jax.named_scope("reverse_sums"):
-            sums[first : last + 1] = scatter(back, sources, first, last + 1, after)
+            sums[first : last + 1] = scatter(back, sources, first, last + 1, after, us)
         return sums[first]
 
     step = export(meta)
@@ -349,35 +354,46 @@
             compiler_params=params(8),
             cost_estimate=takes(2.5),
         )(step, meta, segments[0])
-    step = export(info)
     with jax.named_scope("order_operators"):
         ordered = call(
             order_kernel,
             jax.ShapeDtypeStruct((classes, rows, coefficients), BF16),
             [operators.transpose(1, 0, 2)],
-            step,
+            info,
             limit=8,
             us=1.3,
         )
+    early = min(16, classes // 2)
     step = export(ordered)
     with jax.named_scope("reverse_terms"):
-        back = apply(picked, True, step)
-    step = export(back)
-    step = more_sums(step)
+        back = apply(picked, True, step, 0, early)
+    step = export(back) if len(segments) <= cuts else back
+    with jax.named_scope("reverse_terms"):
+        back = apply(picked, True, step, early, classes, [back])
+    step = more_sums(back, 0.1)
+    step = give_back(step)
+    step = export(step) if len(segments) <= cuts else step
+    step = more_sums(step, 4.0)
     step = give_back(step)
     while len(segments) <= cuts:
         step = export(step)
-    step = more_sums(step)
+    while any(part is None for part in sums[1:]):
+        step = more_sums(step, 4.0)
     step = give_back(step)
     with jax.named_scope("forward_columns"):
-        ahead = pick(segments, sources, step)
-    step = give_back(ahead)
-    with jax.named_scope("forward_terms"):
-        ahead = apply(ahead, False, step)
+        columns = pick(segments, sources, step)
+    ends = [classes * part // 4 for part in range(5)]
+    ahead, step = [], columns
+    for part in range(4):
+        after = columns
+        if part >= 2 and len(returned) < cuts:
+            after = give_back(ahead[0])
+        with jax.named_scope("forward_terms"):
+            ahead = [apply(columns, False, after, ends[part], ends[part + 1], ahead)]
+    (ahead,) = ahead
     step = ahead
     while len(returned) < cuts:
         step = give_back(step)
-        step = more_sums(step)
     with jax.named_scope("local_sums"):
         local = call(
             lambda *refs: local_kernel(3 * classes + 1, *refs),
@@ -386,7 +402,7 @@
             step,
             limit=8,
             scratch=[pltpu.VMEM((2 * rows, cells), F32)],
-            us=2.0,
+            us=0.1,
         )
     with jax.named_scope("last_sum"):
         return call(

time: 44.9 us -> 42.1 us (0.938); the launches traced: 44.8 us -> 42.5 us
  waiting for transfers between devices: 3.26 us -> 1.88 us
  starting transfers between devices: 13.9 us -> 12.9 us
    ppermute x10, waiting for transfers between devices: 3.26 us -> 1.88 us  [from_partner(): return lax.ppermute(block, AXES, route)]
    ppermute x10, starting transfers between devices: 13.9 us -> 12.9 us  [from_partner(): return lax.ppermute(block, AXES, route)]
    pallas_call x18 -> x22, Pallas kernels: 23 us -> 22.8 us  [call(): pl.pallas_call(lambda _, *refs: kernel(*refs), out_shape=out_shape, in_sp...]
  transfers between devices with their start and end apart: 10 -> 10, of which waited for: 4 -> 4; matrix products, arithmetic and copies ran while one was open for 0% -> 0% of each run, Pallas kernels for 50% -> 53%
where the time goes in v4:
time: 42.1 us; the launch traced here: 42.5 us
  Pallas kernels  24.8 us (59%)
  starting transfers between devices  12.9 us (31%)
  waiting for transfers between devices  1.88 us (4%)
  local copies, waits for them, and re-layouts  1.7 us (4%)
  other arithmetic  1.05 us (2%)
    pallas_call x22, Pallas kernels, call(): pl.pallas_call(lambda _, *refs: kernel(*refs), out_shape=out_shape, in_sp...  22.8 us
    ppermute x10, starting transfers between devices, from_partner(): return lax.ppermute(block, AXES, route)  12.9 us
    pallas_call x1, Pallas kernels, per_device(): pl.pallas_call(lambda _, *refs: pack_kernel(classes, *refs), out_shape=[i...  1.97 us
    ppermute x10, waiting for transfers between devices, from_partner(): return lax.ppermute(block, AXES, route)  1.88 us
    concatenate x1, other arithmetic, per_device(): jnp.concatenate([pair_target, pair_source, jnp.broadcast_to(pair_count, p...  1.05 us
    unnamed x6, local copies, waits for them, and re-layouts  0.89 us
  transfers between devices with their start and end apart: 10, of which 4 were waited for; matrix products, arithmetic and copies ran while one was open for 0% of the time, Pallas kernels for 53%

profile of v4, /device:TPU:0, one launch (start us, length us, event | category | flops | bytes accessed | tf_op | source)
XLA Modules:
  0.0 42.5 jit_solution(6367648084732370545)
XLA Ops:
  0.0 0.8 %pad.2.clone = s32[197]{0:T(256)S(1)} pad(s32[64]{0:T(128)} %bitcast.5, s32[]{:T(128)} %constant.1), padding=128_5 | pad | bytes 1048 | tf_op jit(solution)/shard_map/concatenate | solution.py:298
  0.8 1.0 %pad_add_fusion._.refs_0_ = s32[197,128]{1,0:T(8,128)S(1)} fusion(s32[5,128]{1,0:T(8,128)} %param.8, s32[64,128]{1,0:T(8,128)} %param.10, s32[64,128]{1,0:T(8,128)} %param.9, s32[197]{0:T(256)S(1)} %pad.2.clone), kind=kLoop, calls=%fused_computation | loop fusion | flops 75648 | bytes 169748 | tf_op jit(solution)/shard_map/concatenate | solution.py:298
  1.9 0.9 %copy-done = bf16[165,256]{1,0:T(8,128)(2,1)S(1)} copy-done((bf16[165,256]{1,0:T(8,128)(2,1)S(1)}, bf16[165,256]{1,0:T(8,128)(2,1)}, u32[]{:S(2)}) %copy-start) | copy-done | bytes 84504
  2.9 3.0 %collective-permute-start = (bf16[165,128]{1,0:T(8,128)(2,1)S(1)}, bf16[165,128]{1,0:T(8,128)(2,1)S(1)}, u32[]{:S(2)}, u32[]{:S(2)}) collective-permute-start(bf16[165,128]{1,0:T(8,128)(2,1)S(1)} %get-tuple-element.15._), channel_id=1, source_target_pairs={{0,16},{16,0},{1,17},{17,1},{2,18},{18,2},{3,19},{19,3},{4,20},{20... | collective-permute-start | bytes 126728 | tf_op jit(solution)/shard_map/ppermute | solution.py:72
  5.9 2.0 %pack_slots.1 = (s32[73,128]{1,0:T(8,128)S(1)}, s32[73,128]{1,0:T(8,128)S(1)}, s32[72,128]{1,0:T(8,128)S(1)}, bf16[176,9344]{1,0:T(8,128)(2,1)S(1)}) custom-call(bf16[165,128]{1,0:T(8,128)(2,1)S(1)} %get-tuple-element.15._, s32[197,128]{1,0:T(8,128)S(1)} %pad_add_fusion._.refs_0_, bf16[165,256]{1,0:T(8,128)(2,1)S(1)} %get-tuple-element.16.refs_1_.refs_2_), custom_call_target="tpu_custom_call" | custom-call | flops 2500000000 | tf_op jit(solution)/shard_map/pack_slots/pallas_call | solution.py:343
  7.9 1.3 %order_operators.1._.refs_1_ = bf16[64,176,165]{2,1,0:T(8,128)(2,1)S(1)} custom-call(s32[72,128]{1,0:T(8,128)S(1)} %get-tuple-element.17._.refs_0_.refs_1_, bf16[165,64,165]{2,1,0:T(8,128)(2,1)S(1)} %bitcast.4), custom_call_target="tpu_custom_call" | custom-call | flops 1300000000 | tf_op jit(solution)/shard_map/order_operators/pallas_call | solution.py:36
  9.5 1.1 %reverse_terms.2._.refs_3_ = bf16[352,9344]{1,0:T(8,128)(2,1)S(1)} custom-call(bf16[165,128]{1,0:T(8,128)(2,1)S(1)} %export.6._, s32[72,128]{1,0:T(8,128)S(1)} %get-tuple-element.17._.refs_0_.refs_1_, bf16[64,176,165]{2,1,0:T(8,128)(2,1)S(1)} %order_operators.1._.refs_1_, bf16[176,9344]{1,0:T(8,128)(2,1)S(1)} %get-tuple-element.18.refs_2_), custom_call_target="tpu_custom_call" | custom-call | flops 100000000 | tf_op jit(solution)/shard_map/reverse_terms/pallas_call | solution.py:36
  10.7 0.2 export.7._
  10.9 2.5 %collective-permute-start.2 = (bf16[165,128]{1,0:T(8,128)(2,1)S(1)}, bf16[165,128]{1,0:T(8,128)(2,1)S(1)}, u32[]{:S(2)}, u32[]{:S(2)}) collective-permute-start(bf16[165,128]{1,0:T(8,128)(2,1)S(1)} %export.7._), channel_id=1, source_target_pairs={{0,4},{4,0},{1,5},{5,1},{2,6},{6,2},{3,7},{7,3},{8,12},{12,8},{9,1... | collective-permute-start | bytes 126728 | tf_op jit(solution)/shard_map/ppermute | solution.py:72
  13.4 3.4 %reverse_terms.3._.refs_2_.refs_5_ = bf16[352,9344]{1,0:T(8,128)(2,1)S(1)} custom-call(bf16[165,128]{1,0:T(8,128)(2,1)S(1)} %export.7._, s32[72,128]{1,0:T(8,128)S(1)} %get-tuple-element.17._.refs_0_.refs_1_, bf16[64,176,165]{2,1,0:T(8,128)(2,1)S(1)} %order_operators.1._.refs_1_, ...), custom_call_target="tpu_custom_call", output_to_operand_aliasing={{}: (4, {})} | custom-call | flops 100000000 | tf_op jit(solution)/shard_map/reverse_terms/pallas_call | solution.py:36
  16.8 1.4 %reverse_sums.3 = (f32[165,128]{1,0:T(8,128)S(1)}, f32[165,128]{1,0:T(8,128)S(1)}) custom-call(bf16[352,9344]{1,0:T(8,128)(2,1)S(1)} %reverse_terms.3._.refs_2_.refs_5_, s32[72,128]{1,0:T(8,128)S(1)} %get-tuple-element.17._.refs_0_.refs_1_, s32[73,128]{1,0:T(8,128)S(1)} %get-tuple-element.19.refs_1_.refs_4_, bf16[352,9344]{1,0:T(8,128)(2,1)S(1)} %reverse_terms.3._.refs_2_.refs_5_), custom_call_target="tpu_custom_call" | custom-call | flops 100000000 | tf_op jit(solution)/shard_map/reverse_sums/pallas_call | solution.py:36
  18.1 1.5 %collective-permute-start.3 = (f32[165,128]{1,0:T(8,128)S(1)}, f32[165,128]{1,0:T(8,128)S(1)}, u32[]{:S(2)}, u32[]{:S(2)}) collective-permute-start(f32[165,128]{1,0:T(8,128)S(1)} %get-tuple-element.20._), channel_id=1, source_target_pairs={{0,1},{1,0},{2,3},{3,2},{4,5},{5,4},{6,7},{7,6},{8,9},{9,8},{10,11... | collective-permute-start | bytes 253448 | tf_op jit(solution)/shard_map/ppermute | solution.py:72
  19.6 0.2 export.8._
  19.9 2.0 %collective-permute-start.4 = (bf16[165,128]{1,0:T(8,128)(2,1)S(1)}, bf16[165,128]{1,0:T(8,128)(2,1)S(1)}, u32[]{:S(2)}, u32[]{:S(2)}) collective-permute-start(bf16[165,128]{1,0:T(8,128)(2,1)S(1)} %export.8._), channel_id=1, source_target_pairs={{0,2},{2,0},{1,3},{3,1},{4,6},{6,4},{5,7},{7,5},{8,10},{10,8},{9,1... | collective-permute-start | bytes 126728 | tf_op jit(solution)/shard_map/ppermute | solution.py:72
  21.8 1.4 %reverse_sums.4 = (f32[165,128]{1,0:T(8,128)S(1)}, f32[165,128]{1,0:T(8,128)S(1)}) custom-call(bf16[165,128]{1,0:T(8,128)(2,1)S(1)} %export.8._, s32[72,128]{1,0:T(8,128)S(1)} %get-tuple-element.17._.refs_0_.refs_1_, s32[73,128]{1,0:T(8,128)S(1)} %get-tuple-element.19.refs_1_.refs_4_, bf16[352,9344]{1,0:T(8,128)(2,1)S(1)} %reverse_terms.3._.refs_2_.refs_5_), custom_call_target="tpu_custom_call" | custom-call | flops 4000000000 | tf_op jit(solution)/shard_map/reverse_sums/pallas_call | solution.py:36
  23.4 1.2 %collective-permute-start.5 = (f32[165,128]{1,0:T(8,128)S(1)}, f32[165,128]{1,0:T(8,128)S(1)}, u32[]{:S(2)}, u32[]{:S(2)}) collective-permute-start(f32[165,128]{1,0:T(8,128)S(1)} %return.4._), channel_id=1, source_target_pairs={{0,2},{2,0},{1,3},{3,1},{4,6},{6,4},{5,7},{7,5},{8,10},{10,8},{9,1... | collective-permute-start | bytes 253448 | tf_op jit(solution)/shard_map/ppermute | solution.py:72
  24.7 0.3 export.9._
  25.0 1.8 %collective-permute-start.6 = (bf16[165,128]{1,0:T(8,128)(2,1)S(1)}, bf16[165,128]{1,0:T(8,128)(2,1)S(1)}, u32[]{:S(2)}, u32[]{:S(2)}) collective-permute-start(bf16[165,128]{1,0:T(8,128)(2,1)S(1)} %export.9._), channel_id=1, source_target_pairs={{0,1},{1,0},{2,3},{3,2},{4,5},{5,4},{6,7},{7,6},{8,9},{9,8},{10,11... | collective-permute-start | bytes 126728 | tf_op jit(solution)/shard_map/ppermute | solution.py:72
  26.7 1.3 %reverse_sums.5._.refs_1_ = f32[165,128]{1,0:T(8,128)S(1)} custom-call(bf16[165,128]{1,0:T(8,128)(2,1)S(1)} %export.9._, s32[72,128]{1,0:T(8,128)S(1)} %get-tuple-element.17._.refs_0_.refs_1_, s32[73,128]{1,0:T(8,128)S(1)} %get-tuple-element.19.refs_1_.refs_4_, bf16[352,9344]{1,0:T(8,128)(2,1)S(1)} %reverse_terms.3._.refs_2_.refs_5_), custom_call_target="tpu_custom_call" | custom-call | flops 4000000000 | tf_op jit(solution)/shard_map/reverse_sums/pallas_call | solution.py:36
  28.0 0.3 return.5._
  28.4 0.7 %collective-permute-done.6.refs_7_ = bf16[165,128]{1,0:T(8,128)(2,1)S(1)} collective-permute-done((bf16[165,128]{1,0:T(8,128)(2,1)S(1)}, bf16[165,128]{1,0:T(8,128)(2,1)S(1)}, u32[]{:S(2)}, u32[]{:S(2)}) %collective-permute-start.6) | collective-permute-done | bytes 42272 | tf_op jit(solution)/shard_map/ppermute | solution.py:72
  29.0 2.3 %forward_columns.1._.refs_2_ = bf16[176,9344]{1,0:T(8,128)(2,1)S(1)} custom-call(f32[165,128]{1,0:T(8,128)S(1)} %return.5._, s32[72,128]{1,0:T(8,128)S(1)} %get-tuple-element.17._.refs_0_.refs_1_, s32[73,128]{1,0:T(8,128)S(1)} %get-tuple-element.19.refs_1_.refs_4_, bf16[165,256]{1,0:T(8,128)(2,1)S(1)} %get-tuple-element.16.refs_1_.refs_2_, ...), custom_call_target="tpu_custom_call" | custom-call | flops 4000000000 | tf_op jit(solution)/shard_map/forward_columns/pallas_call | solution.py:36
  31.4 1.1 %forward_terms.4.refs_3_ = bf16[352,9344]{1,0:T(8,128)(2,1)S(1)} custom-call(bf16[176,9344]{1,0:T(8,128)(2,1)S(1)} %forward_columns.1._.refs_2_, s32[72,128]{1,0:T(8,128)S(1)} %get-tuple-element.17._.refs_0_.refs_1_, bf16[64,176,165]{2,1,0:T(8,128)(2,1)S(1)} %order_operators.1._.refs_1_, bf16[176,9344]{1,0:T(8,128)(2,1)S(1)} %forward_columns.1._.refs_2_), custom_call_target="tpu_custom_call" | custom-call | flops 100000000 | tf_op jit(solution)/shard_map/forward_terms/pallas_call | solution.py:36
  32.5 1.1 %forward_terms.5._.refs_3_ = bf16[352,9344]{1,0:T(8,128)(2,1)S(1)} custom-call(bf16[176,9344]{1,0:T(8,128)(2,1)S(1)} %forward_columns.1._.refs_2_, s32[72,128]{1,0:T(8,128)S(1)} %get-tuple-element.17._.refs_0_.refs_1_, bf16[64,176,165]{2,1,0:T(8,128)(2,1)S(1)} %order_operators.1._.refs_1_, ...), custom_call_target="tpu_custom_call", output_to_operand_aliasing={{}: (4, {})} | custom-call | flops 100000000 | tf_op jit(solution)/shard_map/forward_terms/pallas_call | solution.py:36
  33.7 1.0 %collective-permute-done.7.refs_2_.refs_3_.refs_7_ = f32[165,128]{1,0:T(8,128)S(1)} collective-permute-done((f32[165,128]{1,0:T(8,128)S(1)}, f32[165,128]{1,0:T(8,128)S(1)}, u32[]{:S(2)}, u32[]{:S(2)}) %collective-permute-start.7) | collective-permute-done | bytes 84512 | tf_op jit(solution)/shard_map/ppermute | solution.py:72
  34.7 0.3 return.6._
  35.0 1.1 %forward_terms.6._.refs_3_ = bf16[352,9344]{1,0:T(8,128)(2,1)S(1)} custom-call(f32[165,128]{1,0:T(8,128)S(1)} %return.6._, s32[72,128]{1,0:T(8,128)S(1)} %get-tuple-element.17._.refs_0_.refs_1_, bf16[64,176,165]{2,1,0:T(8,128)(2,1)S(1)} %order_operators.1._.refs_1_, bf16[176,9344]{1,0:T(8,128)(2,1)S(1)} %forward_columns.1._.refs_2_, ...), custom_call_target="tpu_custom_call", output_to_operand_aliasing={{}: (4, {})} | custom-call | flops 100000000 | tf_op jit(solution)/shard_map/forward_terms/pallas_call | solution.py:36
  36.3 0.4 return.7._
  36.7 0.8 %collective-permute-start.9 = (f32[165,128]{1,0:T(8,128)S(1)}, f32[165,128]{1,0:T(8,128)S(1)}, u32[]{:S(2)}, u32[]{:S(2)}) collective-permute-start(f32[165,128]{1,0:T(8,128)S(1)} %return.7._), channel_id=1, source_target_pairs={{0,16},{16,0},{1,17},{17,1},{2,18},{18,2},{3,19},{19,3},{4,20},{20... | collective-permute-start | bytes 253448 | tf_op jit(solution)/shard_map/ppermute | solution.py:72
  37.4 1.1 %forward_terms.7._.refs_3_ = bf16[352,9344]{1,0:T(8,128)(2,1)S(1)} custom-call(f32[165,128]{1,0:T(8,128)S(1)} %return.7._, s32[72,128]{1,0:T(8,128)S(1)} %get-tuple-element.17._.refs_0_.refs_1_, bf16[64,176,165]{2,1,0:T(8,128)(2,1)S(1)} %order_operators.1._.refs_1_, bf16[176,9344]{1,0:T(8,128)(2,1)S(1)} %forward_columns.1._.refs_2_, ...), custom_call_target="tpu_custom_call", output_to_operand_aliasing={{}: (4, {})} | custom-call | flops 100000000 | tf_op jit(solution)/shard_map/forward_terms/pallas_call | solution.py:36
  38.6 3.1 %local_sums.1._.refs_1_ = f32[165,256]{1,0:T(8,128)S(1)} custom-call(bf16[352,9344]{1,0:T(8,128)(2,1)S(1)} %forward_terms.7._.refs_3_, s32[197,128]{1,0:T(8,128)S(1)} %pad_add_fusion._.refs_0_, s32[72,128]{1,0:T(8,128)S(1)} %get-tuple-element.17._.refs_0_.refs_1_, s32[73,128]{1,0:T(8,128)S(1)} %get-tuple-element.24.refs_2_, ...), custom_call_target="tpu_custom_call" | custom-call | flops 100000000 | tf_op jit(solution)/shard_map/local_sums/pallas_call | solution.py:36
  41.6 0.9 %last_sum.1 = f32[165,256]{1,0:T(8,128)} custom-call(f32[165,256]{1,0:T(8,128)S(1)} %local_sums.1._.refs_1_, s32[197,128]{1,0:T(8,128)S(1)} %pad_add_fusion._.refs_0_, f32[165,256]{1,0:T(8,128)S(1)} %local_sums.1._.refs_1_, f32[165,128]{1,0:T(8,128)S(1)} %collective-permute-done.9.refs_2_), custom_call_target="tpu_custom_call" | custom-call | flops 300000000 | tf_op jit(solution)/shard_map/last_sum/pallas_call | solution.py:36
  (20 shorter events, 1.0 us)
Async XLA Ops:
  0.0 7.9 %slice-start = ((s8[5406720]{0:T(1024)(128)(4,1)}), s8[4194304]{0:T(1024)(128)(4,1)S(1)}, s32[]{:S(2)}) async-start(s8[5406720]{0:T(1024)(128)(4,1)} %bitcast.2), calls=%async_computation | async-start | bytes 8388608
  1.9 0.9 %copy-start = (bf16[165,256]{1,0:T(8,128)(2,1)S(1)}, bf16[165,256]{1,0:T(8,128)(2,1)}, u32[]{:S(2)}) copy-start(bf16[165,256]{1,0:T(8,128)(2,1)} %refs_1_.1) | copy-start | bytes 253444
  2.9 6.3 %collective-permute-start = (bf16[165,128]{1,0:T(8,128)(2,1)S(1)}, bf16[165,128]{1,0:T(8,128)(2,1)S(1)}, u32[]{:S(2)}, u32[]{:S(2)}) collective-permute-start(bf16[165,128]{1,0:T(8,128)(2,1)S(1)} %get-tuple-element.15._), channel_id=1, source_target_pairs={{0,16},{16,0},{1,17},{17,1},{2,18},{18,2},{3,19},{19,3},{4,20},{20... | collective-permute-start | bytes 126728 | tf_op jit(solution)/shard_map/ppermute | solution.py:72
  5.9 2.0 %slice-start.1 = ((s8[5406720]{0:T(1024)(128)(4,1)}), s8[1212416]{0:T(1024)(128)(4,1)S(1)}, s32[]{:S(2)}) async-start(s8[5406720]{0:T(1024)(128)(4,1)} %bitcast.2), calls=%async_computation.1 | async-start | bytes 2424832
  9.4 1.3 %collective-permute-start.1 = (bf16[165,128]{1,0:T(8,128)(2,1)S(1)}, bf16[165,128]{1,0:T(8,128)(2,1)S(1)}, u32[]{:S(2)}, u32[]{:S(2)}) collective-permute-start(bf16[165,128]{1,0:T(8,128)(2,1)S(1)} %export.6._), channel_id=1, source_target_pairs={{0,8},{8,0},{1,9},{9,1},{2,10},{10,2},{3,11},{11,3},{4,12},{12,4},... | collective-permute-start | bytes 126728 | tf_op jit(solution)/shard_map/ppermute | solution.py:72
  10.9 8.7 %collective-permute-start.2 = (bf16[165,128]{1,0:T(8,128)(2,1)S(1)}, bf16[165,128]{1,0:T(8,128)(2,1)S(1)}, u32[]{:S(2)}, u32[]{:S(2)}) collective-permute-start(bf16[165,128]{1,0:T(8,128)(2,1)S(1)} %export.7._), channel_id=1, source_target_pairs={{0,4},{4,0},{1,5},{5,1},{2,6},{6,2},{3,7},{7,3},{8,12},{12,8},{9,1... | collective-permute-start | bytes 126728 | tf_op jit(solution)/shard_map/ppermute | solution.py:72
  18.1 5.1 %collective-permute-start.3 = (f32[165,128]{1,0:T(8,128)S(1)}, f32[165,128]{1,0:T(8,128)S(1)}, u32[]{:S(2)}, u32[]{:S(2)}) collective-permute-start(f32[165,128]{1,0:T(8,128)S(1)} %get-tuple-element.20._), channel_id=1, source_target_pairs={{0,1},{1,0},{2,3},{3,2},{4,5},{5,4},{6,7},{7,6},{8,9},{9,8},{10,11... | collective-permute-start | bytes 253448 | tf_op jit(solution)/shard_map/ppermute | solution.py:72
  19.9 4.8 %collective-permute-start.4 = (bf16[165,128]{1,0:T(8,128)(2,1)S(1)}, bf16[165,128]{1,0:T(8,128)(2,1)S(1)}, u32[]{:S(2)}, u32[]{:S(2)}) collective-permute-start(bf16[165,128]{1,0:T(8,128)(2,1)S(1)} %export.8._), channel_id=1, source_target_pairs={{0,2},{2,0},{1,3},{3,1},{4,6},{6,4},{5,7},{7,5},{8,10},{10,8},{9,1... | collective-permute-start | bytes 126728 | tf_op jit(solution)/shard_map/ppermute | solution.py:72
  23.4 4.6 %collective-permute-start.5 = (f32[165,128]{1,0:T(8,128)S(1)}, f32[165,128]{1,0:T(8,128)S(1)}, u32[]{:S(2)}, u32[]{:S(2)}) collective-permute-start(f32[165,128]{1,0:T(8,128)S(1)} %return.4._), channel_id=1, source_target_pairs={{0,2},{2,0},{1,3},{3,1},{4,6},{6,4},{5,7},{7,5},{8,10},{10,8},{9,1... | collective-permute-start | bytes 253448 | tf_op jit(solution)/shard_map/ppermute | solution.py:72
  25.0 4.1 %collective-permute-start.6 = (bf16[165,128]{1,0:T(8,128)(2,1)S(1)}, bf16[165,128]{1,0:T(8,128)(2,1)S(1)}, u32[]{:S(2)}, u32[]{:S(2)}) collective-permute-start(bf16[165,128]{1,0:T(8,128)(2,1)S(1)} %export.9._), channel_id=1, source_target_pairs={{0,1},{1,0},{2,3},{3,2},{4,5},{5,4},{6,7},{7,6},{8,9},{9,8},{10,11... | collective-permute-start | bytes 126728 | tf_op jit(solution)/shard_map/ppermute | solution.py:72
  28.3 6.4 %collective-permute-start.7 = (f32[165,128]{1,0:T(8,128)S(1)}, f32[165,128]{1,0:T(8,128)S(1)}, u32[]{:S(2)}, u32[]{:S(2)}) collective-permute-start(f32[165,128]{1,0:T(8,128)S(1)} %return.5._), channel_id=1, source_target_pairs={{0,4},{4,0},{1,5},{5,1},{2,6},{6,2},{3,7},{7,3},{8,12},{12,8},{9,1... | collective-permute-start | bytes 253448 | tf_op jit(solution)/shard_map/ppermute | solution.py:72
  35.0 1.3 %collective-permute-start.8 = (f32[165,128]{1,0:T(8,128)S(1)}, f32[165,128]{1,0:T(8,128)S(1)}, u32[]{:S(2)}, u32[]{:S(2)}) collective-permute-start(f32[165,128]{1,0:T(8,128)S(1)} %return.6._), channel_id=1, source_target_pairs={{0,8},{8,0},{1,9},{9,1},{2,10},{10,2},{3,11},{11,3},{4,12},{12,4},... | collective-permute-start | bytes 253448 | tf_op jit(solution)/shard_map/ppermute | solution.py:72
  36.7 5.0 %collective-permute-start.9 = (f32[165,128]{1,0:T(8,128)S(1)}, f32[165,128]{1,0:T(8,128)S(1)}, u32[]{:S(2)}, u32[]{:S(2)}) collective-permute-start(f32[165,128]{1,0:T(8,128)S(1)} %return.7._), channel_id=1, source_target_pairs={{0,16},{16,0},{1,17},{17,1},{2,18},{18,2},{3,19},{19,3},{4,20},{20... | collective-permute-start | bytes 253448 | tf_op jit(solution)/shard_map/ppermute | solution.py:72

commit v5 on v4

--- a/solution.py
+++ b/solution.py
@@ -121,27 +121,36 @@
 
 
 def pack_kernel(
-    classes, meta_ref, mult_ref, packed_target, packed_source, info_ref, picked, pool
+    classes, shifts, meta_ref, mult_ref, packed_target, packed_source, info_ref, picked, pool, counts, codes
 ):
+    to_source, to_count = shifts
+    codes[...] = meta_ref[:, :LANES]
+    slots = jnp.where(codes[...] >= 0, 1, 0)
+    counts[...] = jnp.broadcast_to(jnp.sum(slots, axis=1, keepdims=True), slots.shape)
     lane = lax.broadcasted_iota(jnp.int32, (1, LANES), 1)
 
-    def place(c, offset):
+    def place(c, carry):
+        offset, current = carry
+        following = offset + counts[c, 0]
         info_ref[pl.ds(c, 1), :] = jnp.full((1, LANES), offset, jnp.int32)
         shift = lax.rem(offset, LANES)
         row = offset // LANES
-        keep = lane >= shift
-        for first, out in ((0, packed_target), (classes, packed_source)):
-            turned = pltpu.roll(meta_ref[pl.ds(first + c, 1), :], shift, 1)
-            out[pl.ds(row, 1), :] = jnp.where(keep, turned, out[pl.ds(row, 1), :])
-            out[pl.ds(row + 1, 1), :] = turned
-        return offset + meta_ref[2 * classes + c, 0]
-
-    total = lax.fori_loop(0, classes, place, 0, unroll=8)
+        turned = pltpu.roll(codes[pl.ds(c, 1), :], shift, 1)
+        current = jnp.where(lane >= shift, turned, current)
+        packed_target[pl.ds(row, 1), :] = current
+        packed_target[pl.ds(row + 1, 1), :] = turned
+        return following, jnp.where(following // LANES == row, current, turned)
+
+    none = jnp.zeros((1, LANES), jnp.int32)
+    total, _ = lax.fori_loop(0, classes, place, (0, none), unroll=8)
     info_ref[classes:, :] = jnp.full((8, LANES), total, jnp.int32)
     position = lax.broadcasted_iota(jnp.int32, packed_target.shape, 0) * LANES
     position = position + lax.broadcasted_iota(jnp.int32, packed_target.shape, 1)
-    for out in (packed_target, packed_source):
-        out[...] = jnp.where(position < total, out[...], -1)
+    used = position < total
+    code = packed_target[...]
+    source = (code >> to_source) & ((1 << (to_count - to_source)) - 1)
+    packed_source[...] = jnp.where(used, source, -1)
+    packed_target[...] = jnp.where(used, code & ((1 << to_source) - 1), -1)
 
     pool[...] = jnp.zeros_like(pool)
     pool[: mult_ref.shape[0], :] = mult_ref[...]
@@ -212,7 +221,7 @@
 
 def export_kernel(starts, list_row, meta_ref, *refs):
     segs, out_ref = refs[: len(starts)], refs[len(starts)]
-    row = meta_ref[list_row : list_row + 1, :]
+    row = meta_ref[list_row : list_row + 1, LANES:]
     out = 0.0
     for seg, first in zip(segs, starts):
         out = out + dot(seg[...], one_hot(row, first, seg.shape[1]))
@@ -224,7 +233,7 @@
 def came_back(first, row, meta_ref, returned, width):
     out = 0.0
     for i, ref in enumerate(returned):
-        hot = one_hot(meta_ref[row + i : row + i + 1, :], first, width)
+        hot = one_hot(meta_ref[row + i : row + i + 1, LANES:], first, width)
         high, low = halves(ref[...])
         out = out + dot_nt(high, hot) + dot_nt(low, hot)
     return out
@@ -295,9 +304,16 @@
         )
 
     segments, returned, sums = [multipoles], [], [None] * (cuts + 1)
-    meta = jnp.concatenate(
-        [pair_target, pair_source, jnp.broadcast_to(pair_count, pair_target.shape), boundary], axis=0
-    )
+    to_source = (cells - 1).bit_length()
+    to_count = to_source + (pool_width - 1).bit_length()
+    assert to_count < 32
+    assert width == sent == LANES and classes >= cuts
+    beside = ((0, 0), (0, sent))
+    code = jnp.pad(pair_target, beside) | jnp.pad(pair_source, beside) << to_source
+    lane = lax.broadcasted_iota(jnp.int32, code.shape, 1)
+    code = jnp.where(lane < pair_count, code, -1)
+    lists = jnp.pad(boundary, ((0, classes - cuts), (width, 0)))
+    meta = jnp.where(lane < width, code, lists)
 
     def export(after):
         cut = len(segments) - 1
@@ -306,7 +322,7 @@
             if cut == 0:
                 out.append(shape(coefficients, cells, BF16))
             exported, *own = call(
-                lambda *refs: export_kernel(starts[: cut + 1], 3 * classes + cut, *refs),
+                lambda *refs: export_kernel(starts[: cut + 1], cut, *refs),
                 out,
                 [meta] + segments,
                 after,
@@ -321,7 +337,7 @@
         if returned:
             with jax.named_scope("return"):
                 outgoing = call(
-                    lambda *refs: return_kernel(starts[cut + 1], 3 * classes + cut + 1, *refs),
+                    lambda *refs: return_kernel(starts[cut + 1], cut + 1, *refs),
                     shape(coefficients, sent, F32),
                     [meta, outgoing] + returned,
                     after,
@@ -333,7 +349,7 @@
         last = max((cut for cut in range(1, cuts + 1) if sums[cut] is None), default=0)
         if last == 0:
             return after
-        first = max(last - 1, 1)
+        first = last if last == cuts else max(last - 1, 1)
         with jax.named_scope("reverse_sums"):
             sums[first : last + 1] = scatter(back, sources, first, last + 1, after, us)
         return sums[first]
@@ -341,7 +357,7 @@
     step = export(meta)
     with jax.named_scope("pack_slots"):
         targets, sources, info, picked = pl.pallas_call(
-            lambda _, *refs: pack_kernel(classes, *refs),
+            lambda _, *refs: pack_kernel(classes, (to_source, to_count), *refs),
             out_shape=[
                 index_shape,
                 index_shape,
@@ -350,7 +366,8 @@
             ],
             in_specs=[pl.BlockSpec(memory_space=pl.ANY), VMEM, VMEM],
             out_specs=[VMEM] * 4,
-            scratch_shapes=[pltpu.VMEM((rows, cells), BF16)],
+            scratch_shapes=[pltpu.VMEM((rows, cells), BF16)]
+            + [pltpu.VMEM((classes, LANES), jnp.int32)] * 2,
             compiler_params=params(8),
             cost_estimate=takes(2.5),
         )(step, meta, segments[0])
@@ -396,7 +413,7 @@
         step = give_back(step)
     with jax.named_scope("local_sums"):
         local = call(
-            lambda *refs: local_kernel(3 * classes + 1, *refs),
+            lambda *refs: local_kernel(1, *refs),
             shape(coefficients, cells, F32),
             [meta, info, targets, ahead, sources, back] + returned[1:],
             step,
@@ -406,7 +423,7 @@
         )
     with jax.named_scope("last_sum"):
         return call(
-            lambda *refs: return_kernel(0, 3 * classes, *refs),
+            lambda *refs: return_kernel(0, 0, *refs),
             shape(coefficients, cells, F32),
             [meta, local, returned[0]],
             local,

time: 42.1 us -> 42 us (level); the launches traced: 42.5 us -> 41.9 us
  local copies, waits for them, and re-layouts: 1.7 us -> 1.15 us
    concatenate x1 -> x0, other arithmetic: 1.05 us -> none  [per_device(): jnp.concatenate([pair_target, pair_source, jnp.broadcast_to(pair_count, p...]
    select_n x0 -> x1, other arithmetic: none -> 1.02 us  [per_device(): meta = jnp.where(lane < width, code, lists)]
    concatenate x1 -> x0, local copies, waits for them, and re-layouts: 0.81 us -> none  [per_device(): jnp.concatenate([pair_target, pair_source, jnp.broadcast_to(pair_count, p...]
  transfers between devices with their start and end apart: 10 -> 10, of which waited for: 4 -> 4; matrix products, arithmetic and copies ran while one was open for 0% -> 0% of each run, Pallas kernels for 53% -> 54%
where the time goes in v5:
time: 42 us; the launch traced here: 41.9 us
  Pallas kernels  24.8 us (59%)
  starting transfers between devices  13.1 us (31%)
  waiting for transfers between devices  1.64 us (4%)
  local copies, waits for them, and re-layouts  1.15 us (3%)
  other arithmetic  1.02 us (2%)
    pallas_call x22, Pallas kernels, call(): pl.pallas_call(lambda _, *refs: kernel(*refs), out_shape=out_shape, in_sp...  22.8 us
    ppermute x10, starting transfers between devices, from_partner(): return lax.ppermute(block, AXES, route)  13.1 us
    pallas_call x1, Pallas kernels, per_device(): pl.pallas_call(lambda _, *refs: pack_kernel(classes, (to_source, to_count...  1.98 us
    ppermute x10, waiting for transfers between devices, from_partner(): return lax.ppermute(block, AXES, route)  1.64 us
    unnamed x6, local copies, waits for them, and re-layouts  1.15 us
    select_n x1, other arithmetic, per_device(): meta = jnp.where(lane < width, code, lists)  1.02 us
  transfers between devices with their start and end apart: 10, of which 4 were waited for; matrix products, arithmetic and copies ran while one was open for 0% of the time, Pallas kernels for 54%

profile of v5, /device:TPU:0, one launch (start us, length us, event | category | flops | bytes accessed | tf_op | source)
XLA Modules:
  0.0 41.9 jit_solution(6840559986946054706)
XLA Ops:
  0.0 1.0 %pad_select_fusion._.refs_0_ = s32[64,256]{1,0:T(8,128)S(1)} fusion(s32[5,128]{1,0:T(8,128)} %param.8, s32[64,128]{1,0:T(8,128)} %param.10, s32[64,128]{1,0:T(8,128)} %param.9, s32[64]{0:T(128)} %bitcast.5, pred[256]{0:T(512)(128)(4,1)S(1)} %iota_compare_fusion.1), kind=kLoop, calls=%fused_computation | loop fusion | flops 81920 | bytes 134144 | tf_op jit(solution)/shard_map/jit(_where)/select_n | solution.py:316
  1.0 1.1 %copy-done = bf16[165,256]{1,0:T(8,128)(2,1)S(1)} copy-done((bf16[165,256]{1,0:T(8,128)(2,1)S(1)}, bf16[165,256]{1,0:T(8,128)(2,1)}, u32[]{:S(2)}) %copy-start) | copy-done | bytes 84504
  2.3 3.0 %collective-permute-start = (bf16[165,128]{1,0:T(8,128)(2,1)S(1)}, bf16[165,128]{1,0:T(8,128)(2,1)S(1)}, u32[]{:S(2)}, u32[]{:S(2)}) collective-permute-start(bf16[165,128]{1,0:T(8,128)(2,1)S(1)} %get-tuple-element.15._), channel_id=1, source_target_pairs={{0,16},{16,0},{1,17},{17,1},{2,18},{18,2},{3,19},{19,3},{4,20},{20... | collective-permute-start | bytes 126728 | tf_op jit(solution)/shard_map/ppermute | solution.py:72
  5.4 2.0 %pack_slots.1 = (s32[73,128]{1,0:T(8,128)S(1)}, s32[73,128]{1,0:T(8,128)S(1)}, s32[72,128]{1,0:T(8,128)S(1)}, bf16[176,9344]{1,0:T(8,128)(2,1)S(1)}) custom-call(bf16[165,128]{1,0:T(8,128)(2,1)S(1)} %get-tuple-element.15._, s32[64,256]{1,0:T(8,128)S(1)} %pad_select_fusion._.refs_0_, bf16[165,256]{1,0:T(8,128)(2,1)S(1)} %get-tuple-element.16.refs_1_.refs_2_), custom_call_target="tpu_custom_call" | custom-call | flops 2500000000 | tf_op jit(solution)/shard_map/pack_slots/pallas_call | solution.py:359
  7.4 1.3 %order_operators.1._.refs_1_ = bf16[64,176,165]{2,1,0:T(8,128)(2,1)S(1)} custom-call(s32[72,128]{1,0:T(8,128)S(1)} %get-tuple-element.17._.refs_0_.refs_1_, bf16[165,64,165]{2,1,0:T(8,128)(2,1)S(1)} %bitcast.4), custom_call_target="tpu_custom_call" | custom-call | flops 1300000000 | tf_op jit(solution)/shard_map/order_operators/pallas_call | solution.py:36
  8.9 1.1 %reverse_terms.2._.refs_3_ = bf16[352,9344]{1,0:T(8,128)(2,1)S(1)} custom-call(bf16[165,128]{1,0:T(8,128)(2,1)S(1)} %export.6._, s32[72,128]{1,0:T(8,128)S(1)} %get-tuple-element.17._.refs_0_.refs_1_, bf16[64,176,165]{2,1,0:T(8,128)(2,1)S(1)} %order_operators.1._.refs_1_, bf16[176,9344]{1,0:T(8,128)(2,1)S(1)} %get-tuple-element.18.refs_2_), custom_call_target="tpu_custom_call" | custom-call | flops 100000000 | tf_op jit(solution)/shard_map/reverse_terms/pallas_call | solution.py:36
  10.1 0.2 export.7._
  10.4 2.7 %collective-permute-start.2 = (bf16[165,128]{1,0:T(8,128)(2,1)S(1)}, bf16[165,128]{1,0:T(8,128)(2,1)S(1)}, u32[]{:S(2)}, u32[]{:S(2)}) collective-permute-start(bf16[165,128]{1,0:T(8,128)(2,1)S(1)} %export.7._), channel_id=1, source_target_pairs={{0,4},{4,0},{1,5},{5,1},{2,6},{6,2},{3,7},{7,3},{8,12},{12,8},{9,1... | collective-permute-start | bytes 126728 | tf_op jit(solution)/shard_map/ppermute | solution.py:72
  13.0 3.4 %reverse_terms.3._.refs_2_.refs_5_ = bf16[352,9344]{1,0:T(8,128)(2,1)S(1)} custom-call(bf16[165,128]{1,0:T(8,128)(2,1)S(1)} %export.7._, s32[72,128]{1,0:T(8,128)S(1)} %get-tuple-element.17._.refs_0_.refs_1_, bf16[64,176,165]{2,1,0:T(8,128)(2,1)S(1)} %order_operators.1._.refs_1_, ...), custom_call_target="tpu_custom_call", output_to_operand_aliasing={{}: (4, {})} | custom-call | flops 100000000 | tf_op jit(solution)/shard_map/reverse_terms/pallas_call | solution.py:36
  16.4 1.3 %reverse_sums.3._ = f32[165,128]{1,0:T(8,128)S(1)} custom-call(bf16[352,9344]{1,0:T(8,128)(2,1)S(1)} %reverse_terms.3._.refs_2_.refs_5_, s32[72,128]{1,0:T(8,128)S(1)} %get-tuple-element.17._.refs_0_.refs_1_, s32[73,128]{1,0:T(8,128)S(1)} %get-tuple-element.19.refs_1_.refs_4_, bf16[352,9344]{1,0:T(8,128)(2,1)S(1)} %reverse_terms.3._.refs_2_.refs_5_), custom_call_target="tpu_custom_call" | custom-call | flops 100000000 | tf_op jit(solution)/shard_map/reverse_sums/pallas_call | solution.py:36
  17.7 1.6 %collective-permute-start.3 = (f32[165,128]{1,0:T(8,128)S(1)}, f32[165,128]{1,0:T(8,128)S(1)}, u32[]{:S(2)}, u32[]{:S(2)}) collective-permute-start(f32[165,128]{1,0:T(8,128)S(1)} %reverse_sums.3._), channel_id=1, source_target_pairs={{0,1},{1,0},{2,3},{3,2},{4,5},{5,4},{6,7},{7,6},{8,9},{9,8},{10,11... | collective-permute-start | bytes 253448 | tf_op jit(solution)/shard_map/ppermute | solution.py:72
  19.3 0.2 export.8._
  19.5 1.4 %collective-permute-start.4 = (bf16[165,128]{1,0:T(8,128)(2,1)S(1)}, bf16[165,128]{1,0:T(8,128)(2,1)S(1)}, u32[]{:S(2)}, u32[]{:S(2)}) collective-permute-start(bf16[165,128]{1,0:T(8,128)(2,1)S(1)} %export.8._), channel_id=1, source_target_pairs={{0,2},{2,0},{1,3},{3,1},{4,6},{6,4},{5,7},{7,5},{8,10},{10,8},{9,1... | collective-permute-start | bytes 126728 | tf_op jit(solution)/shard_map/ppermute | solution.py:72
  20.9 1.4 %reverse_sums.4 = (f32[165,128]{1,0:T(8,128)S(1)}, f32[165,128]{1,0:T(8,128)S(1)}) custom-call(bf16[165,128]{1,0:T(8,128)(2,1)S(1)} %export.8._, s32[72,128]{1,0:T(8,128)S(1)} %get-tuple-element.17._.refs_0_.refs_1_, s32[73,128]{1,0:T(8,128)S(1)} %get-tuple-element.19.refs_1_.refs_4_, bf16[352,9344]{1,0:T(8,128)(2,1)S(1)} %reverse_terms.3._.refs_2_.refs_5_), custom_call_target="tpu_custom_call" | custom-call | flops 4000000000 | tf_op jit(solution)/shard_map/reverse_sums/pallas_call | solution.py:36
  22.5 1.5 %collective-permute-start.5 = (f32[165,128]{1,0:T(8,128)S(1)}, f32[165,128]{1,0:T(8,128)S(1)}, u32[]{:S(2)}, u32[]{:S(2)}) collective-permute-start(f32[165,128]{1,0:T(8,128)S(1)} %return.4._), channel_id=1, source_target_pairs={{0,2},{2,0},{1,3},{3,1},{4,6},{6,4},{5,7},{7,5},{8,10},{10,8},{9,1... | collective-permute-start | bytes 253448 | tf_op jit(solution)/shard_map/ppermute | solution.py:72
  24.1 0.3 export.9._
  24.4 1.5 %collective-permute-start.6 = (bf16[165,128]{1,0:T(8,128)(2,1)S(1)}, bf16[165,128]{1,0:T(8,128)(2,1)S(1)}, u32[]{:S(2)}, u32[]{:S(2)}) collective-permute-start(bf16[165,128]{1,0:T(8,128)(2,1)S(1)} %export.9._), channel_id=1, source_target_pairs={{0,1},{1,0},{2,3},{3,2},{4,5},{5,4},{6,7},{7,6},{8,9},{9,8},{10,11... | collective-permute-start | bytes 126728 | tf_op jit(solution)/shard_map/ppermute | solution.py:72
  25.8 1.4 %reverse_sums.5 = (f32[165,128]{1,0:T(8,128)S(1)}, f32[165,128]{1,0:T(8,128)S(1)}) custom-call(bf16[165,128]{1,0:T(8,128)(2,1)S(1)} %export.9._, s32[72,128]{1,0:T(8,128)S(1)} %get-tuple-element.17._.refs_0_.refs_1_, s32[73,128]{1,0:T(8,128)S(1)} %get-tuple-element.19.refs_1_.refs_4_, bf16[352,9344]{1,0:T(8,128)(2,1)S(1)} %reverse_terms.3._.refs_2_.refs_5_), custom_call_target="tpu_custom_call" | custom-call | flops 4000000000 | tf_op jit(solution)/shard_map/reverse_sums/pallas_call | solution.py:36
  27.2 0.3 return.5._
  27.5 0.4 collective-permute-start.7
  27.8 0.6 %collective-permute-done.6.refs_7_ = bf16[165,128]{1,0:T(8,128)(2,1)S(1)} collective-permute-done((bf16[165,128]{1,0:T(8,128)(2,1)S(1)}, bf16[165,128]{1,0:T(8,128)(2,1)S(1)}, u32[]{:S(2)}, u32[]{:S(2)}) %collective-permute-start.6) | collective-permute-done | bytes 42272 | tf_op jit(solution)/shard_map/ppermute | solution.py:72
  28.5 2.3 %forward_columns.1._.refs_2_ = bf16[176,9344]{1,0:T(8,128)(2,1)S(1)} custom-call(f32[165,128]{1,0:T(8,128)S(1)} %return.5._, s32[72,128]{1,0:T(8,128)S(1)} %get-tuple-element.17._.refs_0_.refs_1_, s32[73,128]{1,0:T(8,128)S(1)} %get-tuple-element.19.refs_1_.refs_4_, bf16[165,256]{1,0:T(8,128)(2,1)S(1)} %get-tuple-element.16.refs_1_.refs_2_, ...), custom_call_target="tpu_custom_call" | custom-call | flops 4000000000 | tf_op jit(solution)/shard_map/forward_columns/pallas_call | solution.py:36
  30.8 1.1 %forward_terms.4.refs_3_ = bf16[352,9344]{1,0:T(8,128)(2,1)S(1)} custom-call(bf16[176,9344]{1,0:T(8,128)(2,1)S(1)} %forward_columns.1._.refs_2_, s32[72,128]{1,0:T(8,128)S(1)} %get-tuple-element.17._.refs_0_.refs_1_, bf16[64,176,165]{2,1,0:T(8,128)(2,1)S(1)} %order_operators.1._.refs_1_, bf16[176,9344]{1,0:T(8,128)(2,1)S(1)} %forward_columns.1._.refs_2_), custom_call_target="tpu_custom_call" | custom-call | flops 100000000 | tf_op jit(solution)/shard_map/forward_terms/pallas_call | solution.py:36
  32.0 1.1 %forward_terms.5._.refs_3_ = bf16[352,9344]{1,0:T(8,128)(2,1)S(1)} custom-call(bf16[176,9344]{1,0:T(8,128)(2,1)S(1)} %forward_columns.1._.refs_2_, s32[72,128]{1,0:T(8,128)S(1)} %get-tuple-element.17._.refs_0_.refs_1_, bf16[64,176,165]{2,1,0:T(8,128)(2,1)S(1)} %order_operators.1._.refs_1_, ...), custom_call_target="tpu_custom_call", output_to_operand_aliasing={{}: (4, {})} | custom-call | flops 100000000 | tf_op jit(solution)/shard_map/forward_terms/pallas_call | solution.py:36
  33.1 0.7 %collective-permute-done.7.refs_2_.refs_3_.refs_7_ = f32[165,128]{1,0:T(8,128)S(1)} collective-permute-done((f32[165,128]{1,0:T(8,128)S(1)}, f32[165,128]{1,0:T(8,128)S(1)}, u32[]{:S(2)}, u32[]{:S(2)}) %collective-permute-start.7) | collective-permute-done | bytes 84512 | tf_op jit(solution)/shard_map/ppermute | solution.py:72
  33.8 0.3 return.6._
  34.2 1.1 %forward_terms.6._.refs_3_ = bf16[352,9344]{1,0:T(8,128)(2,1)S(1)} custom-call(f32[165,128]{1,0:T(8,128)S(1)} %return.6._, s32[72,128]{1,0:T(8,128)S(1)} %get-tuple-element.17._.refs_0_.refs_1_, bf16[64,176,165]{2,1,0:T(8,128)(2,1)S(1)} %order_operators.1._.refs_1_, bf16[176,9344]{1,0:T(8,128)(2,1)S(1)} %forward_columns.1._.refs_2_, ...), custom_call_target="tpu_custom_call", output_to_operand_aliasing={{}: (4, {})} | custom-call | flops 100000000 | tf_op jit(solution)/shard_map/forward_terms/pallas_call | solution.py:36
  35.5 0.4 return.7._
  35.9 0.9 %collective-permute-start.9 = (f32[165,128]{1,0:T(8,128)S(1)}, f32[165,128]{1,0:T(8,128)S(1)}, u32[]{:S(2)}, u32[]{:S(2)}) collective-permute-start(f32[165,128]{1,0:T(8,128)S(1)} %return.7._), channel_id=1, source_target_pairs={{0,16},{16,0},{1,17},{17,1},{2,18},{18,2},{3,19},{19,3},{4,20},{20... | collective-permute-start | bytes 253448 | tf_op jit(solution)/shard_map/ppermute | solution.py:72
  36.8 1.1 %forward_terms.7._.refs_3_ = bf16[352,9344]{1,0:T(8,128)(2,1)S(1)} custom-call(f32[165,128]{1,0:T(8,128)S(1)} %return.7._, s32[72,128]{1,0:T(8,128)S(1)} %get-tuple-element.17._.refs_0_.refs_1_, bf16[64,176,165]{2,1,0:T(8,128)(2,1)S(1)} %order_operators.1._.refs_1_, bf16[176,9344]{1,0:T(8,128)(2,1)S(1)} %forward_columns.1._.refs_2_, ...), custom_call_target="tpu_custom_call", output_to_operand_aliasing={{}: (4, {})} | custom-call | flops 100000000 | tf_op jit(solution)/shard_map/forward_terms/pallas_call | solution.py:36
  37.9 3.1 %local_sums.1._.refs_1_ = f32[165,256]{1,0:T(8,128)S(1)} custom-call(bf16[352,9344]{1,0:T(8,128)(2,1)S(1)} %forward_terms.7._.refs_3_, s32[64,256]{1,0:T(8,128)S(1)} %pad_select_fusion._.refs_0_, s32[72,128]{1,0:T(8,128)S(1)} %get-tuple-element.17._.refs_0_.refs_1_, s32[73,128]{1,0:T(8,128)S(1)} %get-tuple-element.24.refs_2_, ...), custom_call_target="tpu_custom_call" | custom-call | flops 100000000 | tf_op jit(solution)/shard_map/local_sums/pallas_call | solution.py:36
  41.0 0.9 %last_sum.1 = f32[165,256]{1,0:T(8,128)} custom-call(f32[165,256]{1,0:T(8,128)S(1)} %local_sums.1._.refs_1_, s32[64,256]{1,0:T(8,128)S(1)} %pad_select_fusion._.refs_0_, f32[165,256]{1,0:T(8,128)S(1)} %local_sums.1._.refs_1_, f32[165,128]{1,0:T(8,128)S(1)} %collective-permute-done.9.refs_2_), custom_call_target="tpu_custom_call" | custom-call | flops 300000000 | tf_op jit(solution)/shard_map/last_sum/pallas_call | solution.py:36
  (20 shorter events, 1.0 us)
Async XLA Ops:
  0.0 7.3 %slice-start = ((s8[5406720]{0:T(1024)(128)(4,1)}), s8[4194304]{0:T(1024)(128)(4,1)S(1)}, s32[]{:S(2)}) async-start(s8[5406720]{0:T(1024)(128)(4,1)} %bitcast.2), calls=%async_computation | async-start | bytes 8388608
  1.0 1.1 %copy-start = (bf16[165,256]{1,0:T(8,128)(2,1)S(1)}, bf16[165,256]{1,0:T(8,128)(2,1)}, u32[]{:S(2)}) copy-start(bf16[165,256]{1,0:T(8,128)(2,1)} %refs_1_.1) | copy-start | bytes 253444
  2.3 6.3 %collective-permute-start = (bf16[165,128]{1,0:T(8,128)(2,1)S(1)}, bf16[165,128]{1,0:T(8,128)(2,1)S(1)}, u32[]{:S(2)}, u32[]{:S(2)}) collective-permute-start(bf16[165,128]{1,0:T(8,128)(2,1)S(1)} %get-tuple-element.15._), channel_id=1, source_target_pairs={{0,16},{16,0},{1,17},{17,1},{2,18},{18,2},{3,19},{19,3},{4,20},{20... | collective-permute-start | bytes 126728 | tf_op jit(solution)/shard_map/ppermute | solution.py:72
  5.4 2.0 %slice-start.1 = ((s8[5406720]{0:T(1024)(128)(4,1)}), s8[1212416]{0:T(1024)(128)(4,1)S(1)}, s32[]{:S(2)}) async-start(s8[5406720]{0:T(1024)(128)(4,1)} %bitcast.2), calls=%async_computation.1 | async-start | bytes 2424832
  8.9 1.3 %collective-permute-start.1 = (bf16[165,128]{1,0:T(8,128)(2,1)S(1)}, bf16[165,128]{1,0:T(8,128)(2,1)S(1)}, u32[]{:S(2)}, u32[]{:S(2)}) collective-permute-start(bf16[165,128]{1,0:T(8,128)(2,1)S(1)} %export.6._), channel_id=1, source_target_pairs={{0,8},{8,0},{1,9},{9,1},{2,10},{10,2},{3,11},{11,3},{4,12},{12,4},... | collective-permute-start | bytes 126728 | tf_op jit(solution)/shard_map/ppermute | solution.py:72
  10.4 8.9 %collective-permute-start.2 = (bf16[165,128]{1,0:T(8,128)(2,1)S(1)}, bf16[165,128]{1,0:T(8,128)(2,1)S(1)}, u32[]{:S(2)}, u32[]{:S(2)}) collective-permute-start(bf16[165,128]{1,0:T(8,128)(2,1)S(1)} %export.7._), channel_id=1, source_target_pairs={{0,4},{4,0},{1,5},{5,1},{2,6},{6,2},{3,7},{7,3},{8,12},{12,8},{9,1... | collective-permute-start | bytes 126728 | tf_op jit(solution)/shard_map/ppermute | solution.py:72
  17.7 4.7 %collective-permute-start.3 = (f32[165,128]{1,0:T(8,128)S(1)}, f32[165,128]{1,0:T(8,128)S(1)}, u32[]{:S(2)}, u32[]{:S(2)}) collective-permute-start(f32[165,128]{1,0:T(8,128)S(1)} %reverse_sums.3._), channel_id=1, source_target_pairs={{0,1},{1,0},{2,3},{3,2},{4,5},{5,4},{6,7},{7,6},{8,9},{9,8},{10,11... | collective-permute-start | bytes 253448 | tf_op jit(solution)/shard_map/ppermute | solution.py:72
  19.5 4.5 %collective-permute-start.4 = (bf16[165,128]{1,0:T(8,128)(2,1)S(1)}, bf16[165,128]{1,0:T(8,128)(2,1)S(1)}, u32[]{:S(2)}, u32[]{:S(2)}) collective-permute-start(bf16[165,128]{1,0:T(8,128)(2,1)S(1)} %export.8._), channel_id=1, source_target_pairs={{0,2},{2,0},{1,3},{3,1},{4,6},{6,4},{5,7},{7,5},{8,10},{10,8},{9,1... | collective-permute-start | bytes 126728 | tf_op jit(solution)/shard_map/ppermute | solution.py:72
  22.5 4.7 %collective-permute-start.5 = (f32[165,128]{1,0:T(8,128)S(1)}, f32[165,128]{1,0:T(8,128)S(1)}, u32[]{:S(2)}, u32[]{:S(2)}) collective-permute-start(f32[165,128]{1,0:T(8,128)S(1)} %return.4._), channel_id=1, source_target_pairs={{0,2},{2,0},{1,3},{3,1},{4,6},{6,4},{5,7},{7,5},{8,10},{10,8},{9,1... | collective-permute-start | bytes 253448 | tf_op jit(solution)/shard_map/ppermute | solution.py:72
  24.4 4.1 %collective-permute-start.6 = (bf16[165,128]{1,0:T(8,128)(2,1)S(1)}, bf16[165,128]{1,0:T(8,128)(2,1)S(1)}, u32[]{:S(2)}, u32[]{:S(2)}) collective-permute-start(bf16[165,128]{1,0:T(8,128)(2,1)S(1)} %export.9._), channel_id=1, source_target_pairs={{0,1},{1,0},{2,3},{3,2},{4,5},{5,4},{6,7},{7,6},{8,9},{9,8},{10,11... | collective-permute-start | bytes 126728 | tf_op jit(solution)/shard_map/ppermute | solution.py:72
  27.5 6.4 %collective-permute-start.7 = (f32[165,128]{1,0:T(8,128)S(1)}, f32[165,128]{1,0:T(8,128)S(1)}, u32[]{:S(2)}, u32[]{:S(2)}) collective-permute-start(f32[165,128]{1,0:T(8,128)S(1)} %return.5._), channel_id=1, source_target_pairs={{0,4},{4,0},{1,5},{5,1},{2,6},{6,2},{3,7},{7,3},{8,12},{12,8},{9,1... | collective-permute-start | bytes 253448 | tf_op jit(solution)/shard_map/ppermute | solution.py:72
  34.2 1.3 %collective-permute-start.8 = (f32[165,128]{1,0:T(8,128)S(1)}, f32[165,128]{1,0:T(8,128)S(1)}, u32[]{:S(2)}, u32[]{:S(2)}) collective-permute-start(f32[165,128]{1,0:T(8,128)S(1)} %return.6._), channel_id=1, source_target_pairs={{0,8},{8,0},{1,9},{9,1},{2,10},{10,2},{3,11},{11,3},{4,12},{12,4},... | collective-permute-start | bytes 253448 | tf_op jit(solution)/shard_map/ppermute | solution.py:72
  35.9 5.1 %collective-permute-start.9 = (f32[165,128]{1,0:T(8,128)S(1)}, f32[165,128]{1,0:T(8,128)S(1)}, u32[]{:S(2)}, u32[]{:S(2)}) collective-permute-start(f32[165,128]{1,0:T(8,128)S(1)} %return.7._), channel_id=1, source_target_pairs={{0,16},{16,0},{1,17},{17,1},{2,18},{18,2},{3,19},{19,3},{4,20},{20... | collective-permute-start | bytes 253448 | tf_op jit(solution)/shard_map/ppermute | solution.py:72

commit v6 on v5

--- a/solution.py
+++ b/solution.py
@@ -222,21 +222,19 @@
 def export_kernel(starts, list_row, meta_ref, *refs):
     segs, out_ref = refs[: len(starts)], refs[len(starts)]
     row = meta_ref[list_row : list_row + 1, LANES:]
-    out = 0.0
-    for seg, first in zip(segs, starts):
-        out = out + dot(seg[...], one_hot(row, first, seg.shape[1]))
-    out_ref[...] = out.astype(BF16)
+    pool = jnp.concatenate([seg[...] for seg in segs], axis=1)
+    out_ref[...] = dot(pool, one_hot(row, 0, pool.shape[1])).astype(BF16)
     for own in refs[len(starts) + 1 :]:
         own[...] = segs[0][...]
 
 
 def came_back(first, row, meta_ref, returned, width):
-    out = 0.0
+    parts, hots = [], []
     for i, ref in enumerate(returned):
         hot = one_hot(meta_ref[row + i : row + i + 1, LANES:], first, width)
-        high, low = halves(ref[...])
-        out = out + dot_nt(high, hot) + dot_nt(low, hot)
-    return out
+        parts += halves(ref[...])
+        hots += [hot, hot]
+    return dot_nt(jnp.concatenate(parts, axis=1), jnp.concatenate(hots, axis=1))
 
 
 def return_kernel(first, row, meta_ref, base_ref, *refs):

time: 42 us -> 41.3 us (0.983); the launches traced: 41.9 us -> 40.7 us
  Pallas kernels: 24.8 us -> 22.4 us
  starting transfers between devices: 13.1 us -> 15 us
  waiting for transfers between devices: 1.64 us -> 0.95 us
    pallas_call x22, Pallas kernels: 22.8 us -> 20.6 us  [call(): pl.pallas_call(lambda _, *refs: kernel(*refs), out_shape=out_shape, in_sp...]
    ppermute x10, starting transfers between devices: 13.1 us -> 15 us  [from_partner(): return lax.ppermute(block, AXES, route)]
    ppermute x10, waiting for transfers between devices: 1.64 us -> 0.95 us  [from_partner(): return lax.ppermute(block, AXES, route)]
  transfers between devices with their start and end apart: 10 -> 10, of which waited for: 4 -> 3; matrix products, arithmetic and copies ran while one was open for 0% -> 0% of each run, Pallas kernels for 54% -> 50%
where the time goes in v6:
time: 41.3 us; the launch traced here: 40.7 us
  Pallas kernels  22.4 us (54%)
  starting transfers between devices  15 us (36%)
  local copies, waits for them, and re-layouts  1.15 us (3%)
  other arithmetic  1.02 us (2%)
  waiting for transfers between devices  0.95 us (2%)
    pallas_call x22, Pallas kernels, call(): pl.pallas_call(lambda _, *refs: kernel(*refs), out_shape=out_shape, in_sp...  20.6 us
    ppermute x10, starting transfers between devices, from_partner(): return lax.ppermute(block, AXES, route)  15 us
    pallas_call x1, Pallas kernels, per_device(): pl.pallas_call(lambda _, *refs: pack_kernel(classes, (to_source, to_count...  1.78 us
    unnamed x6, local copies, waits for them, and re-layouts  1.15 us
    select_n x1, other arithmetic, per_device(): meta = jnp.where(lane < width, code, lists)  1.02 us
    ppermute x10, waiting for transfers between devices, from_partner(): return lax.ppermute(block, AXES, route)  0.95 us
  transfers between devices with their start and end apart: 10, of which 3 were waited for; matrix products, arithmetic and copies ran while one was open for 0% of the time, Pallas kernels for 50%

profile of v6, /device:TPU:0, one launch (start us, length us, event | category | flops | bytes accessed | tf_op | source)
XLA Modules:
  0.0 40.7 jit_solution(4940921219596815550)
XLA Ops:
  0.0 1.0 %pad_select_fusion._.refs_0_ = s32[64,256]{1,0:T(8,128)S(1)} fusion(s32[5,128]{1,0:T(8,128)} %param.8, s32[64,128]{1,0:T(8,128)} %param.10, s32[64,128]{1,0:T(8,128)} %param.9, s32[64]{0:T(128)} %bitcast.5, pred[256]{0:T(512)(128)(4,1)S(1)} %iota_compare_fusion.1), kind=kLoop, calls=%fused_computation | loop fusion | flops 81920 | bytes 134144 | tf_op jit(solution)/shard_map/jit(_where)/select_n | solution.py:314
  1.0 1.1 %copy-done = bf16[165,256]{1,0:T(8,128)(2,1)S(1)} copy-done((bf16[165,256]{1,0:T(8,128)(2,1)S(1)}, bf16[165,256]{1,0:T(8,128)(2,1)}, u32[]{:S(2)}) %copy-start) | copy-done | bytes 84504
  2.3 3.0 %collective-permute-start = (bf16[165,128]{1,0:T(8,128)(2,1)S(1)}, bf16[165,128]{1,0:T(8,128)(2,1)S(1)}, u32[]{:S(2)}, u32[]{:S(2)}) collective-permute-start(bf16[165,128]{1,0:T(8,128)(2,1)S(1)} %get-tuple-element.15._), channel_id=1, source_target_pairs={{0,16},{16,0},{1,17},{17,1},{2,18},{18,2},{3,19},{19,3},{4,20},{20... | collective-permute-start | bytes 126728 | tf_op jit(solution)/shard_map/ppermute | solution.py:72
  5.4 1.8 %pack_slots.1 = (s32[73,128]{1,0:T(8,128)S(1)}, s32[73,128]{1,0:T(8,128)S(1)}, s32[72,128]{1,0:T(8,128)S(1)}, bf16[176,9344]{1,0:T(8,128)(2,1)S(1)}) custom-call(bf16[165,128]{1,0:T(8,128)(2,1)S(1)} %get-tuple-element.15._, s32[64,256]{1,0:T(8,128)S(1)} %pad_select_fusion._.refs_0_, bf16[165,256]{1,0:T(8,128)(2,1)S(1)} %get-tuple-element.16.refs_1_.refs_2_), custom_call_target="tpu_custom_call" | custom-call | flops 2500000000 | tf_op jit(solution)/shard_map/pack_slots/pallas_call | solution.py:357
  7.2 1.3 %order_operators.1._.refs_1_ = bf16[64,176,165]{2,1,0:T(8,128)(2,1)S(1)} custom-call(s32[72,128]{1,0:T(8,128)S(1)} %get-tuple-element.17._.refs_0_.refs_1_, bf16[165,64,165]{2,1,0:T(8,128)(2,1)S(1)} %bitcast.4), custom_call_target="tpu_custom_call" | custom-call | flops 1300000000 | tf_op jit(solution)/shard_map/order_operators/pallas_call | solution.py:36
  8.5 0.2 export.6._
  8.7 1.1 %reverse_terms.2._.refs_3_ = bf16[352,9344]{1,0:T(8,128)(2,1)S(1)} custom-call(bf16[165,128]{1,0:T(8,128)(2,1)S(1)} %export.6._, s32[72,128]{1,0:T(8,128)S(1)} %get-tuple-element.17._.refs_0_.refs_1_, bf16[64,176,165]{2,1,0:T(8,128)(2,1)S(1)} %order_operators.1._.refs_1_, bf16[176,9344]{1,0:T(8,128)(2,1)S(1)} %get-tuple-element.18.refs_2_), custom_call_target="tpu_custom_call" | custom-call | flops 100000000 | tf_op jit(solution)/shard_map/reverse_terms/pallas_call | solution.py:36
  10.0 0.2 export.7._
  10.2 2.7 %collective-permute-start.2 = (bf16[165,128]{1,0:T(8,128)(2,1)S(1)}, bf16[165,128]{1,0:T(8,128)(2,1)S(1)}, u32[]{:S(2)}, u32[]{:S(2)}) collective-permute-start(bf16[165,128]{1,0:T(8,128)(2,1)S(1)} %export.7._), channel_id=1, source_target_pairs={{0,4},{4,0},{1,5},{5,1},{2,6},{6,2},{3,7},{7,3},{8,12},{12,8},{9,1... | collective-permute-start | bytes 126728 | tf_op jit(solution)/shard_map/ppermute | solution.py:72
  12.8 3.4 %reverse_terms.3._.refs_2_.refs_5_ = bf16[352,9344]{1,0:T(8,128)(2,1)S(1)} custom-call(bf16[165,128]{1,0:T(8,128)(2,1)S(1)} %export.7._, s32[72,128]{1,0:T(8,128)S(1)} %get-tuple-element.17._.refs_0_.refs_1_, bf16[64,176,165]{2,1,0:T(8,128)(2,1)S(1)} %order_operators.1._.refs_1_, ...), custom_call_target="tpu_custom_call", output_to_operand_aliasing={{}: (4, {})} | custom-call | flops 100000000 | tf_op jit(solution)/shard_map/reverse_terms/pallas_call | solution.py:36
  16.2 1.0 %reverse_sums.3._ = f32[165,128]{1,0:T(8,128)S(1)} custom-call(bf16[352,9344]{1,0:T(8,128)(2,1)S(1)} %reverse_terms.3._.refs_2_.refs_5_, s32[72,128]{1,0:T(8,128)S(1)} %get-tuple-element.17._.refs_0_.refs_1_, s32[73,128]{1,0:T(8,128)S(1)} %get-tuple-element.19.refs_1_.refs_4_, bf16[352,9344]{1,0:T(8,128)(2,1)S(1)} %reverse_terms.3._.refs_2_.refs_5_), custom_call_target="tpu_custom_call" | custom-call | flops 100000000 | tf_op jit(solution)/shard_map/reverse_sums/pallas_call | solution.py:36
  17.2 2.0 %collective-permute-start.3 = (f32[165,128]{1,0:T(8,128)S(1)}, f32[165,128]{1,0:T(8,128)S(1)}, u32[]{:S(2)}, u32[]{:S(2)}) collective-permute-start(f32[165,128]{1,0:T(8,128)S(1)} %reverse_sums.3._), channel_id=1, source_target_pairs={{0,1},{1,0},{2,3},{3,2},{4,5},{5,4},{6,7},{7,6},{8,9},{9,8},{10,11... | collective-permute-start | bytes 253448 | tf_op jit(solution)/shard_map/ppermute | solution.py:72
  19.3 0.2 export.8._
  19.5 1.7 %collective-permute-start.4 = (bf16[165,128]{1,0:T(8,128)(2,1)S(1)}, bf16[165,128]{1,0:T(8,128)(2,1)S(1)}, u32[]{:S(2)}, u32[]{:S(2)}) collective-permute-start(bf16[165,128]{1,0:T(8,128)(2,1)S(1)} %export.8._), channel_id=1, source_target_pairs={{0,2},{2,0},{1,3},{3,1},{4,6},{6,4},{5,7},{7,5},{8,10},{10,8},{9,1... | collective-permute-start | bytes 126728 | tf_op jit(solution)/shard_map/ppermute | solution.py:72
  21.2 1.1 %reverse_sums.4 = (f32[165,128]{1,0:T(8,128)S(1)}, f32[165,128]{1,0:T(8,128)S(1)}) custom-call(bf16[165,128]{1,0:T(8,128)(2,1)S(1)} %export.8._, s32[72,128]{1,0:T(8,128)S(1)} %get-tuple-element.17._.refs_0_.refs_1_, s32[73,128]{1,0:T(8,128)S(1)} %get-tuple-element.19.refs_1_.refs_4_, bf16[352,9344]{1,0:T(8,128)(2,1)S(1)} %reverse_terms.3._.refs_2_.refs_5_), custom_call_target="tpu_custom_call" | custom-call | flops 4000000000 | tf_op jit(solution)/shard_map/reverse_sums/pallas_call | solution.py:36
  22.4 1.6 %collective-permute-start.5 = (f32[165,128]{1,0:T(8,128)S(1)}, f32[165,128]{1,0:T(8,128)S(1)}, u32[]{:S(2)}, u32[]{:S(2)}) collective-permute-start(f32[165,128]{1,0:T(8,128)S(1)} %return.4._), channel_id=1, source_target_pairs={{0,2},{2,0},{1,3},{3,1},{4,6},{6,4},{5,7},{7,5},{8,10},{10,8},{9,1... | collective-permute-start | bytes 253448 | tf_op jit(solution)/shard_map/ppermute | solution.py:72
  24.0 0.2 export.9._
  24.2 1.7 %collective-permute-start.6 = (bf16[165,128]{1,0:T(8,128)(2,1)S(1)}, bf16[165,128]{1,0:T(8,128)(2,1)S(1)}, u32[]{:S(2)}, u32[]{:S(2)}) collective-permute-start(bf16[165,128]{1,0:T(8,128)(2,1)S(1)} %export.9._), channel_id=1, source_target_pairs={{0,1},{1,0},{2,3},{3,2},{4,5},{5,4},{6,7},{7,6},{8,9},{9,8},{10,11... | collective-permute-start | bytes 126728 | tf_op jit(solution)/shard_map/ppermute | solution.py:72
  25.9 1.1 %reverse_sums.5 = (f32[165,128]{1,0:T(8,128)S(1)}, f32[165,128]{1,0:T(8,128)S(1)}) custom-call(bf16[165,128]{1,0:T(8,128)(2,1)S(1)} %export.9._, s32[72,128]{1,0:T(8,128)S(1)} %get-tuple-element.17._.refs_0_.refs_1_, s32[73,128]{1,0:T(8,128)S(1)} %get-tuple-element.19.refs_1_.refs_4_, bf16[352,9344]{1,0:T(8,128)(2,1)S(1)} %reverse_terms.3._.refs_2_.refs_5_), custom_call_target="tpu_custom_call" | custom-call | flops 4000000000 | tf_op jit(solution)/shard_map/reverse_sums/pallas_call | solution.py:36
  27.0 0.2 return.5._
  27.2 0.4 %collective-permute-start.7 = (f32[165,128]{1,0:T(8,128)S(1)}, f32[165,128]{1,0:T(8,128)S(1)}, u32[]{:S(2)}, u32[]{:S(2)}) collective-permute-start(f32[165,128]{1,0:T(8,128)S(1)} %return.5._), channel_id=1, source_target_pairs={{0,4},{4,0},{1,5},{5,1},{2,6},{6,2},{3,7},{7,3},{8,12},{12,8},{9,1... | collective-permute-start | bytes 253448 | tf_op jit(solution)/shard_map/ppermute | solution.py:72
  27.6 0.7 %collective-permute-done.6.refs_7_ = bf16[165,128]{1,0:T(8,128)(2,1)S(1)} collective-permute-done((bf16[165,128]{1,0:T(8,128)(2,1)S(1)}, bf16[165,128]{1,0:T(8,128)(2,1)S(1)}, u32[]{:S(2)}, u32[]{:S(2)}) %collective-permute-start.6) | collective-permute-done | bytes 42272 | tf_op jit(solution)/shard_map/ppermute | solution.py:72
  28.3 2.0 %forward_columns.1._.refs_2_ = bf16[176,9344]{1,0:T(8,128)(2,1)S(1)} custom-call(f32[165,128]{1,0:T(8,128)S(1)} %return.5._, s32[72,128]{1,0:T(8,128)S(1)} %get-tuple-element.17._.refs_0_.refs_1_, s32[73,128]{1,0:T(8,128)S(1)} %get-tuple-element.19.refs_1_.refs_4_, bf16[165,256]{1,0:T(8,128)(2,1)S(1)} %get-tuple-element.16.refs_1_.refs_2_, ...), custom_call_target="tpu_custom_call" | custom-call | flops 4000000000 | tf_op jit(solution)/shard_map/forward_columns/pallas_call | solution.py:36
  30.3 1.1 %forward_terms.4.refs_3_ = bf16[352,9344]{1,0:T(8,128)(2,1)S(1)} custom-call(bf16[176,9344]{1,0:T(8,128)(2,1)S(1)} %forward_columns.1._.refs_2_, s32[72,128]{1,0:T(8,128)S(1)} %get-tuple-element.17._.refs_0_.refs_1_, bf16[64,176,165]{2,1,0:T(8,128)(2,1)S(1)} %order_operators.1._.refs_1_, bf16[176,9344]{1,0:T(8,128)(2,1)S(1)} %forward_columns.1._.refs_2_), custom_call_target="tpu_custom_call" | custom-call | flops 100000000 | tf_op jit(solution)/shard_map/forward_terms/pallas_call | solution.py:36
  31.5 1.1 %forward_terms.5._.refs_3_ = bf16[352,9344]{1,0:T(8,128)(2,1)S(1)} custom-call(bf16[176,9344]{1,0:T(8,128)(2,1)S(1)} %forward_columns.1._.refs_2_, s32[72,128]{1,0:T(8,128)S(1)} %get-tuple-element.17._.refs_0_.refs_1_, bf16[64,176,165]{2,1,0:T(8,128)(2,1)S(1)} %order_operators.1._.refs_1_, ...), custom_call_target="tpu_custom_call", output_to_operand_aliasing={{}: (4, {})} | custom-call | flops 100000000 | tf_op jit(solution)/shard_map/forward_terms/pallas_call | solution.py:36
  32.6 0.2 return.6._
  33.0 1.1 %forward_terms.6._.refs_3_ = bf16[352,9344]{1,0:T(8,128)(2,1)S(1)} custom-call(f32[165,128]{1,0:T(8,128)S(1)} %return.6._, s32[72,128]{1,0:T(8,128)S(1)} %get-tuple-element.17._.refs_0_.refs_1_, bf16[64,176,165]{2,1,0:T(8,128)(2,1)S(1)} %order_operators.1._.refs_1_, bf16[176,9344]{1,0:T(8,128)(2,1)S(1)} %forward_columns.1._.refs_2_, ...), custom_call_target="tpu_custom_call", output_to_operand_aliasing={{}: (4, {})} | custom-call | flops 100000000 | tf_op jit(solution)/shard_map/forward_terms/pallas_call | solution.py:36
  34.2 0.3 return.7._
  34.5 1.8 %collective-permute-start.9 = (f32[165,128]{1,0:T(8,128)S(1)}, f32[165,128]{1,0:T(8,128)S(1)}, u32[]{:S(2)}, u32[]{:S(2)}) collective-permute-start(f32[165,128]{1,0:T(8,128)S(1)} %return.7._), channel_id=1, source_target_pairs={{0,16},{16,0},{1,17},{17,1},{2,18},{18,2},{3,19},{19,3},{4,20},{20... | collective-permute-start | bytes 253448 | tf_op jit(solution)/shard_map/ppermute | solution.py:72
  36.3 1.1 %forward_terms.7._.refs_3_ = bf16[352,9344]{1,0:T(8,128)(2,1)S(1)} custom-call(f32[165,128]{1,0:T(8,128)S(1)} %return.7._, s32[72,128]{1,0:T(8,128)S(1)} %get-tuple-element.17._.refs_0_.refs_1_, bf16[64,176,165]{2,1,0:T(8,128)(2,1)S(1)} %order_operators.1._.refs_1_, bf16[176,9344]{1,0:T(8,128)(2,1)S(1)} %forward_columns.1._.refs_2_, ...), custom_call_target="tpu_custom_call", output_to_operand_aliasing={{}: (4, {})} | custom-call | flops 100000000 | tf_op jit(solution)/shard_map/forward_terms/pallas_call | solution.py:36
  37.4 2.4 %local_sums.1._.refs_1_ = f32[165,256]{1,0:T(8,128)S(1)} custom-call(bf16[352,9344]{1,0:T(8,128)(2,1)S(1)} %forward_terms.7._.refs_3_, s32[64,256]{1,0:T(8,128)S(1)} %pad_select_fusion._.refs_0_, s32[72,128]{1,0:T(8,128)S(1)} %get-tuple-element.17._.refs_0_.refs_1_, s32[73,128]{1,0:T(8,128)S(1)} %get-tuple-element.24.refs_2_, ...), custom_call_target="tpu_custom_call" | custom-call | flops 100000000 | tf_op jit(solution)/shard_map/local_sums/pallas_call | solution.py:36
  39.9 0.9 %last_sum.1 = f32[165,256]{1,0:T(8,128)} custom-call(f32[165,256]{1,0:T(8,128)S(1)} %local_sums.1._.refs_1_, s32[64,256]{1,0:T(8,128)S(1)} %pad_select_fusion._.refs_0_, f32[165,256]{1,0:T(8,128)S(1)} %local_sums.1._.refs_1_, f32[165,128]{1,0:T(8,128)S(1)} %collective-permute-done.9.refs_2_), custom_call_target="tpu_custom_call" | custom-call | flops 300000000 | tf_op jit(solution)/shard_map/last_sum/pallas_call | solution.py:36
  (20 shorter events, 0.8 us)
Async XLA Ops:
  0.0 7.1 %slice-start = ((s8[5406720]{0:T(1024)(128)(4,1)}), s8[4194304]{0:T(1024)(128)(4,1)S(1)}, s32[]{:S(2)}) async-start(s8[5406720]{0:T(1024)(128)(4,1)} %bitcast.2), calls=%async_computation | async-start | bytes 8388608
  1.0 1.1 %copy-start = (bf16[165,256]{1,0:T(8,128)(2,1)S(1)}, bf16[165,256]{1,0:T(8,128)(2,1)}, u32[]{:S(2)}) copy-start(bf16[165,256]{1,0:T(8,128)(2,1)} %refs_1_.1) | copy-start | bytes 253444
  2.3 6.1 %collective-permute-start = (bf16[165,128]{1,0:T(8,128)(2,1)S(1)}, bf16[165,128]{1,0:T(8,128)(2,1)S(1)}, u32[]{:S(2)}, u32[]{:S(2)}) collective-permute-start(bf16[165,128]{1,0:T(8,128)(2,1)S(1)} %get-tuple-element.15._), channel_id=1, source_target_pairs={{0,16},{16,0},{1,17},{17,1},{2,18},{18,2},{3,19},{19,3},{4,20},{20... | collective-permute-start | bytes 126728 | tf_op jit(solution)/shard_map/ppermute | solution.py:72
  5.4 1.8 %slice-start.1 = ((s8[5406720]{0:T(1024)(128)(4,1)}), s8[1212416]{0:T(1024)(128)(4,1)S(1)}, s32[]{:S(2)}) async-start(s8[5406720]{0:T(1024)(128)(4,1)} %bitcast.2), calls=%async_computation.1 | async-start | bytes 2424832
  8.7 1.3 %collective-permute-start.1 = (bf16[165,128]{1,0:T(8,128)(2,1)S(1)}, bf16[165,128]{1,0:T(8,128)(2,1)S(1)}, u32[]{:S(2)}, u32[]{:S(2)}) collective-permute-start(bf16[165,128]{1,0:T(8,128)(2,1)S(1)} %export.6._), channel_id=1, source_target_pairs={{0,8},{8,0},{1,9},{9,1},{2,10},{10,2},{3,11},{11,3},{4,12},{12,4},... | collective-permute-start | bytes 126728 | tf_op jit(solution)/shard_map/ppermute | solution.py:72
  10.2 9.1 %collective-permute-start.2 = (bf16[165,128]{1,0:T(8,128)(2,1)S(1)}, bf16[165,128]{1,0:T(8,128)(2,1)S(1)}, u32[]{:S(2)}, u32[]{:S(2)}) collective-permute-start(bf16[165,128]{1,0:T(8,128)(2,1)S(1)} %export.7._), channel_id=1, source_target_pairs={{0,4},{4,0},{1,5},{5,1},{2,6},{6,2},{3,7},{7,3},{8,12},{12,8},{9,1... | collective-permute-start | bytes 126728 | tf_op jit(solution)/shard_map/ppermute | solution.py:72
  17.2 5.0 %collective-permute-start.3 = (f32[165,128]{1,0:T(8,128)S(1)}, f32[165,128]{1,0:T(8,128)S(1)}, u32[]{:S(2)}, u32[]{:S(2)}) collective-permute-start(f32[165,128]{1,0:T(8,128)S(1)} %reverse_sums.3._), channel_id=1, source_target_pairs={{0,1},{1,0},{2,3},{3,2},{4,5},{5,4},{6,7},{7,6},{8,9},{9,8},{10,11... | collective-permute-start | bytes 253448 | tf_op jit(solution)/shard_map/ppermute | solution.py:72
  19.5 4.5 %collective-permute-start.4 = (bf16[165,128]{1,0:T(8,128)(2,1)S(1)}, bf16[165,128]{1,0:T(8,128)(2,1)S(1)}, u32[]{:S(2)}, u32[]{:S(2)}) collective-permute-start(bf16[165,128]{1,0:T(8,128)(2,1)S(1)} %export.8._), channel_id=1, source_target_pairs={{0,2},{2,0},{1,3},{3,1},{4,6},{6,4},{5,7},{7,5},{8,10},{10,8},{9,1... | collective-permute-start | bytes 126728 | tf_op jit(solution)/shard_map/ppermute | solution.py:72
  22.4 4.5 %collective-permute-start.5 = (f32[165,128]{1,0:T(8,128)S(1)}, f32[165,128]{1,0:T(8,128)S(1)}, u32[]{:S(2)}, u32[]{:S(2)}) collective-permute-start(f32[165,128]{1,0:T(8,128)S(1)} %return.4._), channel_id=1, source_target_pairs={{0,2},{2,0},{1,3},{3,1},{4,6},{6,4},{5,7},{7,5},{8,10},{10,8},{9,1... | collective-permute-start | bytes 253448 | tf_op jit(solution)/shard_map/ppermute | solution.py:72
  24.2 4.1 %collective-permute-start.6 = (bf16[165,128]{1,0:T(8,128)(2,1)S(1)}, bf16[165,128]{1,0:T(8,128)(2,1)S(1)}, u32[]{:S(2)}, u32[]{:S(2)}) collective-permute-start(bf16[165,128]{1,0:T(8,128)(2,1)S(1)} %export.9._), channel_id=1, source_target_pairs={{0,1},{1,0},{2,3},{3,2},{4,5},{5,4},{6,7},{7,6},{8,9},{9,8},{10,11... | collective-permute-start | bytes 126728 | tf_op jit(solution)/shard_map/ppermute | solution.py:72
  27.2 5.4 %collective-permute-start.7 = (f32[165,128]{1,0:T(8,128)S(1)}, f32[165,128]{1,0:T(8,128)S(1)}, u32[]{:S(2)}, u32[]{:S(2)}) collective-permute-start(f32[165,128]{1,0:T(8,128)S(1)} %return.5._), channel_id=1, source_target_pairs={{0,4},{4,0},{1,5},{5,1},{2,6},{6,2},{3,7},{7,3},{8,12},{12,8},{9,1... | collective-permute-start | bytes 253448 | tf_op jit(solution)/shard_map/ppermute | solution.py:72
  32.9 1.3 %collective-permute-start.8 = (f32[165,128]{1,0:T(8,128)S(1)}, f32[165,128]{1,0:T(8,128)S(1)}, u32[]{:S(2)}, u32[]{:S(2)}) collective-permute-start(f32[165,128]{1,0:T(8,128)S(1)} %return.6._), channel_id=1, source_target_pairs={{0,8},{8,0},{1,9},{9,1},{2,10},{10,2},{3,11},{11,3},{4,12},{12,4},... | collective-permute-start | bytes 253448 | tf_op jit(solution)/shard_map/ppermute | solution.py:72
  34.5 5.3 %collective-permute-start.9 = (f32[165,128]{1,0:T(8,128)S(1)}, f32[165,128]{1,0:T(8,128)S(1)}, u32[]{:S(2)}, u32[]{:S(2)}) collective-permute-start(f32[165,128]{1,0:T(8,128)S(1)} %return.7._), channel_id=1, source_target_pairs={{0,16},{16,0},{1,17},{17,1},{2,18},{18,2},{3,19},{19,3},{4,20},{20... | collective-permute-start | bytes 253448 | tf_op jit(solution)/shard_map/ppermute | solution.py:72

commit v7 on v6

--- a/solution.py
+++ b/solution.py
@@ -142,7 +142,7 @@
         return following, jnp.where(following // LANES == row, current, turned)
 
     none = jnp.zeros((1, LANES), jnp.int32)
-    total, _ = lax.fori_loop(0, classes, place, (0, none), unroll=8)
+    total, _ = lax.fori_loop(0, classes, place, (0, none), unroll=32)
     info_ref[classes:, :] = jnp.full((8, LANES), total, jnp.int32)
     position = lax.broadcasted_iota(jnp.int32, packed_target.shape, 0) * LANES
     position = position + lax.broadcasted_iota(jnp.int32, packed_target.shape, 1)

time: 41.3 us -> 41.2 us (level)
  starting transfers between devices: 15 us -> 12.6 us
  Pallas kernels: 22.4 us -> 23.9 us
  waiting for transfers between devices: 0.95 us -> 1.93 us
    ppermute x10, starting transfers between devices: 15 us -> 12.6 us  [from_partner(): return lax.ppermute(block, AXES, route)]
    pallas_call x22, Pallas kernels: 20.6 us -> 22.4 us  [call(): pl.pallas_call(lambda _, *refs: kernel(*refs), out_shape=out_shape, in_sp...]
    ppermute x10, waiting for transfers between devices: 0.95 us -> 1.93 us  [from_partner(): return lax.ppermute(block, AXES, route)]
  transfers between devices with their start and end apart: 10 -> 10, of which waited for: 3 -> 5; matrix products, arithmetic and copies ran while one was open for 0% -> 0% of each run, Pallas kernels for 50% -> 54%
where the time goes in v7:
time: 41.2 us; the launch traced here: 40.9 us
  Pallas kernels  23.9 us (58%)
  starting transfers between devices  12.6 us (31%)
  waiting for transfers between devices  1.93 us (5%)
  local copies, waits for them, and re-layouts  1.15 us (3%)
  other arithmetic  1.02 us (2%)
    pallas_call x22, Pallas kernels, call(): pl.pallas_call(lambda _, *refs: kernel(*refs), out_shape=out_shape, in_sp...  22.4 us
    ppermute x10, starting transfers between devices, from_partner(): return lax.ppermute(block, AXES, route)  12.6 us
    ppermute x10, waiting for transfers between devices, from_partner(): return lax.ppermute(block, AXES, route)  1.93 us
    pallas_call x1, Pallas kernels, per_device(): pl.pallas_call(lambda _, *refs: pack_kernel(classes, (to_source, to_count...  1.49 us
    unnamed x6, local copies, waits for them, and re-layouts  1.15 us
    select_n x1, other arithmetic, per_device(): meta = jnp.where(lane < width, code, lists)  1.02 us
  transfers between devices with their start and end apart: 10, of which 5 were waited for; matrix products, arithmetic and copies ran while one was open for 0% of the time, Pallas kernels for 54%

profile of v7, /device:TPU:0, one launch (start us, length us, event | category | flops | bytes accessed | tf_op | source)
XLA Modules:
  0.0 40.9 jit_solution(1502775778564123220)
XLA Ops:
  0.0 1.0 %pad_select_fusion._.refs_0_ = s32[64,256]{1,0:T(8,128)S(1)} fusion(s32[5,128]{1,0:T(8,128)} %param.8, s32[64,128]{1,0:T(8,128)} %param.10, s32[64,128]{1,0:T(8,128)} %param.9, s32[64]{0:T(128)} %bitcast.5, pred[256]{0:T(512)(128)(4,1)S(1)} %iota_compare_fusion.1), kind=kLoop, calls=%fused_computation | loop fusion | flops 81920 | bytes 134144 | tf_op jit(solution)/shard_map/jit(_where)/select_n | solution.py:314
  1.0 1.1 %copy-done = bf16[165,256]{1,0:T(8,128)(2,1)S(1)} copy-done((bf16[165,256]{1,0:T(8,128)(2,1)S(1)}, bf16[165,256]{1,0:T(8,128)(2,1)}, u32[]{:S(2)}) %copy-start) | copy-done | bytes 84504
  2.3 3.0 %collective-permute-start = (bf16[165,128]{1,0:T(8,128)(2,1)S(1)}, bf16[165,128]{1,0:T(8,128)(2,1)S(1)}, u32[]{:S(2)}, u32[]{:S(2)}) collective-permute-start(bf16[165,128]{1,0:T(8,128)(2,1)S(1)} %get-tuple-element.15._), channel_id=1, source_target_pairs={{0,16},{16,0},{1,17},{17,1},{2,18},{18,2},{3,19},{19,3},{4,20},{20... | collective-permute-start | bytes 126728 | tf_op jit(solution)/shard_map/ppermute | solution.py:72
  5.4 1.5 %pack_slots.1 = (s32[73,128]{1,0:T(8,128)S(1)}, s32[73,128]{1,0:T(8,128)S(1)}, s32[72,128]{1,0:T(8,128)S(1)}, bf16[176,9344]{1,0:T(8,128)(2,1)S(1)}) custom-call(bf16[165,128]{1,0:T(8,128)(2,1)S(1)} %get-tuple-element.15._, s32[64,256]{1,0:T(8,128)S(1)} %pad_select_fusion._.refs_0_, bf16[165,256]{1,0:T(8,128)(2,1)S(1)} %get-tuple-element.16.refs_1_.refs_2_), custom_call_target="tpu_custom_call" | custom-call | flops 2500000000 | tf_op jit(solution)/shard_map/pack_slots/pallas_call | solution.py:357
  6.9 1.3 %order_operators.1._.refs_1_ = bf16[64,176,165]{2,1,0:T(8,128)(2,1)S(1)} custom-call(s32[72,128]{1,0:T(8,128)S(1)} %get-tuple-element.17._.refs_0_.refs_1_, bf16[165,64,165]{2,1,0:T(8,128)(2,1)S(1)} %bitcast.4), custom_call_target="tpu_custom_call" | custom-call | flops 1300000000 | tf_op jit(solution)/shard_map/order_operators/pallas_call | solution.py:36
  8.4 1.1 %reverse_terms.2._.refs_3_ = bf16[352,9344]{1,0:T(8,128)(2,1)S(1)} custom-call(bf16[165,128]{1,0:T(8,128)(2,1)S(1)} %export.6._, s32[72,128]{1,0:T(8,128)S(1)} %get-tuple-element.17._.refs_0_.refs_1_, bf16[64,176,165]{2,1,0:T(8,128)(2,1)S(1)} %order_operators.1._.refs_1_, bf16[176,9344]{1,0:T(8,128)(2,1)S(1)} %get-tuple-element.18.refs_2_), custom_call_target="tpu_custom_call" | custom-call | flops 100000000 | tf_op jit(solution)/shard_map/reverse_terms/pallas_call | solution.py:36
  9.8 2.7 %collective-permute-start.2 = (bf16[165,128]{1,0:T(8,128)(2,1)S(1)}, bf16[165,128]{1,0:T(8,128)(2,1)S(1)}, u32[]{:S(2)}, u32[]{:S(2)}) collective-permute-start(bf16[165,128]{1,0:T(8,128)(2,1)S(1)} %export.7._), channel_id=1, source_target_pairs={{0,4},{4,0},{1,5},{5,1},{2,6},{6,2},{3,7},{7,3},{8,12},{12,8},{9,1... | collective-permute-start | bytes 126728 | tf_op jit(solution)/shard_map/ppermute | solution.py:72
  12.5 3.4 %reverse_terms.3._.refs_2_.refs_5_ = bf16[352,9344]{1,0:T(8,128)(2,1)S(1)} custom-call(bf16[165,128]{1,0:T(8,128)(2,1)S(1)} %export.7._, s32[72,128]{1,0:T(8,128)S(1)} %get-tuple-element.17._.refs_0_.refs_1_, bf16[64,176,165]{2,1,0:T(8,128)(2,1)S(1)} %order_operators.1._.refs_1_, ...), custom_call_target="tpu_custom_call", output_to_operand_aliasing={{}: (4, {})} | custom-call | flops 100000000 | tf_op jit(solution)/shard_map/reverse_terms/pallas_call | solution.py:36
  15.9 1.3 %reverse_sums.3._ = f32[165,128]{1,0:T(8,128)S(1)} custom-call(bf16[352,9344]{1,0:T(8,128)(2,1)S(1)} %reverse_terms.3._.refs_2_.refs_5_, s32[72,128]{1,0:T(8,128)S(1)} %get-tuple-element.17._.refs_0_.refs_1_, s32[73,128]{1,0:T(8,128)S(1)} %get-tuple-element.19.refs_1_.refs_4_, bf16[352,9344]{1,0:T(8,128)(2,1)S(1)} %reverse_terms.3._.refs_2_.refs_5_), custom_call_target="tpu_custom_call" | custom-call | flops 100000000 | tf_op jit(solution)/shard_map/reverse_sums/pallas_call | solution.py:36
  17.2 1.3 %collective-permute-start.3 = (f32[165,128]{1,0:T(8,128)S(1)}, f32[165,128]{1,0:T(8,128)S(1)}, u32[]{:S(2)}, u32[]{:S(2)}) collective-permute-start(f32[165,128]{1,0:T(8,128)S(1)} %reverse_sums.3._), channel_id=1, source_target_pairs={{0,1},{1,0},{2,3},{3,2},{4,5},{5,4},{6,7},{7,6},{8,9},{9,8},{10,11... | collective-permute-start | bytes 253448 | tf_op jit(solution)/shard_map/ppermute | solution.py:72
  18.5 0.2 export.8._
  18.8 1.6 %collective-permute-start.4 = (bf16[165,128]{1,0:T(8,128)(2,1)S(1)}, bf16[165,128]{1,0:T(8,128)(2,1)S(1)}, u32[]{:S(2)}, u32[]{:S(2)}) collective-permute-start(bf16[165,128]{1,0:T(8,128)(2,1)S(1)} %export.8._), channel_id=1, source_target_pairs={{0,2},{2,0},{1,3},{3,1},{4,6},{6,4},{5,7},{7,5},{8,10},{10,8},{9,1... | collective-permute-start | bytes 126728 | tf_op jit(solution)/shard_map/ppermute | solution.py:72
  20.4 1.4 %reverse_sums.4 = (f32[165,128]{1,0:T(8,128)S(1)}, f32[165,128]{1,0:T(8,128)S(1)}) custom-call(bf16[165,128]{1,0:T(8,128)(2,1)S(1)} %export.8._, s32[72,128]{1,0:T(8,128)S(1)} %get-tuple-element.17._.refs_0_.refs_1_, s32[73,128]{1,0:T(8,128)S(1)} %get-tuple-element.19.refs_1_.refs_4_, bf16[352,9344]{1,0:T(8,128)(2,1)S(1)} %reverse_terms.3._.refs_2_.refs_5_), custom_call_target="tpu_custom_call" | custom-call | flops 4000000000 | tf_op jit(solution)/shard_map/reverse_sums/pallas_call | solution.py:36
  22.0 1.5 %collective-permute-start.5 = (f32[165,128]{1,0:T(8,128)S(1)}, f32[165,128]{1,0:T(8,128)S(1)}, u32[]{:S(2)}, u32[]{:S(2)}) collective-permute-start(f32[165,128]{1,0:T(8,128)S(1)} %return.4._), channel_id=1, source_target_pairs={{0,2},{2,0},{1,3},{3,1},{4,6},{6,4},{5,7},{7,5},{8,10},{10,8},{9,1... | collective-permute-start | bytes 253448 | tf_op jit(solution)/shard_map/ppermute | solution.py:72
  23.5 0.2 export.9._
  23.7 1.5 %collective-permute-start.6 = (bf16[165,128]{1,0:T(8,128)(2,1)S(1)}, bf16[165,128]{1,0:T(8,128)(2,1)S(1)}, u32[]{:S(2)}, u32[]{:S(2)}) collective-permute-start(bf16[165,128]{1,0:T(8,128)(2,1)S(1)} %export.9._), channel_id=1, source_target_pairs={{0,1},{1,0},{2,3},{3,2},{4,5},{5,4},{6,7},{7,6},{8,9},{9,8},{10,11... | collective-permute-start | bytes 126728 | tf_op jit(solution)/shard_map/ppermute | solution.py:72
  25.2 1.4 %reverse_sums.5 = (f32[165,128]{1,0:T(8,128)S(1)}, f32[165,128]{1,0:T(8,128)S(1)}) custom-call(bf16[165,128]{1,0:T(8,128)(2,1)S(1)} %export.9._, s32[72,128]{1,0:T(8,128)S(1)} %get-tuple-element.17._.refs_0_.refs_1_, s32[73,128]{1,0:T(8,128)S(1)} %get-tuple-element.19.refs_1_.refs_4_, bf16[352,9344]{1,0:T(8,128)(2,1)S(1)} %reverse_terms.3._.refs_2_.refs_5_), custom_call_target="tpu_custom_call" | custom-call | flops 4000000000 | tf_op jit(solution)/shard_map/reverse_sums/pallas_call | solution.py:36
  26.6 0.2 return.5._
  26.8 0.4 %collective-permute-start.7 = (f32[165,128]{1,0:T(8,128)S(1)}, f32[165,128]{1,0:T(8,128)S(1)}, u32[]{:S(2)}, u32[]{:S(2)}) collective-permute-start(f32[165,128]{1,0:T(8,128)S(1)} %return.5._), channel_id=1, source_target_pairs={{0,4},{4,0},{1,5},{5,1},{2,6},{6,2},{3,7},{7,3},{8,12},{12,8},{9,1... | collective-permute-start | bytes 253448 | tf_op jit(solution)/shard_map/ppermute | solution.py:72
  27.3 0.6 %collective-permute-done.6.refs_7_ = bf16[165,128]{1,0:T(8,128)(2,1)S(1)} collective-permute-done((bf16[165,128]{1,0:T(8,128)(2,1)S(1)}, bf16[165,128]{1,0:T(8,128)(2,1)S(1)}, u32[]{:S(2)}, u32[]{:S(2)}) %collective-permute-start.6) | collective-permute-done | bytes 42272 | tf_op jit(solution)/shard_map/ppermute | solution.py:72
  27.8 2.3 %forward_columns.1._.refs_2_ = bf16[176,9344]{1,0:T(8,128)(2,1)S(1)} custom-call(f32[165,128]{1,0:T(8,128)S(1)} %return.5._, s32[72,128]{1,0:T(8,128)S(1)} %get-tuple-element.17._.refs_0_.refs_1_, s32[73,128]{1,0:T(8,128)S(1)} %get-tuple-element.19.refs_1_.refs_4_, bf16[165,256]{1,0:T(8,128)(2,1)S(1)} %get-tuple-element.16.refs_1_.refs_2_, ...), custom_call_target="tpu_custom_call" | custom-call | flops 4000000000 | tf_op jit(solution)/shard_map/forward_columns/pallas_call | solution.py:36
  30.2 1.1 %forward_terms.4.refs_3_ = bf16[352,9344]{1,0:T(8,128)(2,1)S(1)} custom-call(bf16[176,9344]{1,0:T(8,128)(2,1)S(1)} %forward_columns.1._.refs_2_, s32[72,128]{1,0:T(8,128)S(1)} %get-tuple-element.17._.refs_0_.refs_1_, bf16[64,176,165]{2,1,0:T(8,128)(2,1)S(1)} %order_operators.1._.refs_1_, bf16[176,9344]{1,0:T(8,128)(2,1)S(1)} %forward_columns.1._.refs_2_), custom_call_target="tpu_custom_call" | custom-call | flops 100000000 | tf_op jit(solution)/shard_map/forward_terms/pallas_call | solution.py:36
  31.3 1.1 %forward_terms.5._.refs_3_ = bf16[352,9344]{1,0:T(8,128)(2,1)S(1)} custom-call(bf16[176,9344]{1,0:T(8,128)(2,1)S(1)} %forward_columns.1._.refs_2_, s32[72,128]{1,0:T(8,128)S(1)} %get-tuple-element.17._.refs_0_.refs_1_, bf16[64,176,165]{2,1,0:T(8,128)(2,1)S(1)} %order_operators.1._.refs_1_, ...), custom_call_target="tpu_custom_call", output_to_operand_aliasing={{}: (4, {})} | custom-call | flops 100000000 | tf_op jit(solution)/shard_map/forward_terms/pallas_call | solution.py:36
  32.5 0.8 %collective-permute-done.7.refs_2_.refs_3_.refs_7_ = f32[165,128]{1,0:T(8,128)S(1)} collective-permute-done((f32[165,128]{1,0:T(8,128)S(1)}, f32[165,128]{1,0:T(8,128)S(1)}, u32[]{:S(2)}, u32[]{:S(2)}) %collective-permute-start.7) | collective-permute-done | bytes 84512 | tf_op jit(solution)/shard_map/ppermute | solution.py:72
  33.2 0.2 return.6._
  33.5 1.1 %forward_terms.6._.refs_3_ = bf16[352,9344]{1,0:T(8,128)(2,1)S(1)} custom-call(f32[165,128]{1,0:T(8,128)S(1)} %return.6._, s32[72,128]{1,0:T(8,128)S(1)} %get-tuple-element.17._.refs_0_.refs_1_, bf16[64,176,165]{2,1,0:T(8,128)(2,1)S(1)} %order_operators.1._.refs_1_, bf16[176,9344]{1,0:T(8,128)(2,1)S(1)} %forward_columns.1._.refs_2_, ...), custom_call_target="tpu_custom_call", output_to_operand_aliasing={{}: (4, {})} | custom-call | flops 100000000 | tf_op jit(solution)/shard_map/forward_terms/pallas_call | solution.py:36
  34.8 0.3 return.7._
  35.1 0.3 collective-permute-start.9
  35.4 1.1 %forward_terms.7._.refs_3_ = bf16[352,9344]{1,0:T(8,128)(2,1)S(1)} custom-call(f32[165,128]{1,0:T(8,128)S(1)} %return.7._, s32[72,128]{1,0:T(8,128)S(1)} %get-tuple-element.17._.refs_0_.refs_1_, bf16[64,176,165]{2,1,0:T(8,128)(2,1)S(1)} %order_operators.1._.refs_1_, bf16[176,9344]{1,0:T(8,128)(2,1)S(1)} %forward_columns.1._.refs_2_, ...), custom_call_target="tpu_custom_call", output_to_operand_aliasing={{}: (4, {})} | custom-call | flops 100000000 | tf_op jit(solution)/shard_map/forward_terms/pallas_call | solution.py:36
  36.6 3.0 %local_sums.1._.refs_1_ = f32[165,256]{1,0:T(8,128)S(1)} custom-call(bf16[352,9344]{1,0:T(8,128)(2,1)S(1)} %forward_terms.7._.refs_3_, s32[64,256]{1,0:T(8,128)S(1)} %pad_select_fusion._.refs_0_, s32[72,128]{1,0:T(8,128)S(1)} %get-tuple-element.17._.refs_0_.refs_1_, s32[73,128]{1,0:T(8,128)S(1)} %get-tuple-element.24.refs_2_, ...), custom_call_target="tpu_custom_call" | custom-call | flops 100000000 | tf_op jit(solution)/shard_map/local_sums/pallas_call | solution.py:36
  39.6 0.4 collective-permute-done.9.refs_2_
  40.0 0.9 %last_sum.1 = f32[165,256]{1,0:T(8,128)} custom-call(f32[165,256]{1,0:T(8,128)S(1)} %local_sums.1._.refs_1_, s32[64,256]{1,0:T(8,128)S(1)} %pad_select_fusion._.refs_0_, f32[165,256]{1,0:T(8,128)S(1)} %local_sums.1._.refs_1_, f32[165,128]{1,0:T(8,128)S(1)} %collective-permute-done.9.refs_2_), custom_call_target="tpu_custom_call" | custom-call | flops 300000000 | tf_op jit(solution)/shard_map/last_sum/pallas_call | solution.py:36
  (20 shorter events, 1.1 us)
Async XLA Ops:
  0.0 6.8 %slice-start = ((s8[5406720]{0:T(1024)(128)(4,1)}), s8[4194304]{0:T(1024)(128)(4,1)S(1)}, s32[]{:S(2)}) async-start(s8[5406720]{0:T(1024)(128)(4,1)} %bitcast.2), calls=%async_computation | async-start | bytes 8388608
  1.0 1.1 %copy-start = (bf16[165,256]{1,0:T(8,128)(2,1)S(1)}, bf16[165,256]{1,0:T(8,128)(2,1)}, u32[]{:S(2)}) copy-start(bf16[165,256]{1,0:T(8,128)(2,1)} %refs_1_.1) | copy-start | bytes 253444
  2.3 5.8 %collective-permute-start = (bf16[165,128]{1,0:T(8,128)(2,1)S(1)}, bf16[165,128]{1,0:T(8,128)(2,1)S(1)}, u32[]{:S(2)}, u32[]{:S(2)}) collective-permute-start(bf16[165,128]{1,0:T(8,128)(2,1)S(1)} %get-tuple-element.15._), channel_id=1, source_target_pairs={{0,16},{16,0},{1,17},{17,1},{2,18},{18,2},{3,19},{19,3},{4,20},{20... | collective-permute-start | bytes 126728 | tf_op jit(solution)/shard_map/ppermute | solution.py:72
  5.4 1.5 %slice-start.1 = ((s8[5406720]{0:T(1024)(128)(4,1)}), s8[1212416]{0:T(1024)(128)(4,1)S(1)}, s32[]{:S(2)}) async-start(s8[5406720]{0:T(1024)(128)(4,1)} %bitcast.2), calls=%async_computation.1 | async-start | bytes 2424832
  8.4 1.3 %collective-permute-start.1 = (bf16[165,128]{1,0:T(8,128)(2,1)S(1)}, bf16[165,128]{1,0:T(8,128)(2,1)S(1)}, u32[]{:S(2)}, u32[]{:S(2)}) collective-permute-start(bf16[165,128]{1,0:T(8,128)(2,1)S(1)} %export.6._), channel_id=1, source_target_pairs={{0,8},{8,0},{1,9},{9,1},{2,10},{10,2},{3,11},{11,3},{4,12},{12,4},... | collective-permute-start | bytes 126728 | tf_op jit(solution)/shard_map/ppermute | solution.py:72
  9.8 8.7 %collective-permute-start.2 = (bf16[165,128]{1,0:T(8,128)(2,1)S(1)}, bf16[165,128]{1,0:T(8,128)(2,1)S(1)}, u32[]{:S(2)}, u32[]{:S(2)}) collective-permute-start(bf16[165,128]{1,0:T(8,128)(2,1)S(1)} %export.7._), channel_id=1, source_target_pairs={{0,4},{4,0},{1,5},{5,1},{2,6},{6,2},{3,7},{7,3},{8,12},{12,8},{9,1... | collective-permute-start | bytes 126728 | tf_op jit(solution)/shard_map/ppermute | solution.py:72
  17.2 4.6 %collective-permute-start.3 = (f32[165,128]{1,0:T(8,128)S(1)}, f32[165,128]{1,0:T(8,128)S(1)}, u32[]{:S(2)}, u32[]{:S(2)}) collective-permute-start(f32[165,128]{1,0:T(8,128)S(1)} %reverse_sums.3._), channel_id=1, source_target_pairs={{0,1},{1,0},{2,3},{3,2},{4,5},{5,4},{6,7},{7,6},{8,9},{9,8},{10,11... | collective-permute-start | bytes 253448 | tf_op jit(solution)/shard_map/ppermute | solution.py:72
  18.8 4.7 %collective-permute-start.4 = (bf16[165,128]{1,0:T(8,128)(2,1)S(1)}, bf16[165,128]{1,0:T(8,128)(2,1)S(1)}, u32[]{:S(2)}, u32[]{:S(2)}) collective-permute-start(bf16[165,128]{1,0:T(8,128)(2,1)S(1)} %export.8._), channel_id=1, source_target_pairs={{0,2},{2,0},{1,3},{3,1},{4,6},{6,4},{5,7},{7,5},{8,10},{10,8},{9,1... | collective-permute-start | bytes 126728 | tf_op jit(solution)/shard_map/ppermute | solution.py:72
  22.0 4.7 %collective-permute-start.5 = (f32[165,128]{1,0:T(8,128)S(1)}, f32[165,128]{1,0:T(8,128)S(1)}, u32[]{:S(2)}, u32[]{:S(2)}) collective-permute-start(f32[165,128]{1,0:T(8,128)S(1)} %return.4._), channel_id=1, source_target_pairs={{0,2},{2,0},{1,3},{3,1},{4,6},{6,4},{5,7},{7,5},{8,10},{10,8},{9,1... | collective-permute-start | bytes 253448 | tf_op jit(solution)/shard_map/ppermute | solution.py:72
  23.7 4.1 %collective-permute-start.6 = (bf16[165,128]{1,0:T(8,128)(2,1)S(1)}, bf16[165,128]{1,0:T(8,128)(2,1)S(1)}, u32[]{:S(2)}, u32[]{:S(2)}) collective-permute-start(bf16[165,128]{1,0:T(8,128)(2,1)S(1)} %export.9._), channel_id=1, source_target_pairs={{0,1},{1,0},{2,3},{3,2},{4,5},{5,4},{6,7},{7,6},{8,9},{9,8},{10,11... | collective-permute-start | bytes 126728 | tf_op jit(solution)/shard_map/ppermute | solution.py:72
  26.8 6.4 %collective-permute-start.7 = (f32[165,128]{1,0:T(8,128)S(1)}, f32[165,128]{1,0:T(8,128)S(1)}, u32[]{:S(2)}, u32[]{:S(2)}) collective-permute-start(f32[165,128]{1,0:T(8,128)S(1)} %return.5._), channel_id=1, source_target_pairs={{0,4},{4,0},{1,5},{5,1},{2,6},{6,2},{3,7},{7,3},{8,12},{12,8},{9,1... | collective-permute-start | bytes 253448 | tf_op jit(solution)/shard_map/ppermute | solution.py:72
  33.5 1.3 %collective-permute-start.8 = (f32[165,128]{1,0:T(8,128)S(1)}, f32[165,128]{1,0:T(8,128)S(1)}, u32[]{:S(2)}, u32[]{:S(2)}) collective-permute-start(f32[165,128]{1,0:T(8,128)S(1)} %return.6._), channel_id=1, source_target_pairs={{0,8},{8,0},{1,9},{9,1},{2,10},{10,2},{3,11},{11,3},{4,12},{12,4},... | collective-permute-start | bytes 253448 | tf_op jit(solution)/shard_map/ppermute | solution.py:72
  35.1 4.9 %collective-permute-start.9 = (f32[165,128]{1,0:T(8,128)S(1)}, f32[165,128]{1,0:T(8,128)S(1)}, u32[]{:S(2)}, u32[]{:S(2)}) collective-permute-start(f32[165,128]{1,0:T(8,128)S(1)} %return.7._), channel_id=1, source_target_pairs={{0,16},{16,0},{1,17},{17,1},{2,18},{18,2},{3,19},{19,3},{4,20},{20... | collective-permute-start | bytes 253448 | tf_op jit(solution)/shard_map/ppermute | solution.py:72
